TPU v7x, 32 devices: a whole 2x2x4 slice. The times are simulated.
32 devices in a mesh: groups: 2 (over x), seq: 16 (over z, y, core).
Axes of the slice: x: 2, y: 2, z: 4, core: 2. Of those that a mesh axis runs over, the one named last changes fastest.
Arguments:
- queries: bfloat16 [4096, 2560], P(('groups', 'seq')), parts along dimension 0, may hold values from -6 to 6
- key_vectors: bfloat16 [4096, 2560], P(('groups', 'seq')), parts along dimension 0, may hold values from -6 to 6
- value_vectors: bfloat16 [4096, 2560], P(('groups', 'seq')), parts along dimension 0, may hold values from -6 to 6
- token_rates: float32 [4096, 20], P(('groups', 'seq')), parts along dimension 0, may hold values from 0.25 to 2.5
- fast_weights: bfloat16 [1024, 3, 20, 128], P(('groups', 'seq')), parts along dimension 0, may hold values from -4 to 4
Outputs:
- applied: bfloat16 [4096, 2560], P(('groups', 'seq')), parts along dimension 0
- renewed: bfloat16 [1024, 3, 20, 128], P(('groups', 'seq')), parts along dimension 0
There are 2 independent parts, one for each index of `groups`. A program takes and returns all parts, laid end to end along the dimension named above; each array names one. Nothing has to cross between parts.
All inputs are finite; a program needn't handle non-finite values.
Results may differ from a plain program's by a relative error of at most 0.0049.
Values may be sent and summed in bfloat16 or wider, within the bound.
No kernel may reach another device: no remote copies, remote signals or barrier semaphores. Data moves between devices by JAX's collectives and lax.ppermute only.
A program may use at most 128 MiB of HBM per device.

v0:
```python
import math

import jax
import jax.numpy as jnp
from jax import lax
from jax.sharding import PartitionSpec as P

HID = 512
NS_STEPS = 2


coef_a = 3.4445
coef_b = -4.775
coef_c = 2.0315


def newton_factor(gram_matrix):
    exact = lax.Precision.HIGHEST
    head_size = gram_matrix.shape[-1]
    trace_sum = jnp.trace(gram_matrix, axis1=-2, axis2=-1)
    factor = 1.0 / (jnp.sqrt(trace_sum) + 1e-07)
    poly_factor = factor[..., None, None] * jnp.eye(head_size, dtype=jnp.float32)
    for newton_step in range(NS_STEPS):
        inner_term = jnp.matmul(gram_matrix, poly_factor, precision=exact)
        square = jnp.matmul(poly_factor, inner_term, precision=exact)
        mixed_term = coef_b * square + coef_c * jnp.matmul(square, square, precision=exact)
        poly_factor = coef_a * poly_factor + jnp.matmul(mixed_term, poly_factor, precision=exact)
    return poly_factor


def hidden_block(query_heads, key_heads, scaled_v, weight_block):
    head_size = query_heads.shape[2]
    scale_in = 1.0 / math.sqrt(head_size)
    scale_out = 1.0 / math.sqrt(HID)
    query_first = scale_in * jnp.einsum(
        "thd,jhd->thj", query_heads, weight_block[:, 0], preferred_element_type=jnp.float32
    )
    query_third = scale_in * jnp.einsum(
        "thd,jhd->thj", query_heads, weight_block[:, 1], preferred_element_type=jnp.float32
    )
    hidden_q = (query_first * jax.nn.sigmoid(query_first) * query_third).astype(jnp.bfloat16)
    partial_out = scale_out * jnp.einsum(
        "thj,jhd->thd", hidden_q, weight_block[:, 2], preferred_element_type=jnp.float32
    )
    key_first = scale_in * jnp.einsum(
        "thd,jhd->thj", key_heads, weight_block[:, 0], preferred_element_type=jnp.float32
    )
    key_third = scale_in * jnp.einsum(
        "thd,jhd->thj", key_heads, weight_block[:, 1], preferred_element_type=jnp.float32
    )
    sigmoid_k = jax.nn.sigmoid(key_first)
    activated = key_first * sigmoid_k
    hidden_k = (activated * key_third).astype(jnp.bfloat16)
    back_grad = jnp.einsum(
        "thd,jhd->thj", scaled_v, weight_block[:, 2], preferred_element_type=jnp.float32
    )
    grad_third = (back_grad * activated).astype(jnp.bfloat16)
    grad_first = (back_grad * key_third * sigmoid_k * (1.0 + key_first * (1.0 - sigmoid_k))).astype(
        jnp.bfloat16
    )
    return (partial_out, hidden_k, grad_first, grad_third)


def add_sources(received):
    return (
        jnp.sum(received[0], axis=1),
        jnp.sum(received[1], axis=1),
        jnp.sum(received[2], axis=1),
    )


def body(queries, key_vectors, value_vectors, token_rates, fast_weights):
    exact = lax.Precision.HIGHEST
    row_count = queries.shape[0]
    num_heads = fast_weights.shape[2]
    head_size = fast_weights.shape[3]
    scale_in = 1.0 / math.sqrt(head_size)
    scale_out = 1.0 / math.sqrt(HID)
    query_heads = queries.reshape(row_count, num_heads, head_size)
    key_heads = key_vectors.reshape(row_count, num_heads, head_size)
    value_heads = value_vectors.reshape(row_count, num_heads, head_size)
    scaled_v = (-scale_out * token_rates[:, :, None] * value_heads.astype(jnp.float32)).astype(
        jnp.bfloat16
    )
    gathered = lax.all_gather(fast_weights, "seq", axis=0, tiled=True)
    out_sum, hidden_k, grad_first, grad_third = hidden_block(
        query_heads, key_heads, scaled_v, gathered
    )
    applied = out_sum.astype(jnp.bfloat16).reshape(row_count, num_heads * head_size)
    full_rows = HID
    term_one = scale_in * jnp.einsum(
        "thj,thd->jhd", grad_first, key_heads, preferred_element_type=jnp.float32
    )
    term_two = scale_in * jnp.einsum(
        "thj,thd->jhd", grad_third, key_heads, preferred_element_type=jnp.float32
    )
    term_out = jnp.einsum("thj,thd->jhd", hidden_k, scaled_v, preferred_element_type=jnp.float32)
    term_one = term_one.reshape(full_rows, 1, num_heads, head_size)
    term_two = term_two.reshape(full_rows, 1, num_heads, head_size)
    term_out = term_out.reshape(full_rows, 1, num_heads, head_size)
    sum_one, sum_two, sum_out = add_sources(
        (
            lax.all_to_all(term_one, "seq", split_axis=0, concat_axis=1, tiled=True),
            lax.all_to_all(term_two, "seq", split_axis=0, concat_axis=1, tiled=True),
            lax.all_to_all(term_out, "seq", split_axis=0, concat_axis=1, tiled=True),
        )
    )
    gradient = jnp.stack([sum_one, sum_two, sum_out], axis=1)
    partial_gram = jnp.einsum("jmhd,jmhe->mhde", gradient, gradient, precision=exact)
    gram_matrix = lax.psum(partial_gram, "seq")
    poly_factor = newton_factor(gram_matrix)
    update = jnp.einsum("mhde,jmhe->jmhd", poly_factor, gradient, precision=exact)
    renewed = (fast_weights.astype(jnp.float32) - math.sqrt(HID) * update).astype(jnp.bfloat16)
    return (applied, renewed)


def solution(mesh):
    in_specs = (
        P(("groups", "seq"), None),
        P(("groups", "seq"), None),
        P(("groups", "seq"), None),
        P(("groups", "seq"), None),
        P(("groups", "seq"), None, None, None),
    )
    out_specs = (P(("groups", "seq"), None), P(("groups", "seq"), None, None, None))
    return jax.shard_map(body, mesh=mesh, in_specs=in_specs, out_specs=out_specs, check_vma=False)
```

profile of v0, /device:TPU:0, one launch (start us, length us, event | category | flops | bytes accessed | tf_op | source)
XLA Modules:
  0.0 655.5 jit_solution(7122451401268588256)
XLA Ops:
  7.2 0.0 all-gather.2.cloned.1.call-start
  7.2 0.7 all-gather.2.cloned.1.call-update
  7.9 1.4 copy.82
  9.3 1.4 copy.79
  10.7 0.7 broadcast_multiply_fusion
  11.4 76.4 %all-gather.2.cloned.1.call-done = bf16[512,3,20,128]{3,0,2,1:T(8,128)(2,1)} async-done(((bf16[32,3,20,128]{3,0,2,1:T(8,128)(2,1)}), bf16[512,3,20,128]{3,0,2,1:T(8,128)(2,1)}) %all-gather.2.cloned.1.call-update) | async-done | bytes 7864336 | tf_op jit(solution)/shard_map/all_gather | solution.py:85
  87.9 2.6 fusion.50
  90.5 0.0 copy-start.2
  90.5 4.5 fusion.48
  94.9 0.0 copy-start.3
  94.9 0.0 copy-done.2
  94.9 2.3 copy-done.3
  97.2 4.4 fusion.45
  101.7 11.7 %copy.96 = f32[512,1,20,128]{3,1,2,0:T(1,128)} copy(f32[512,1,20,128]{0,3,2,1:T(8,128)} %fusion.45) | data formatting | bytes 10485760 | tf_op jit(solution)/shard_map/reshape | solution.py:100
  113.3 5.1 all-to-all-start.2
  118.4 0.0 copy-start.4
  118.5 2.7 fusion.52
  121.2 0.0 copy-start.1
  121.2 2.3 copy-done.1
  123.5 0.0 copy-done.4
  123.5 4.2 multiply_bitcast_fusion
  127.7 10.2 %copy.91 = f32[512,1,20,128]{3,1,2,0:T(1,128)} copy(f32[512,1,20,128]{3,0,2,1:T(8,128)} %multiply_bitcast_fusion) | data formatting | bytes 10485760 | tf_op jit(solution)/shard_map/reshape | solution.py:99
  137.9 76.4 %all-to-all-done.2 = f32[512,1,20,128]{3,1,2,0:T(1,128)} async-done(((f32[512,1,20,128]{3,1,2,0:T(1,128)}), f32[512,1,20,128]{3,1,2,0:T(1,128)}, u32[]{:S(2)}, u32[]{:S(2)}) %all-to-all-start.2) | async-done | bytes 5242912 | tf_op jit(solution)/shard_map/all_to_all | solution.py:105
  214.3 24.0 %all-to-all-start.1 = ((f32[512,1,20,128]{3,1,2,0:T(1,128)}), f32[512,1,20,128]{3,1,2,0:T(1,128)}, u32[]{:S(2)}, u32[]{:S(2)}) async-start(f32[512,1,20,128]{3,1,2,0:T(1,128)} %copy.91), calls=%async_computation.1 | async-start | bytes 10485760 | tf_op jit(solution)/shard_map/all_to_all | solution.py:104
  238.4 10.5 %multiply_bitcast_fusion.1 = f32[512,1,20,128]{3,0,2,1:T(8,128)} fusion(bf16[128,20,128]{0,2,1:T(8,128)(2,1)S(1)} %bitcast.164, f32[20,128,512]{1,2,0:T(8,128)} %copy-done.1, f32[20,512,128]{2,1,0:T(8,128)} %copy-done.3, f32[20,512,128]{2,1,0:T(8,128)} %copy-done.2), kind=kOutput, calls=%fused_computation.30 | convolution fusion | flops 352583680 | bytes 21626880 | tf_op jit(solution)/shard_map/thj,thd->jhd/dot_general | solution.py:91
  248.9 10.2 %copy.86 = f32[512,1,20,128]{3,1,2,0:T(1,128)} copy(f32[512,1,20,128]{3,0,2,1:T(8,128)} %multiply_bitcast_fusion.1) | data formatting | bytes 10485760 | tf_op jit(solution)/shard_map/reshape | solution.py:98
  259.1 75.2 %all-to-all-done.1 = f32[512,1,20,128]{3,1,2,0:T(1,128)} async-done(((f32[512,1,20,128]{3,1,2,0:T(1,128)}), f32[512,1,20,128]{3,1,2,0:T(1,128)}, u32[]{:S(2)}, u32[]{:S(2)}) %all-to-all-start.1) | async-done | bytes 5242912 | tf_op jit(solution)/shard_map/all_to_all | solution.py:104
  334.3 23.9 %all-to-all-start = ((f32[512,1,20,128]{3,1,2,0:T(1,128)}), f32[512,1,20,128]{3,1,2,0:T(1,128)}, u32[]{:S(2)}, u32[]{:S(2)}) async-start(f32[512,1,20,128]{3,1,2,0:T(1,128)} %copy.86), calls=%async_computation | async-start | bytes 10485760 | tf_op jit(solution)/shard_map/all_to_all | solution.py:103
  358.2 0.3 all-reduce.2.cloned.1.call-start
  358.4 5.4 copy.97
  363.8 3.2 reduce_sum.39
  367.0 5.5 copy.111
  372.5 3.2 reduce_sum.38
  375.6 78.5 %all-to-all-done = f32[512,1,20,128]{3,1,2,0:T(1,128)} async-done(((f32[512,1,20,128]{3,1,2,0:T(1,128)}), f32[512,1,20,128]{3,1,2,0:T(1,128)}, u32[]{:S(2)}, u32[]{:S(2)}) %all-to-all-start) | async-done | bytes 5242912 | tf_op jit(solution)/shard_map/all_to_all | solution.py:103
  454.1 5.6 copy.110
  459.7 3.2 reduce_sum.37
  462.9 0.1 copy_bitcast_fusion
  463.0 0.0 copy-start.6
  463.0 8.2 %fusion.85 = f32[3,20,128,128]{3,2,1,0:T(8,128)} fusion(f32[32,1,20,128]{3,0,2,1:T(8,128)S(1)} %bitcast.165, f32[32,1,20,128]{3,0,2,1:T(8,128)S(1)} %get-tuple-element.12, f32[32,1,20,128]{3,0,2,1:T(8,128)S(1)} %get-tuple-element.13), kind=kOutput, calls=%fused_computation.77 | convolution fusion | flops 377978880 | bytes 4915200 | tf_op jit(solution)/shard_map/jmhd,jmhe->mhde/dot_general | solution.py:109
  471.3 0.0 all-reduce.2.cloned.1.call-update
  471.3 0.0 copy-done.6
  471.3 0.3 copy.74
  471.7 4.8 fusion.49
  476.5 7.1 %fusion.69 = bf16[20,128,128]{1,2,0:T(8,128)(2,1)S(1)} fusion(bf16[512,3,20,128]{3,0,2,1:T(8,128)(2,1)} %all-gather.2.cloned.1.call-done, f32[20,512,128]{2,1,0:T(8,128)} %fusion.49, bf16[128,20,128]{0,2,1:T(8,128)(2,1)S(1)} %bitcast.170), kind=kOutput, calls=%fused_computation.69 | convolution fusion | flops 682229760 | bytes 11796480 | tf_op jit(solution)/shard_map/thj,jhd->thd/dot_general | solution.py:42
  483.6 1.1 copy.98
  484.7 114.8 %all-reduce.2.cloned.1.call-done = f32[3,20,128,128]{3,2,1,0:T(8,128)} async-done(((f32[3,20,128,128]{3,2,1,0:T(8,128)}), f32[3,20,128,128]{3,2,1,0:T(8,128)}) %all-reduce.2.cloned.1.call-update) | async-done | bytes 3932176 | tf_op jit(solution)/shard_map/psum | solution.py:110
  599.5 0.0 copy-start
  599.5 2.7 select_reduce_fusion
  602.2 0.6 copy-done
  602.8 5.0 fusion.4
  607.7 5.1 fusion.2
  612.9 4.4 fusion.104
  617.2 5.1 fusion.19
  622.3 5.2 fusion.105
  627.6 4.6 fusion.106
  632.2 4.1 fusion.107
  636.2 0.0 copy-start.5
  636.2 4.9 fusion.22
  641.2 0.0 copy-done.5
  641.2 7.0 %fusion.82 = bf16[32,3,20,128]{3,0,2,1:T(8,128)(2,1)} fusion(f32[3,20,128,128]{3,2,1,0:T(8,128)S(1)} %fusion.22, f32[3,20,128,128]{3,2,1,0:T(8,128)S(1)} %fusion.19, bf16[32,3,20,128]{3,0,2,1:T(8,128)(2,1)S(1)} %copy-done.5, f32[32,1,20,128]{3,0,2,1:T(8,128)S(1)} %bitcast.166, f32[32,1,20,128]{3,0,2,1:T(8,128)S(1)} %get-tuple-element.12, ...), kind=kOutput, calls=%fused_computation.75 | convolution fusion | flops 380928000 | bytes 9830400 | tf_op jit(solution)/shard_map/mhde,jmhe->jmhd/dot_general | solution.py:112
  (3 shorter events, 0.0 us)
Async XLA Ops:
  7.2 80.7 %all-gather.2.cloned.1.call-start = ((), (), s32[]{:S(2)}) async-start(), calls=%async_computation.3 | async-start | bytes 8355840 | tf_op jit(solution)/shard_map/all_gather | solution.py:85
  90.5 4.5 copy-start.2
  94.9 2.3 copy-start.3
  113.3 101.0 %all-to-all-start.2 = ((f32[512,1,20,128]{3,1,2,0:T(1,128)}), f32[512,1,20,128]{3,1,2,0:T(1,128)}, u32[]{:S(2)}, u32[]{:S(2)}) async-start(f32[512,1,20,128]{3,1,2,0:T(1,128)} %copy.96), calls=%async_computation.2 | async-start | bytes 10485760 | tf_op jit(solution)/shard_map/all_to_all | solution.py:105
  118.4 5.1 copy-start.4
  121.2 2.3 copy-start.1
  214.3 120.0 %all-to-all-start.1 = ((f32[512,1,20,128]{3,1,2,0:T(1,128)}), f32[512,1,20,128]{3,1,2,0:T(1,128)}, u32[]{:S(2)}, u32[]{:S(2)}) async-start(f32[512,1,20,128]{3,1,2,0:T(1,128)} %copy.91), calls=%async_computation.1 | async-start | bytes 10485760 | tf_op jit(solution)/shard_map/all_to_all | solution.py:104
  334.3 119.8 %all-to-all-start = ((f32[512,1,20,128]{3,1,2,0:T(1,128)}), f32[512,1,20,128]{3,1,2,0:T(1,128)}, u32[]{:S(2)}, u32[]{:S(2)}) async-start(f32[512,1,20,128]{3,1,2,0:T(1,128)} %copy.86), calls=%async_computation | async-start | bytes 10485760 | tf_op jit(solution)/shard_map/all_to_all | solution.py:103
  358.2 241.3 %all-reduce.2.cloned.1.call-start = ((), (), s32[]{:S(2)}) async-start(), calls=%async_computation.4 | async-start | bytes 7864320 | tf_op jit(solution)/shard_map/psum | solution.py:110
  463.0 8.3 %copy-start.6 = (bf16[128,2560]{1,0:T(8,128)(2,1)S(1)}, bf16[128,2560]{1,0:T(8,128)(2,1)}, u32[]{:S(2)}) copy-start(bf16[128,2560]{1,0:T(8,128)(2,1)} %param.5) | copy-start | bytes 1966084
  599.5 3.3 copy-start
  636.2 5.0 copy-start.5
Sparse Core Ops, SparseCore 0:
  10.2 77.6 all-gather.1
  471.4 128.0 all-reduce.1
where the time goes:
time: 660 us; the launch traced here: 655 us
  waiting for transfers between devices  422 us (64%)
  matrix products  94.4 us (14%)
  local copies, waits for them, and re-layouts  58.1 us (9%)
  starting transfers between devices  53.3 us (8%)
  between operations  14.7 us (2%)
  other arithmetic  12.9 us (2%)
    psum x1, waiting for transfers between devices, body(): gram_matrix = lax.psum(partial_gram, 'seq')  115 us
    all_to_all x1, waiting for transfers between devices, body(): lax.all_to_all(term_one, 'seq', split_axis=0, concat_axis=1, tiled=True)  78.5 us
    all_to_all x1, waiting for transfers between devices, body(): lax.all_to_all(term_out, 'seq', split_axis=0, concat_axis=1, tiled=True)  76.4 us
    all_gather x1, waiting for transfers between devices, body(): gathered = lax.all_gather(fast_weights, 'seq', axis=0, tiled=True)  76.4 us
    all_to_all x1, waiting for transfers between devices, body(): lax.all_to_all(term_two, 'seq', split_axis=0, concat_axis=1, tiled=True)  75.2 us
    all_to_all x1, starting transfers between devices, body(): lax.all_to_all(term_two, 'seq', split_axis=0, concat_axis=1, tiled=True)  24 us
    all_to_all x1, starting transfers between devices, body(): lax.all_to_all(term_one, 'seq', split_axis=0, concat_axis=1, tiled=True)  23.9 us
  transfers between devices with their start and end apart: 5, of which 5 were waited for; matrix products, arithmetic and copies ran while one was open for 11% of the time, Pallas kernels for 0%

commit v1 on v0

--- a/solution.py
+++ b/solution.py
@@ -1,17 +1,233 @@
+import functools
 import math
 
 import jax
 import jax.numpy as jnp
 from jax import lax
+from jax.experimental import pallas as pl
+from jax.experimental.pallas import tpu as pltpu
 from jax.sharding import PartitionSpec as P
 
 HID = 512
 NS_STEPS = 2
-
+PLANE = 4
 
 coef_a = 3.4445
 coef_b = -4.775
 coef_c = 2.0315
+
+VMEM = pltpu.VMEM
+SMEM = pltpu.SMEM
+NT = (((1,), (1,)), ((), ()))
+NN = (((1,), (0,)), ((), ()))
+TN = (((0,), (0,)), ((), ()))
+
+
+def dot(a, b, dims, precision=None):
+    return lax.dot_general(a, b, dims, precision=precision, preferred_element_type=jnp.float32)
+
+
+def key_kernel(heads, place_ref, k_ref, s_ref, w0, w1, w2, w3, keep_ref, send_ref, weights):
+    place = place_ref[0]
+    planes, rows, head_size = k_ref.shape
+    slots = keep_ref.shape[1]
+    tokens = planes * rows
+    step = pl.program_id(0)
+    scale_in = 1.0 / math.sqrt(head_size)
+    quarter = weights.shape[1] // PLANE
+    for rel, w in enumerate((w0, w1, w2, w3)):
+        at = pl.multiple_of((place ^ rel) * quarter, quarter)
+        for matrix in range(3):
+            weights[matrix, pl.ds(at, quarter), :] = w[:, 0, matrix].reshape(quarter, head_size)
+    keys = k_ref[...].reshape(tokens, head_size)
+    scaled = s_ref[...].reshape(tokens, head_size)
+    hid = weights.shape[1]
+
+    @pl.when(step == 0)
+    def _():
+        for index in range(3 * heads, PLANE * slots):
+            rel = (index // slots) ^ place
+            keep_ref[rel // 2, index % slots] = jnp.zeros((hid, head_size), keep_ref.dtype)
+            send_ref[rel // 2, index % slots] = jnp.zeros((hid, head_size), send_ref.dtype)
+
+    block = 128
+    for at in range(0, hid, block):
+        rows_at = slice(at, at + block)
+        raw_first = dot(weights[0, rows_at], keys, NT)
+        raw_third = dot(weights[1, rows_at], keys, NT)
+        back = dot(weights[2, rows_at], scaled, NT)
+        first = raw_first * scale_in
+        sig = 0.5 * jnp.tanh(0.5 * first) + 0.5
+        act = first * sig
+        hidden = (act * raw_third).astype(jnp.bfloat16)
+        grad_third = (back * act).astype(jnp.bfloat16)
+        slope = sig + act * (1.0 - sig)
+        grad_first = (back * raw_third * slope).astype(jnp.bfloat16)
+        terms = (
+            dot(grad_first, keys, NN) * (scale_in * scale_in),
+            dot(grad_third, keys, NN) * scale_in,
+            dot(hidden, scaled, NN) * scale_in,
+        )
+        for matrix in range(3):
+            index = 3 * step + matrix
+            rel = (index // slots) ^ place
+            slot = index % slots
+            half = rel // 2
+
+            @pl.when(rel % 2 == 0)
+            def _():
+                keep_ref[half, slot, rows_at, :] = terms[matrix]
+
+            @pl.when(rel % 2 == 1)
+            def _():
+                send_ref[half, slot, rows_at, :] = terms[matrix].astype(send_ref.dtype)
+
+
+def query_kernel(place_ref, q_ref, w0, w1, w2, w3, out_ref, weights):
+    place = place_ref[0]
+    planes, rows, head_size = q_ref.shape
+    tokens = planes * rows
+    scale_in = 1.0 / math.sqrt(head_size)
+    scale_out = 1.0 / math.sqrt(HID)
+    quarter = weights.shape[1] // PLANE
+    for rel, w in enumerate((w0, w1, w2, w3)):
+        at = pl.multiple_of((place ^ rel) * quarter, quarter)
+        for matrix in range(3):
+            weights[matrix, pl.ds(at, quarter), :] = w[:, 0, matrix].reshape(quarter, head_size)
+    for plane in range(planes):
+        queries = q_ref[plane]
+        first = dot(queries, weights[0], NT) * scale_in
+        third = dot(queries, weights[1], NT) * scale_in
+        sig = 0.5 * jnp.tanh(0.5 * first) + 0.5
+        hidden = (first * sig * third).astype(jnp.bfloat16)
+        out_ref[plane] = (dot(hidden, weights[2], NN) * scale_out).astype(out_ref.dtype)
+
+
+def renew_kernel(place_ref, mine_ref, got_ref, w0, w1, w2, w3, out_ref, updates):
+    place = place_ref[0]
+    slots, hid, head_size = mine_ref.shape
+    planes, heads = w0.shape[0], w0.shape[1]
+    exact = lax.Precision.HIGHEST
+    quarter = hid // PLANE
+    rows = quarter // planes
+    eye = (
+        lax.broadcasted_iota(jnp.int32, (head_size, head_size), 0)
+        == lax.broadcasted_iota(jnp.int32, (head_size, head_size), 1)
+    ).astype(jnp.float32)
+    grads = [mine_ref[slot] + got_ref[slot].astype(jnp.float32) for slot in range(slots)]
+    grams = [dot(grad, grad, TN, exact) for grad in grads]
+    factors = [eye * (1.0 / (jnp.sqrt(jnp.sum(gram * eye)) + 1e-07)) for gram in grams]
+    for _ in range(NS_STEPS):
+        inner = [dot(gram, factor, NN, exact) for gram, factor in zip(grams, factors)]
+        square = [dot(factor, term, NN, exact) for factor, term in zip(factors, inner)]
+        mixed = [coef_b * term + coef_c * dot(term, term, NN, exact) for term in square]
+        factors = [coef_a * factor + dot(term, factor, NN, exact) for term, factor in zip(mixed, factors)]
+    for slot in range(slots):
+        updates[slot] = math.sqrt(HID) * dot(grads[slot], factors[slot], NT, exact)
+    for slot in range(slots):
+        index = jnp.minimum(place * slots + slot, 3 * heads - 1)
+        head, matrix = index // 3, index % 3
+        for rel, w in enumerate((w0, w1, w2, w3)):
+            spot = place ^ rel
+            for plane in range(planes):
+                at = pl.multiple_of(spot * quarter + plane * rows, rows)
+                old = w[plane, head, matrix].astype(jnp.float32)
+                out_ref[plane, spot, slot] = (old - updates[slot, pl.ds(at, rows), :]).astype(out_ref.dtype)
+
+
+def plane_body(queries, key_vectors, value_vectors, token_rates, fast_weights, planes):
+    row_count = queries.shape[0]
+    own_rows, _, num_heads, head_size = fast_weights.shape
+    heads = num_heads // planes
+    width = heads * head_size
+    size = planes * PLANE
+    slots = -(-3 * heads // PLANE)
+    scale_out = 1.0 / math.sqrt(HID)
+    lines = [[PLANE * plane + spot for plane in range(planes)] for spot in range(PLANE)]
+    place = (lax.axis_index("seq") % PLANE).astype(jnp.int32).reshape(1)
+
+    def along(array):
+        return lax.all_to_all(array, "seq", 0, 0, axis_index_groups=lines, tiled=True)
+
+    def swap(array, bit):
+        return lax.ppermute(array, "seq", [(at, at ^ bit) for at in range(size)])
+
+    sent_w = fast_weights.reshape(own_rows, 3, planes, heads, head_size).transpose(2, 3, 1, 0, 4)
+    w0 = along(sent_w)
+    w2 = swap(w0, 2)
+    w1 = swap(w0, 1)
+    w3 = swap(w2, 1)
+    weights = (w0, w1, w2, w3)
+
+    scaled_v = (
+        (-scale_out * token_rates[:, :, None])
+        * value_vectors.reshape(row_count, num_heads, head_size).astype(jnp.float32)
+    ).astype(jnp.bfloat16).reshape(row_count, num_heads * head_size)
+
+    def split(array):
+        return array.reshape(row_count, planes, width).transpose(1, 0, 2)
+
+    keys = along(split(key_vectors))
+    scaled = along(split(scaled_v))
+    moved_q = along(split(queries))
+
+    smem = pl.BlockSpec(memory_space=SMEM)
+    rows_spec = pl.BlockSpec((planes, row_count, head_size), lambda h: (0, 0, h))
+    weight_spec = pl.BlockSpec((planes, 1, 3, own_rows, head_size), lambda h: (0, h, 0, 0, 0))
+    hid = size * own_rows
+    grad_shape = (2, slots, hid, head_size)
+    keep, send = pl.pallas_call(
+        functools.partial(key_kernel, heads),
+        grid=(heads,),
+        in_specs=[smem, rows_spec, rows_spec] + [weight_spec] * 4,
+        out_specs=[pl.BlockSpec(grad_shape, lambda h: (0, 0, 0, 0))] * 2,
+        out_shape=[
+            jax.ShapeDtypeStruct(grad_shape, jnp.float32),
+            jax.ShapeDtypeStruct(grad_shape, jnp.bfloat16),
+        ],
+        scratch_shapes=[VMEM((3, hid, head_size), jnp.bfloat16)],
+        compiler_params=pltpu.CompilerParams(vmem_limit_bytes=32 * 2**20),
+        cost_estimate=pl.CostEstimate(flops=2 * 10**9, bytes_accessed=10**7, transcendentals=10**6),
+        name="key_side",
+    )(place, keys, scaled, *weights)
+
+    got = swap(send, 1).astype(jnp.float32)
+    mine = keep[0] + got[0]
+    other = (keep[1] + got[1]).astype(jnp.bfloat16)
+    last = swap(other, 2)
+
+    renewed = pl.pallas_call(
+        renew_kernel,
+        in_specs=[smem] + [pl.BlockSpec(memory_space=VMEM)] * 6,
+        out_specs=pl.BlockSpec(memory_space=VMEM),
+        out_shape=jax.ShapeDtypeStruct((planes, PLANE, slots, own_rows, head_size), jnp.bfloat16),
+        scratch_shapes=[VMEM((slots, hid, head_size), jnp.float32)],
+        compiler_params=pltpu.CompilerParams(vmem_limit_bytes=32 * 2**20),
+        cost_estimate=pl.CostEstimate(flops=10**9, bytes_accessed=10**7, transcendentals=0),
+        name="renew",
+    )(place, mine, last, *weights)
+    back = lax.all_to_all(
+        renewed.reshape(size, slots, own_rows, head_size), "seq", 0, 0, tiled=True
+    ).reshape(planes, PLANE * slots, own_rows, head_size)[:, : 3 * heads]
+    renewed_out = (
+        back.reshape(planes, heads, 3, own_rows, head_size)
+        .transpose(3, 2, 0, 1, 4)
+        .reshape(own_rows, 3, num_heads, head_size)
+    )
+
+    moved_out = pl.pallas_call(
+        query_kernel,
+        grid=(heads,),
+        in_specs=[smem, rows_spec] + [weight_spec] * 4,
+        out_specs=rows_spec,
+        out_shape=jax.ShapeDtypeStruct((planes, row_count, width), jnp.bfloat16),
+        scratch_shapes=[VMEM((3, hid, head_size), jnp.bfloat16)],
+        compiler_params=pltpu.CompilerParams(vmem_limit_bytes=32 * 2**20),
+        cost_estimate=pl.CostEstimate(flops=10**9, bytes_accessed=10**7, transcendentals=10**6),
+        name="query_side",
+    )(place, moved_q, *weights)
+    applied = along(moved_out).transpose(1, 0, 2).reshape(row_count, planes * width)
+    return applied, renewed_out
 
 
 def newton_factor(gram_matrix):
@@ -61,15 +277,7 @@
     return (partial_out, hidden_k, grad_first, grad_third)
 
 
-def add_sources(received):
-    return (
-        jnp.sum(received[0], axis=1),
-        jnp.sum(received[1], axis=1),
-        jnp.sum(received[2], axis=1),
-    )
-
-
-def body(queries, key_vectors, value_vectors, token_rates, fast_weights):
+def gather_body(queries, key_vectors, value_vectors, token_rates, fast_weights):
     exact = lax.Precision.HIGHEST
     row_count = queries.shape[0]
     num_heads = fast_weights.shape[2]
@@ -87,31 +295,35 @@
         query_heads, key_heads, scaled_v, gathered
     )
     applied = out_sum.astype(jnp.bfloat16).reshape(row_count, num_heads * head_size)
-    full_rows = HID
-    term_one = scale_in * jnp.einsum(
-        "thj,thd->jhd", grad_first, key_heads, preferred_element_type=jnp.float32
-    )
-    term_two = scale_in * jnp.einsum(
-        "thj,thd->jhd", grad_third, key_heads, preferred_element_type=jnp.float32
-    )
-    term_out = jnp.einsum("thj,thd->jhd", hidden_k, scaled_v, preferred_element_type=jnp.float32)
-    term_one = term_one.reshape(full_rows, 1, num_heads, head_size)
-    term_two = term_two.reshape(full_rows, 1, num_heads, head_size)
-    term_out = term_out.reshape(full_rows, 1, num_heads, head_size)
-    sum_one, sum_two, sum_out = add_sources(
-        (
-            lax.all_to_all(term_one, "seq", split_axis=0, concat_axis=1, tiled=True),
-            lax.all_to_all(term_two, "seq", split_axis=0, concat_axis=1, tiled=True),
-            lax.all_to_all(term_out, "seq", split_axis=0, concat_axis=1, tiled=True),
+    terms = (
+        scale_in
+        * jnp.einsum("thj,thd->jhd", grad_first, key_heads, preferred_element_type=jnp.float32),
+        scale_in
+        * jnp.einsum("thj,thd->jhd", grad_third, key_heads, preferred_element_type=jnp.float32),
+        jnp.einsum("thj,thd->jhd", hidden_k, scaled_v, preferred_element_type=jnp.float32),
+    )
+    sums = [
+        jnp.sum(
+            lax.all_to_all(term[:, None], "seq", split_axis=0, concat_axis=1, tiled=True), axis=1
         )
-    )
-    gradient = jnp.stack([sum_one, sum_two, sum_out], axis=1)
+        for term in terms
+    ]
+    gradient = jnp.stack(sums, axis=1)
     partial_gram = jnp.einsum("jmhd,jmhe->mhde", gradient, gradient, precision=exact)
     gram_matrix = lax.psum(partial_gram, "seq")
     poly_factor = newton_factor(gram_matrix)
     update = jnp.einsum("mhde,jmhe->jmhd", poly_factor, gradient, precision=exact)
     renewed = (fast_weights.astype(jnp.float32) - math.sqrt(HID) * update).astype(jnp.bfloat16)
     return (applied, renewed)
+
+
+def body(size, queries, key_vectors, value_vectors, token_rates, fast_weights):
+    planes = size // PLANE
+    if size == PLANE * planes and planes > 1 and fast_weights.shape[2] % planes == 0:
+        return plane_body(
+            queries, key_vectors, value_vectors, token_rates, fast_weights, planes
+        )
+    return gather_body(queries, key_vectors, value_vectors, token_rates, fast_weights)
 
 
 def solution(mesh):
@@ -123,4 +335,10 @@
         P(("groups", "seq"), None, None, None),
     )
     out_specs = (P(("groups", "seq"), None), P(("groups", "seq"), None, None, None))
-    return jax.shard_map(body, mesh=mesh, in_specs=in_specs, out_specs=out_specs, check_vma=False)
+    return jax.shard_map(
+        functools.partial(body, mesh.shape["seq"]),
+        mesh=mesh,
+        in_specs=in_specs,
+        out_specs=out_specs,
+        check_vma=False,
+    )

time: 660 us -> 143 us (0.22)
  waiting for transfers between devices: 422 us -> 62.2 us
  matrix products: 94.4 us -> 0 us
  local copies, waits for them, and re-layouts: 58.1 us -> 18.2 us
  Pallas kernels: 0 us -> 27 us
  starting transfers between devices: 53.3 us -> 31.5 us
  between operations: 14.7 us -> 0.8 us
  other arithmetic: 12.9 us -> 2.62 us
    all_to_all x3 -> x6, waiting for transfers between devices: 230 us -> 39 us  [the longest x5 26 us: along(): lax.all_to_all(array, 'seq', 0, 0, axis_index_groups=lines, tiled=True)]
    psum x1 -> x0, waiting for transfers between devices: 115 us -> none  [body(): gram_matrix = lax.psum(partial_gram, 'seq')]
    dot_general x18 -> x0, matrix products: 94.4 us -> none  [the longest x1 10.5 us: body(): jnp.einsum('thj,thd->jhd', grad_first, key_heads, preferred_element_type=...]
    all_gather x1 -> x0, waiting for transfers between devices: 76.4 us -> none  [body(): gathered = lax.all_gather(fast_weights, 'seq', axis=0, tiled=True)]
    reshape x3 -> x2, local copies, waits for them, and re-layouts: 32 us -> 2.19 us  [split(): return array.reshape(row_count, planes, width).transpose(1, 0, 2)]
    pallas_call x0 -> x3, Pallas kernels: none -> 27 us  [the longest x1 13.7 us: plane_body(): pl.pallas_call(functools.partial(key_kernel, heads), grid=(heads,), in_sp...]
    all_to_all x3 -> x6, starting transfers between devices: 53 us -> 28.4 us  [the longest x5 22.5 us: along(): lax.all_to_all(array, 'seq', 0, 0, axis_index_groups=lines, tiled=True)]
    ppermute x0 -> x5, waiting for transfers between devices: none -> 23.2 us  [swap(): return lax.ppermute(array, 'seq', [(at, at ^ bit) for at in range(size)])]
  transfers between devices with their start and end apart: 5 -> 11, of which waited for: 5 -> 6; matrix products, arithmetic and copies ran while one was open for 11% -> 8% of each run, Pallas kernels for 0% -> 19%
where the time goes in v1:
time: 143 us; the launch traced here: 142 us
  waiting for transfers between devices  62.2 us (43%)
  starting transfers between devices  31.5 us (22%)
  Pallas kernels  27 us (19%)
  local copies, waits for them, and re-layouts  18.2 us (13%)
  other arithmetic  2.62 us (2%)
    all_to_all x5, waiting for transfers between devices, along(): lax.all_to_all(array, 'seq', 0, 0, axis_index_groups=lines, tiled=True)  26 us
    ppermute x5, waiting for transfers between devices, swap(): return lax.ppermute(array, 'seq', [(at, at ^ bit) for at in range(size)])  23.2 us
    all_to_all x5, starting transfers between devices, along(): lax.all_to_all(array, 'seq', 0, 0, axis_index_groups=lines, tiled=True)  22.5 us
    unnamed x30, local copies, waits for them, and re-layouts  13.8 us
    pallas_call x1, Pallas kernels, plane_body(): pl.pallas_call(functools.partial(key_kernel, heads), grid=(heads,), in_sp...  13.7 us
    all_to_all x1, waiting for transfers between devices, plane_body(): lax.all_to_all(renewed.reshape(size, slots, own_rows, head_size), 'seq',...  13 us
    pallas_call x1, Pallas kernels, plane_body(): pl.pallas_call(query_kernel, grid=(heads,), in_specs=[smem, rows_spec] +...  7.35 us
    pallas_call x1, Pallas kernels, plane_body(): pl.pallas_call(renew_kernel, in_specs=[smem] + [pl.BlockSpec(memory_space...  5.94 us
  transfers between devices with their start and end apart: 11, of which 6 were waited for; matrix products, arithmetic and copies ran while one was open for 8% of the time, Pallas kernels for 19%

profile of v1, /device:TPU:0, one launch (start us, length us, event | category | flops | bytes accessed | tf_op | source)
XLA Modules:
  0.0 142.4 jit_solution(17398628911537915599)
XLA Ops:
  0.6 0.0 copy-start.11
  0.6 1.8 %copy.11 = bf16[32,3,20,128]{3,0,1,2:T(8,128)(2,1)} copy(bf16[32,3,20,128]{3,0,2,1:T(8,128)(2,1)} %param.9) | data formatting | bytes 983040 | tf_op args[4]
  2.5 6.3 %all-to-all-start.1 = ((bf16[4,5,3,32,128]{4,3,2,1,0:T(8,128)(2,1)}), bf16[4,5,3,32,128]{4,3,2,1,0:T(8,128)(2,1)S(1)}, u32[]{:S(2)}, u32[]{:S(2)}) async-start(bf16[4,5,3,32,128]{4,3,2,1,0:T(8,128)(2,1)} %bitcast.4), calls=%async_computation.1 | async-start | bytes 983040 | tf_op jit(solution)/shard_map/all_to_all | solution.py:150
  8.8 0.0 copy-done.11
  8.8 0.1 mul.20
  8.9 0.4 copy.16
  9.3 2.2 %copy.15 = bf16[128,2560]{0,1:T(8,128)(2,1)} copy(bf16[128,2560]{1,0:T(8,128)(2,1)} %param.7) | data formatting | bytes 1310720 | tf_op args[2]
  11.5 1.3 copy.17
  12.8 1.0 fusion.2
  13.8 0.0 copy-start.10
  13.8 8.8 %all-to-all-done.1.w0 = bf16[4,5,3,32,128]{4,3,2,1,0:T(8,128)(2,1)S(1)} async-done(((bf16[4,5,3,32,128]{4,3,2,1,0:T(8,128)(2,1)}), bf16[4,5,3,32,128]{4,3,2,1,0:T(8,128)(2,1)S(1)}, u32[]{:S(2)}, u32[]{:S(2)}) %all-to-all-start.1) | async-done | bytes 491552 | tf_op jit(solution)/shard_map/all_to_all | solution.py:150
  22.6 3.5 %all-to-all-start.4 = ((bf16[4,128,640]{2,1,0:T(8,128)(2,1)}), bf16[4,128,640]{2,1,0:T(8,128)(2,1)S(1)}, u32[]{:S(2)}, u32[]{:S(2)}) async-start(bf16[4,128,640]{2,1,0:T(8,128)(2,1)} %fusion.2), calls=%async_computation.4 | async-start | bytes 1310720 | tf_op jit(solution)/shard_map/all_to_all | solution.py:150
  26.1 0.0 copy-done.10
  26.1 0.3 copy.13
  26.4 1.1 copy.14
  27.5 15.3 %all-to-all-done.4.s_ref = bf16[4,128,640]{2,1,0:T(8,128)(2,1)S(1)} async-done(((bf16[4,128,640]{2,1,0:T(8,128)(2,1)}), bf16[4,128,640]{2,1,0:T(8,128)(2,1)S(1)}, u32[]{:S(2)}, u32[]{:S(2)}) %all-to-all-start.4) | async-done | bytes 655392 | tf_op jit(solution)/shard_map/all_to_all | solution.py:150
  42.9 3.5 %all-to-all-start.3 = ((bf16[4,128,640]{2,1,0:T(8,128)(2,1)}), bf16[4,128,640]{2,1,0:T(8,128)(2,1)S(1)}, u32[]{:S(2)}, u32[]{:S(2)}) async-start(bf16[4,128,640]{2,1,0:T(8,128)(2,1)} %bitcast.8), calls=%async_computation.3 | async-start | bytes 1310720 | tf_op jit(solution)/shard_map/all_to_all | solution.py:150
  46.3 1.6 %collective-permute-start.1 = (bf16[4,5,3,32,128]{4,3,2,1,0:T(8,128)(2,1)S(1)}, bf16[4,5,3,32,128]{4,3,2,1,0:T(8,128)(2,1)S(1)}, u32[]{:S(2)}, u32[]{:S(2)}) collective-permute-start(bf16[4,5,3,32,128]{4,3,2,1,0:T(8,128)(2,1)S(1)} %all-to-all-done.1.w0), channel_id=1, source_target_pairs={{0,2},{1,3},{2,0},{3,1},{4,6},{5,7},{6,4},{7,5},{8,10},{9,11},{10,... | collective-permute-start | bytes 1474568 | tf_op jit(solution)/shard_map/ppermute | solution.py:153
  47.9 0.0 collective-permute-start
  47.9 10.6 %collective-permute-done.1.w2 = bf16[4,5,3,32,128]{4,3,2,1,0:T(8,128)(2,1)S(1)} collective-permute-done((bf16[4,5,3,32,128]{4,3,2,1,0:T(8,128)(2,1)S(1)}, bf16[4,5,3,32,128]{4,3,2,1,0:T(8,128)(2,1)S(1)}, u32[]{:S(2)}, u32[]{:S(2)}) %collective-permute-start.1) | collective-permute-done | bytes 491552 | tf_op jit(solution)/shard_map/ppermute | solution.py:153
  58.6 0.0 copy-start.2
  58.6 0.0 collective-permute-start.2
  58.6 1.6 %copy.9 = bf16[128,2560]{0,1:T(8,128)(2,1)S(1)} copy(bf16[128,2560]{1,0:T(8,128)(2,1)} %param.5) | data formatting | bytes 1310720 | tf_op args[0]
  60.2 1.1 copy.10
  61.3 0.0 copy-done.2
  61.3 1.8 %all-to-all-done.3.k_ref = bf16[4,128,640]{2,1,0:T(8,128)(2,1)S(1)} async-done(((bf16[4,128,640]{2,1,0:T(8,128)(2,1)}), bf16[4,128,640]{2,1,0:T(8,128)(2,1)S(1)}, u32[]{:S(2)}, u32[]{:S(2)}) %all-to-all-start.3) | async-done | bytes 655392 | tf_op jit(solution)/shard_map/all_to_all | solution.py:150
  63.1 0.0 copy-start
  63.1 4.2 %all-to-all-start = ((bf16[4,128,640]{2,1,0:T(8,128)(2,1)}), bf16[4,128,640]{2,1,0:T(8,128)(2,1)}, u32[]{:S(2)}, u32[]{:S(2)}) async-start(bf16[4,128,640]{2,1,0:T(8,128)(2,1)} %bitcast.2), calls=%async_computation | async-start | bytes 1310720 | tf_op jit(solution)/shard_map/all_to_all | solution.py:150
  67.3 0.0 collective-permute-done.w1
  67.3 0.0 copy-start.6
  67.3 0.8 copy-done.6
  68.1 0.0 collective-permute-done.2.w3
  68.1 0.0 copy-done
  68.1 0.0 copy-start.1
  68.1 1.1 copy-done.1
  69.2 0.0 copy-start.3
  69.2 1.0 copy-done.3
  70.2 0.0 copy-start.7
  70.2 1.0 copy-done.7
  71.2 13.7 %key_side.1 = (f32[2,4,512,128]{3,2,1,0:T(8,128)S(1)}, bf16[2,4,512,128]{3,2,1,0:T(8,128)(2,1)}) custom-call(s32[1]{0:T(128)} %bitcast.place_ref, bf16[4,128,640]{2,1,0:T(8,128)(2,1)S(1)} %copy-done.1, bf16[4,128,640]{2,1,0:T(8,128)(2,1)S(1)} %all-to-all-done.4.s_ref, bf16[4,5,3,32,128]{4,3,2,1,0:T(8,128)(2,1)S(1)} %all-to-all-done.1.w0, ...), custom_call_target="tpu_custom_call" | custom-call | flops 2000000000 | bytes 10000000 | tf_op jit(solution)/shard_map/key_side/pallas_call | solution.py:179
  85.0 0.0 collective-permute-start.3
  85.0 0.0 all-to-all-done.q_ref
  85.0 0.0 copy-start.4
  85.0 1.0 copy-done.4
  86.0 0.0 copy-start.8
  86.0 1.0 copy-done.8
  87.0 7.3 %query_side.1 = bf16[4,128,640]{2,1,0:T(8,128)(2,1)} custom-call(s32[1]{0:T(128)} %bitcast.place_ref, bf16[4,128,640]{2,1,0:T(8,128)(2,1)} %all-to-all-done.q_ref, bf16[4,5,3,32,128]{4,3,2,1,0:T(8,128)(2,1)S(1)} %all-to-all-done.1.w0, bf16[4,5,3,32,128]{4,3,2,1,0:T(8,128)(2,1)S(1)} %copy-done.8, bf16[4,5,3,32,128]{4,3,2,1,0:T(8,128)(2,1)S(1)} %copy-done.4, ...), custom_call_target="tpu_custom_call" | custom-call | flops 1000000000 | bytes 10000000 | tf_op jit(solution)/shard_map/query_side/pallas_call | solution.py:218
  94.4 5.0 %all-to-all-start.2 = ((bf16[4,128,640]{2,1,0:T(8,128)(2,1)}), bf16[4,128,640]{2,1,0:T(8,128)(2,1)S(1)}, u32[]{:S(2)}, u32[]{:S(2)}) async-start(bf16[4,128,640]{2,1,0:T(8,128)(2,1)} %query_side.1), calls=%async_computation.2 | async-start | bytes 1310720 | tf_op jit(solution)/shard_map/all_to_all | solution.py:150
  99.4 0.0 collective-permute-done.3
  99.4 1.4 convert_element_type.23
  100.8 0.0 copy-start.5
  100.8 0.0 copy-start.9
  100.8 0.3 fusion.3
  101.1 1.6 %collective-permute-start.4 = (bf16[4,512,128]{2,1,0:T(8,128)(2,1)S(1)}, bf16[4,512,128]{2,1,0:T(8,128)(2,1)S(1)}, u32[]{:S(2)}, u32[]{:S(2)}) collective-permute-start(bf16[4,512,128]{2,1,0:T(8,128)(2,1)S(1)} %get-tuple-element.8), channel_id=1, source_target_pairs={{0,2},{1,3},{2,0},{3,1},{4,6},{5,7},{6,4},{7,5},{8,10},{9,11},{10,... | collective-permute-start | bytes 1572872 | tf_op jit(solution)/shard_map/ppermute | solution.py:153
  102.7 12.5 %collective-permute-done.4.got_ref = bf16[4,512,128]{2,1,0:T(8,128)(2,1)S(1)} collective-permute-done((bf16[4,512,128]{2,1,0:T(8,128)(2,1)S(1)}, bf16[4,512,128]{2,1,0:T(8,128)(2,1)S(1)}, u32[]{:S(2)}, u32[]{:S(2)}) %collective-permute-start.4) | collective-permute-done | bytes 524320 | tf_op jit(solution)/shard_map/ppermute | solution.py:153
  115.2 0.0 copy-done.5
  115.2 0.0 copy-done.9
  115.2 5.9 %renew.1 = bf16[4,4,4,32,128]{4,3,2,1,0:T(8,128)(2,1)} custom-call(s32[1]{0:T(128)} %bitcast.place_ref, f32[4,512,128]{2,1,0:T(8,128)S(1)} %get-tuple-element.9.mine_ref, bf16[4,512,128]{2,1,0:T(8,128)(2,1)S(1)} %collective-permute-done.4.got_ref, bf16[4,5,3,32,128]{4,3,2,1,0:T(8,128)(2,1)S(1)} %all-to-all-done.1.w0, ...), custom_call_target="tpu_custom_call" | custom-call | flops 1000000000 | bytes 10000000 | tf_op jit(solution)/shard_map/renew/pallas_call | solution.py:199
  121.2 0.0 all-to-all-done.2
  121.2 5.9 %all-to-all-start.5 = ((bf16[16,4,32,128]{3,2,1,0:T(8,128)(2,1)}), bf16[16,4,32,128]{3,2,1,0:T(8,128)(2,1)S(1)}, u32[]{:S(2)}, u32[]{:S(2)}) async-start(bf16[16,4,32,128]{3,2,1,0:T(8,128)(2,1)} %bitcast.14), calls=%async_computation.5 | async-start | bytes 1048576 | tf_op jit(solution)/shard_map/all_to_all | solution.py:209
  127.1 0.3 copy.12
  127.4 1.1 copy.18
  128.5 13.0 %all-to-all-done.5 = bf16[16,4,32,128]{3,2,1,0:T(8,128)(2,1)S(1)} async-done(((bf16[16,4,32,128]{3,2,1,0:T(8,128)(2,1)}), bf16[16,4,32,128]{3,2,1,0:T(8,128)(2,1)S(1)}, u32[]{:S(2)}, u32[]{:S(2)}) %all-to-all-start.5) | async-done | bytes 524320 | tf_op jit(solution)/shard_map/all_to_all | solution.py:209
  141.6 0.8 copy.19
  (2 shorter events, 0.0 us)
Async XLA Ops:
  0.6 8.2 %copy-start.11 = (f32[128,20]{0,1:T(8,128)S(1)}, f32[128,20]{0,1:T(8,128)}, u32[]{:S(2)}) copy-start(f32[128,20]{0,1:T(8,128)} %param.8) | copy-start | bytes 30724
  2.5 20.1 %all-to-all-start.1 = ((bf16[4,5,3,32,128]{4,3,2,1,0:T(8,128)(2,1)}), bf16[4,5,3,32,128]{4,3,2,1,0:T(8,128)(2,1)S(1)}, u32[]{:S(2)}, u32[]{:S(2)}) async-start(bf16[4,5,3,32,128]{4,3,2,1,0:T(8,128)(2,1)} %bitcast.4), calls=%async_computation.1 | async-start | bytes 983040 | tf_op jit(solution)/shard_map/all_to_all | solution.py:150
  13.8 12.3 %copy-start.10 = (bf16[128,2560]{1,0:T(8,128)(2,1)S(1)}, bf16[128,2560]{1,0:T(8,128)(2,1)}, u32[]{:S(2)}) copy-start(bf16[128,2560]{1,0:T(8,128)(2,1)} %param.6) | copy-start | bytes 1966084
  22.6 20.3 %all-to-all-start.4 = ((bf16[4,128,640]{2,1,0:T(8,128)(2,1)}), bf16[4,128,640]{2,1,0:T(8,128)(2,1)S(1)}, u32[]{:S(2)}, u32[]{:S(2)}) async-start(bf16[4,128,640]{2,1,0:T(8,128)(2,1)} %fusion.2), calls=%async_computation.4 | async-start | bytes 1310720 | tf_op jit(solution)/shard_map/all_to_all | solution.py:150
  42.9 20.2 %all-to-all-start.3 = ((bf16[4,128,640]{2,1,0:T(8,128)(2,1)}), bf16[4,128,640]{2,1,0:T(8,128)(2,1)S(1)}, u32[]{:S(2)}, u32[]{:S(2)}) async-start(bf16[4,128,640]{2,1,0:T(8,128)(2,1)} %bitcast.8), calls=%async_computation.3 | async-start | bytes 1310720 | tf_op jit(solution)/shard_map/all_to_all | solution.py:150
  46.3 12.2 %collective-permute-start.1 = (bf16[4,5,3,32,128]{4,3,2,1,0:T(8,128)(2,1)S(1)}, bf16[4,5,3,32,128]{4,3,2,1,0:T(8,128)(2,1)S(1)}, u32[]{:S(2)}, u32[]{:S(2)}) collective-permute-start(bf16[4,5,3,32,128]{4,3,2,1,0:T(8,128)(2,1)S(1)} %all-to-all-done.1.w0), channel_id=1, source_target_pairs={{0,2},{1,3},{2,0},{3,1},{4,6},{5,7},{6,4},{7,5},{8,10},{9,11},{10,... | collective-permute-start | bytes 1474568 | tf_op jit(solution)/shard_map/ppermute | solution.py:153
  47.9 19.3 %collective-permute-start = (bf16[4,5,3,32,128]{4,3,2,1,0:T(8,128)(2,1)S(1)}, bf16[4,5,3,32,128]{4,3,2,1,0:T(8,128)(2,1)S(1)}, u32[]{:S(2)}, u32[]{:S(2)}) collective-permute-start(bf16[4,5,3,32,128]{4,3,2,1,0:T(8,128)(2,1)S(1)} %all-to-all-done.1.w0), channel_id=1, source_target_pairs={{0,1},{1,0},{2,3},{3,2},{4,5},{5,4},{6,7},{7,6},{8,9},{9,8},{10,11... | collective-permute-start | bytes 1474568 | tf_op jit(solution)/shard_map/ppermute | solution.py:153
  58.6 2.7 %copy-start.2 = (bf16[4,5,3,32,128]{4,3,2,1,0:T(8,128)(2,1)}, bf16[4,5,3,32,128]{4,3,2,1,0:T(8,128)(2,1)S(1)}, u32[]{:S(2)}) copy-start(bf16[4,5,3,32,128]{4,3,2,1,0:T(8,128)(2,1)S(1)} %collective-permute-done.1.w2) | copy-start | bytes 1474564
  58.6 9.5 %collective-permute-start.2 = (bf16[4,5,3,32,128]{4,3,2,1,0:T(8,128)(2,1)S(1)}, bf16[4,5,3,32,128]{4,3,2,1,0:T(8,128)(2,1)}, u32[]{:S(2)}, u32[]{:S(2)}) collective-permute-start(bf16[4,5,3,32,128]{4,3,2,1,0:T(8,128)(2,1)S(1)} %collective-permute-done.1.w2), channel_id=1, source_target_pairs={{0,1},{1,0},{2,3},{3,2},{4,5},{5,4},{6,7},{7,6},{8,9},{9,8},{10,11... | collective-permute-start | bytes 1474568 | tf_op jit(solution)/shard_map/ppermute | solution.py:153
  63.1 5.0 %copy-start = (bf16[4,128,640]{2,1,0:T(8,128)(2,1)}, bf16[4,128,640]{2,1,0:T(8,128)(2,1)S(1)}, u32[]{:S(2)}) copy-start(bf16[4,128,640]{2,1,0:T(8,128)(2,1)S(1)} %all-to-all-done.3.k_ref) | copy-start | bytes 1966084
  63.1 21.9 %all-to-all-start = ((bf16[4,128,640]{2,1,0:T(8,128)(2,1)}), bf16[4,128,640]{2,1,0:T(8,128)(2,1)}, u32[]{:S(2)}, u32[]{:S(2)}) async-start(bf16[4,128,640]{2,1,0:T(8,128)(2,1)} %bitcast.2), calls=%async_computation | async-start | bytes 1310720 | tf_op jit(solution)/shard_map/all_to_all | solution.py:150
  67.3 0.8 copy-start.6
  68.1 1.1 copy-start.1
  69.2 1.0 copy-start.3
  70.2 1.0 copy-start.7
  85.0 14.5 %collective-permute-start.3 = (bf16[2,4,512,128]{3,2,1,0:T(8,128)(2,1)}, bf16[2,4,512,128]{3,2,1,0:T(8,128)(2,1)}, u32[]{:S(2)}, u32[]{:S(2)}) collective-permute-start(bf16[2,4,512,128]{3,2,1,0:T(8,128)(2,1)} %get-tuple-element.5), channel_id=1, source_target_pairs={{0,1},{1,0},{2,3},{3,2},{4,5},{5,4},{6,7},{7,6},{8,9},{9,8},{10,11... | collective-permute-start | bytes 3145736 | tf_op jit(solution)/shard_map/ppermute | solution.py:153
  85.0 1.0 copy-start.4
  86.0 1.0 copy-start.8
  94.4 26.8 %all-to-all-start.2 = ((bf16[4,128,640]{2,1,0:T(8,128)(2,1)}), bf16[4,128,640]{2,1,0:T(8,128)(2,1)S(1)}, u32[]{:S(2)}, u32[]{:S(2)}) async-start(bf16[4,128,640]{2,1,0:T(8,128)(2,1)} %query_side.1), calls=%async_computation.2 | async-start | bytes 1310720 | tf_op jit(solution)/shard_map/all_to_all | solution.py:150
  100.8 14.4 %copy-start.5 = (bf16[4,5,3,32,128]{4,3,2,1,0:T(8,128)(2,1)S(1)}, bf16[4,5,3,32,128]{4,3,2,1,0:T(8,128)(2,1)}, u32[]{:S(2)}) copy-start(bf16[4,5,3,32,128]{4,3,2,1,0:T(8,128)(2,1)} %copy-done.2) | copy-start | bytes 1474564
  100.8 14.4 %copy-start.9 = (bf16[4,5,3,32,128]{4,3,2,1,0:T(8,128)(2,1)S(1)}, bf16[4,5,3,32,128]{4,3,2,1,0:T(8,128)(2,1)}, u32[]{:S(2)}) copy-start(bf16[4,5,3,32,128]{4,3,2,1,0:T(8,128)(2,1)} %copy-done.6) | copy-start | bytes 1474564
  101.1 14.1 %collective-permute-start.4 = (bf16[4,512,128]{2,1,0:T(8,128)(2,1)S(1)}, bf16[4,512,128]{2,1,0:T(8,128)(2,1)S(1)}, u32[]{:S(2)}, u32[]{:S(2)}) collective-permute-start(bf16[4,512,128]{2,1,0:T(8,128)(2,1)S(1)} %get-tuple-element.8), channel_id=1, source_target_pairs={{0,2},{1,3},{2,0},{3,1},{4,6},{5,7},{6,4},{7,5},{8,10},{9,11},{10,... | collective-permute-start | bytes 1572872 | tf_op jit(solution)/shard_map/ppermute | solution.py:153
  121.2 20.4 %all-to-all-start.5 = ((bf16[16,4,32,128]{3,2,1,0:T(8,128)(2,1)}), bf16[16,4,32,128]{3,2,1,0:T(8,128)(2,1)S(1)}, u32[]{:S(2)}, u32[]{:S(2)}) async-start(bf16[16,4,32,128]{3,2,1,0:T(8,128)(2,1)} %bitcast.14), calls=%async_computation.5 | async-start | bytes 1048576 | tf_op jit(solution)/shard_map/all_to_all | solution.py:209

commit v2 on v0

--- a/solution.py
+++ b/solution.py
@@ -1,17 +1,346 @@
+import functools
 import math
 
 import jax
 import jax.numpy as jnp
 from jax import lax
+from jax.experimental import pallas as pl
+from jax.experimental.pallas import tpu as pltpu
 from jax.sharding import PartitionSpec as P
 
 HID = 512
 NS_STEPS = 2
-
+PLACES = 4
 
 coef_a = 3.4445
 coef_b = -4.775
 coef_c = 2.0315
+
+VMEM = pltpu.VMEM
+SMEM = pltpu.SMEM
+NT = (((1,), (1,)), ((), ()))
+NN = (((1,), (0,)), ((), ()))
+TN = (((0,), (0,)), ((), ()))
+
+
+def dot(a, b, dims, precision=None):
+    return lax.dot_general(a, b, dims, precision=precision, preferred_element_type=jnp.float32)
+
+
+def split_kernel(where_ref, q_ref, k_ref, v_ref, rate_ref, *refs):
+    outs, scaled = refs[:-1], refs[-1]
+    spot = where_ref[0]
+    width = outs[0].shape[2]
+    num_heads = rate_ref.shape[1]
+    head_size = k_ref.shape[1] // num_heads
+    rates = (-1.0 / math.sqrt(HID)) * rate_ref[...]
+    for head in range(num_heads):
+        at = slice(head * head_size, (head + 1) * head_size)
+        scaled[:, at] = (rates[:, head : head + 1] * v_ref[:, at].astype(jnp.float32)).astype(
+            jnp.bfloat16
+        )
+    for rel, out_ref in enumerate(outs):
+        at = pl.multiple_of((spot ^ rel) * width, width)
+        out_ref[0] = k_ref[:, pl.ds(at, width)]
+        out_ref[1] = scaled[:, pl.ds(at, width)]
+        out_ref[2] = q_ref[:, pl.ds(at, width)]
+
+
+def join_kernel(where_ref, *refs):
+    ins, (out_ref, done_ref) = refs[:-2], refs[-2:]
+    spot = where_ref[0]
+    width = ins[0].shape[1]
+    for rel, in_ref in enumerate(ins):
+        at = pl.multiple_of((spot ^ rel) * width, width)
+        out_ref[:, pl.ds(at, width)] = in_ref[...]
+    done_ref[...] = jnp.zeros_like(done_ref)
+
+
+def weight_rows(w_refs, rel, matrix):
+    pieces = w_refs[2 * rel : 2 * rel + 2]
+    return jnp.concatenate(
+        [w[at, 0, matrix] for w in pieces for at in range(w.shape[0])], axis=0
+    )
+
+
+def key_kernel(squares, begin, first_slot, slots, last, where_ref, *refs):
+    pairs, w_refs, carried = refs[:squares], refs[squares : squares + 8], refs[squares + 8]
+    keep_ref, near_ref = refs[squares + 9 : squares + 11]
+    far_refs = refs[squares + 11 : squares + 11 + slots]
+    carry_ref, terms = refs[-2:]
+    spot, place = where_ref[0], where_ref[1]
+    _, hid, head_size = terms.shape
+    rows = hid // (PLACES * squares)
+    step = pl.program_id(0)
+    scale_in = 1.0 / math.sqrt(head_size)
+
+    def put(number, value):
+        rel = (number % PLACES) ^ place
+        slot = number // PLACES - first_slot
+
+        @pl.when((rel % 2 == 0) & (slot < slots))
+        def _():
+            keep_ref[rel // 2, slot] = value
+
+        @pl.when((rel == 1) & (slot < slots))
+        def _():
+            near_ref[slot] = value.astype(near_ref.dtype)
+
+        for one in range(slots):
+
+            @pl.when((rel == 3) & (slot == one))
+            def _():
+                far_refs[one][...] = value.astype(far_refs[one].dtype)
+
+        if not last:
+
+            @pl.when(slot >= slots)
+            def _():
+                carry_ref[number - PLACES * (first_slot + slots)] = value
+
+    @pl.when(step == 0)
+    def _():
+        if first_slot:
+            for number in range(PLACES * first_slot, 3 * begin):
+                put(number, carried[number - PLACES * first_slot])
+        if last:
+            for number in range(3 * last, PLACES * (first_slot + slots)):
+                put(number, jnp.zeros((hid, head_size), jnp.float32))
+
+    keys = jnp.concatenate([pair[0] for pair in pairs], axis=0)
+    scaled = jnp.concatenate([pair[1] for pair in pairs], axis=0)
+    for rel in range(PLACES):
+        raw_first = dot(weight_rows(w_refs, rel, 0), keys, NT)
+        raw_third = dot(weight_rows(w_refs, rel, 1), keys, NT)
+        back = dot(weight_rows(w_refs, rel, 2), scaled, NT)
+        first = raw_first * scale_in
+        sig = 0.5 * jnp.tanh(0.5 * first) + 0.5
+        act = first * sig
+        hidden = (act * raw_third).astype(jnp.bfloat16)
+        grad_third = (back * act).astype(jnp.bfloat16)
+        slope = sig + act * (1.0 - sig)
+        grad_first = (back * raw_third * slope).astype(jnp.bfloat16)
+        values = (
+            dot(grad_first, keys, NN) * (scale_in * scale_in),
+            dot(grad_third, keys, NN) * scale_in,
+            dot(hidden, scaled, NN) * scale_in,
+        )
+        for apart in range(squares):
+            to = pl.multiple_of(((place ^ rel) * squares + (spot ^ apart)) * rows, rows)
+            for matrix in range(3):
+                terms[matrix, pl.ds(to, rows), :] = values[matrix][apart * rows : (apart + 1) * rows]
+    for matrix in range(3):
+        put(3 * (begin + step) + matrix, terms[matrix])
+
+
+def query_kernel(squares, *refs):
+    ins, w_refs, outs = refs[:squares], refs[squares : squares + 8], refs[-squares:]
+    scale_in = 1.0 / math.sqrt(ins[0].shape[2])
+    scale_out = 1.0 / math.sqrt(HID)
+    first_map, third_map, second = (
+        jnp.concatenate([weight_rows(w_refs, rel, matrix) for rel in range(PLACES)], axis=0)
+        for matrix in range(3)
+    )
+    for q_ref, out_ref in zip(ins, outs):
+        queries = q_ref[0]
+        first = dot(queries, first_map, NT) * scale_in
+        third = dot(queries, third_map, NT) * scale_in
+        sig = 0.5 * jnp.tanh(0.5 * first) + 0.5
+        hidden = (first * sig * third).astype(jnp.bfloat16)
+        out_ref[...] = (dot(hidden, second, NN) * scale_out).astype(out_ref.dtype)
+
+
+def renew_kernel(squares, first_slot, where_ref, mine_ref, near_ref, far_ref, *refs):
+    w_refs, (out_ref, updates) = refs[:8], refs[-2:]
+    spot, place = where_ref[0], where_ref[1]
+    slots, hid, head_size = far_ref.shape
+    heads = w_refs[0].shape[1]
+    rows = out_ref.shape[2]
+    exact = lax.Precision.HIGHEST
+    eye = (
+        lax.broadcasted_iota(jnp.int32, (head_size, head_size), 0)
+        == lax.broadcasted_iota(jnp.int32, (head_size, head_size), 1)
+    ).astype(jnp.float32)
+    grads = [
+        mine_ref[0, slot]
+        + near_ref[slot].astype(jnp.float32)
+        + far_ref[slot].astype(jnp.float32)
+        for slot in range(slots)
+    ]
+    grams = [dot(grad, grad, TN, exact) for grad in grads]
+    factors = [eye * (1.0 / (jnp.sqrt(jnp.sum(gram * eye)) + 1e-07)) for gram in grams]
+    for _ in range(NS_STEPS):
+        inner = [dot(gram, factor, NN, exact) for gram, factor in zip(grams, factors)]
+        square = [dot(factor, term, NN, exact) for factor, term in zip(factors, inner)]
+        mixed = [coef_b * term + coef_c * dot(term, term, NN, exact) for term in square]
+        factors = [
+            coef_a * factor + dot(term, factor, NN, exact) for term, factor in zip(mixed, factors)
+        ]
+    for slot in range(slots):
+        updates[slot] = math.sqrt(HID) * dot(grads[slot], factors[slot], NT, exact)
+    for slot in range(slots):
+        number = jnp.minimum(PLACES * (first_slot + slot) + place, 3 * heads - 1)
+        head, matrix = number // 3, number % 3
+        for rel in range(PLACES):
+            owner = place ^ rel
+            for apart in range(squares):
+                w = w_refs[2 * rel + apart // (squares // 2)]
+                at = pl.multiple_of((owner * squares + (spot ^ apart)) * rows, rows)
+                to = (owner // 2 * squares + (spot ^ apart)) * 2 + owner % 2
+                old = w[apart % (squares // 2), head, matrix].astype(jnp.float32)
+                out_ref[to, slot] = (old - updates[slot, pl.ds(at, rows), :]).astype(out_ref.dtype)
+
+
+def square_body(queries, key_vectors, value_vectors, token_rates, fast_weights, squares):
+    row_count = queries.shape[0]
+    own_rows, _, num_heads, head_size = fast_weights.shape
+    heads = num_heads // squares
+    width = heads * head_size
+    size = squares * PLACES
+    half = size // 2
+    hid = size * own_rows
+    cut = squares // 2
+    position = lax.axis_index("seq").astype(jnp.int32)
+    spot = position % half // 2
+    where = jnp.stack([spot, 2 * (position // half) + position % 2])
+    params = pltpu.CompilerParams(vmem_limit_bytes=40 * 2**20)
+    smem = pl.BlockSpec(memory_space=SMEM)
+    vmem = pl.BlockSpec(memory_space=VMEM)
+
+    def cost(mega_flops):
+        return pl.CostEstimate(
+            flops=mega_flops * 10**6, bytes_accessed=4 * 10**6, transcendentals=0
+        )
+
+    def swap(array, step):
+        return lax.ppermute(array, "seq", [(at, at ^ step) for at in range(size)])
+
+    def across(pieces):
+        return [pieces[0]] + [swap(pieces[rel], 2 * rel) for rel in range(1, squares)]
+
+    def bf16(*shape):
+        return jax.ShapeDtypeStruct(shape, jnp.bfloat16)
+
+    token = jax.ShapeDtypeStruct((8, 128), jnp.float32)
+
+    moved = across(
+        pl.pallas_call(
+            split_kernel,
+            in_specs=[smem] + [vmem] * 4,
+            out_specs=[vmem] * squares,
+            out_shape=[bf16(3, row_count, width)] * squares,
+            scratch_shapes=[VMEM((row_count, num_heads * head_size), jnp.bfloat16)],
+            compiler_params=params,
+            cost_estimate=cost(10),
+            name="split",
+        )(where, queries, key_vectors, value_vectors, token_rates)
+    )
+
+    by_spot = fast_weights.reshape(own_rows, 3, squares, heads, head_size).transpose(2, 3, 1, 0, 4)
+    pieces = across(
+        [
+            lax.dynamic_index_in_dim(by_spot, spot ^ rel, 0, keepdims=False)
+            for rel in range(squares)
+        ]
+    )
+    own = [jnp.stack(pieces[:cut]), jnp.stack(pieces[cut:])]
+    other = [swap(w, half) for w in own]
+    weights = [own, [swap(w, 1) for w in own], other, [swap(w, 1) for w in other]]
+    weights = [w for pair in weights for w in pair]
+
+    def weight_spec(begin=0):
+        return pl.BlockSpec((cut, 1, 3, own_rows, head_size), lambda h: (0, h + begin, 0, 0, 0))
+
+    def key_side(begin, end, first_slot, slots, carry_count, carried):
+        keep_shape = (2, slots, hid, head_size)
+        carry_shape = (max(carry_count, 1), hid, head_size)
+
+        def whole(shape):
+            return pl.BlockSpec(shape, lambda h: (0,) * len(shape))
+
+        return pl.pallas_call(
+            functools.partial(
+                key_kernel, squares, begin, first_slot, slots, heads if end == heads else 0
+            ),
+            grid=(end - begin,),
+            in_specs=[
+                smem,
+                *[pl.BlockSpec((2, row_count, head_size), lambda h: (0, 0, h + begin))] * squares,
+                *[weight_spec(begin)] * 8,
+                whole(carried.shape) if begin else smem,
+            ],
+            out_specs=[whole(keep_shape), whole(keep_shape[1:])]
+            + [whole(keep_shape[2:])] * slots
+            + [whole(carry_shape)],
+            out_shape=[jax.ShapeDtypeStruct(keep_shape, jnp.float32), bf16(*keep_shape[1:])]
+            + [bf16(*keep_shape[2:])] * slots
+            + [jax.ShapeDtypeStruct(carry_shape, jnp.float32)],
+            scratch_shapes=[VMEM((3, hid, head_size), jnp.float32)],
+            compiler_params=params,
+            cost_estimate=cost(1000),
+            name="key_side",
+        )(where, *moved, *weights, carried)
+
+    def add_up(keep, near, *far):
+        got = jnp.stack([swap(one, 1) for one in far])
+        other = (keep[1] + got.astype(jnp.float32)).astype(jnp.bfloat16)
+        return keep, swap(near, 1), swap(other, half)
+
+    middle = -(-heads // 2)
+    slots_all = -(-3 * heads // PLACES)
+    slots_one = 3 * middle // PLACES
+    *sums_one, carry = key_side(0, middle, 0, slots_one, 3 * middle - PLACES * slots_one, where)
+    sums_one = add_up(*sums_one)
+    *sums_two, _ = key_side(middle, heads, slots_one, slots_all - slots_one, 0, carry)
+    sums_two = add_up(*sums_two)
+
+    columns = pl.BlockSpec((row_count, head_size), lambda h: (0, h))
+    parts = pl.pallas_call(
+        functools.partial(query_kernel, squares),
+        grid=(heads,),
+        in_specs=[pl.BlockSpec((1, row_count, head_size), lambda h: (2, 0, h))] * squares
+        + [weight_spec()] * 8,
+        out_specs=[columns] * squares,
+        out_shape=[bf16(row_count, width)] * squares,
+        compiler_params=params,
+        cost_estimate=cost(1000),
+        name="query_side",
+    )(*moved, *weights)
+    applied, joined = pl.pallas_call(
+        join_kernel,
+        in_specs=[smem] + [vmem] * squares,
+        out_specs=[vmem] * 2,
+        out_shape=[bf16(row_count, num_heads * head_size), token],
+        compiler_params=params,
+        cost_estimate=cost(10),
+        name="join",
+    )(where, *across(parts))
+
+    def renew(keep, near, far, first_slot, before):
+        slots = far.shape[0]
+        return pl.pallas_call(
+            functools.partial(renew_kernel, squares, first_slot),
+            in_specs=[smem] + [vmem] * (11 + len(before)),
+            out_specs=vmem,
+            out_shape=bf16(size, slots, own_rows, head_size),
+            scratch_shapes=[VMEM((slots, hid, head_size), jnp.float32)],
+            compiler_params=params,
+            cost_estimate=cost(1000),
+            name="renew",
+        )(where, keep, near, far, *weights, *before)
+
+    renewed = jnp.concatenate(
+        [renew(*sums_one, 0, ()), renew(*sums_two, slots_one, (joined,))], axis=1
+    )
+    back = lax.all_to_all(renewed, "seq", 0, 0, tiled=True)
+    back = back.reshape(2, squares, 2, slots_all, own_rows, head_size).transpose(1, 3, 0, 2, 4, 5)
+    back = back.reshape(squares, PLACES * slots_all, own_rows, head_size)[:, : 3 * heads]
+    renewed_out = (
+        back.reshape(squares, heads, 3, own_rows, head_size)
+        .transpose(3, 2, 0, 1, 4)
+        .reshape(own_rows, 3, num_heads, head_size)
+    )
+    return applied, renewed_out
 
 
 def newton_factor(gram_matrix):
@@ -61,15 +390,7 @@
     return (partial_out, hidden_k, grad_first, grad_third)
 
 
-def add_sources(received):
-    return (
-        jnp.sum(received[0], axis=1),
-        jnp.sum(received[1], axis=1),
-        jnp.sum(received[2], axis=1),
-    )
-
-
-def body(queries, key_vectors, value_vectors, token_rates, fast_weights):
+def gather_body(queries, key_vectors, value_vectors, token_rates, fast_weights):
     exact = lax.Precision.HIGHEST
     row_count = queries.shape[0]
     num_heads = fast_weights.shape[2]
@@ -87,31 +408,40 @@
         query_heads, key_heads, scaled_v, gathered
     )
     applied = out_sum.astype(jnp.bfloat16).reshape(row_count, num_heads * head_size)
-    full_rows = HID
-    term_one = scale_in * jnp.einsum(
-        "thj,thd->jhd", grad_first, key_heads, preferred_element_type=jnp.float32
-    )
-    term_two = scale_in * jnp.einsum(
-        "thj,thd->jhd", grad_third, key_heads, preferred_element_type=jnp.float32
-    )
-    term_out = jnp.einsum("thj,thd->jhd", hidden_k, scaled_v, preferred_element_type=jnp.float32)
-    term_one = term_one.reshape(full_rows, 1, num_heads, head_size)
-    term_two = term_two.reshape(full_rows, 1, num_heads, head_size)
-    term_out = term_out.reshape(full_rows, 1, num_heads, head_size)
-    sum_one, sum_two, sum_out = add_sources(
-        (
-            lax.all_to_all(term_one, "seq", split_axis=0, concat_axis=1, tiled=True),
-            lax.all_to_all(term_two, "seq", split_axis=0, concat_axis=1, tiled=True),
-            lax.all_to_all(term_out, "seq", split_axis=0, concat_axis=1, tiled=True),
+    terms = (
+        scale_in
+        * jnp.einsum("thj,thd->jhd", grad_first, key_heads, preferred_element_type=jnp.float32),
+        scale_in
+        * jnp.einsum("thj,thd->jhd", grad_third, key_heads, preferred_element_type=jnp.float32),
+        jnp.einsum("thj,thd->jhd", hidden_k, scaled_v, preferred_element_type=jnp.float32),
+    )
+    sums = [
+        jnp.sum(
+            lax.all_to_all(term[:, None], "seq", split_axis=0, concat_axis=1, tiled=True), axis=1
         )
-    )
-    gradient = jnp.stack([sum_one, sum_two, sum_out], axis=1)
+        for term in terms
+    ]
+    gradient = jnp.stack(sums, axis=1)
     partial_gram = jnp.einsum("jmhd,jmhe->mhde", gradient, gradient, precision=exact)
     gram_matrix = lax.psum(partial_gram, "seq")
     poly_factor = newton_factor(gram_matrix)
     update = jnp.einsum("mhde,jmhe->jmhd", poly_factor, gradient, precision=exact)
     renewed = (fast_weights.astype(jnp.float32) - math.sqrt(HID) * update).astype(jnp.bfloat16)
     return (applied, renewed)
+
+
+def body(size, queries, key_vectors, value_vectors, token_rates, fast_weights):
+    squares = size // PLACES
+    if (
+        size == PLACES * squares
+        and squares > 1
+        and squares & (squares - 1) == 0
+        and fast_weights.shape[2] % squares == 0
+    ):
+        return square_body(
+            queries, key_vectors, value_vectors, token_rates, fast_weights, squares
+        )
+    return gather_body(queries, key_vectors, value_vectors, token_rates, fast_weights)
 
 
 def solution(mesh):
@@ -123,4 +453,10 @@
         P(("groups", "seq"), None, None, None),
     )
     out_specs = (P(("groups", "seq"), None), P(("groups", "seq"), None, None, None))
-    return jax.shard_map(body, mesh=mesh, in_specs=in_specs, out_specs=out_specs, check_vma=False)
+    return jax.shard_map(
+        functools.partial(body, mesh.shape["seq"]),
+        mesh=mesh,
+        in_specs=in_specs,
+        out_specs=out_specs,
+        check_vma=False,
+    )

time: 660 us -> 122 us (0.18)
  waiting for transfers between devices: 422 us -> 50.9 us
  matrix products: 94.4 us -> 0 us
  local copies, waits for them, and re-layouts: 58.1 us -> 2.87 us
  starting transfers between devices: 53.3 us -> 19.9 us
  Pallas kernels: 0 us -> 27.4 us
  blocking collectives: 0 us -> 19.1 us
  between operations: 14.7 us -> 0.87 us
  other arithmetic: 12.9 us -> 0.32 us
    all_to_all x3 -> x0, waiting for transfers between devices: 230 us -> none  [the longest x1 78.5 us: body(): lax.all_to_all(term_one, 'seq', split_axis=0, concat_axis=1, tiled=True)]
    psum x1 -> x0, waiting for transfers between devices: 115 us -> none  [body(): gram_matrix = lax.psum(partial_gram, 'seq')]
    dot_general x18 -> x0, matrix products: 94.4 us -> none  [the longest x1 10.5 us: body(): jnp.einsum('thj,thd->jhd', grad_first, key_heads, preferred_element_type=...]
    all_gather x1 -> x0, waiting for transfers between devices: 76.4 us -> none  [body(): gathered = lax.all_gather(fast_weights, 'seq', axis=0, tiled=True)]
    all_to_all x3 -> x0, starting transfers between devices: 53 us -> none  [the longest x1 24 us: body(): lax.all_to_all(term_two, 'seq', split_axis=0, concat_axis=1, tiled=True)]
    ppermute x0 -> x23, waiting for transfers between devices: none -> 50.9 us  [swap(): return lax.ppermute(array, 'seq', [(at, at ^ step) for at in range(size)])]
    reshape x3 -> x1, local copies, waits for them, and re-layouts: 32 us -> 0.06 us  [square_body(): back.reshape(2, squares, 2, slots_all, own_rows, head_size)]
    pallas_call x0 -> x7, Pallas kernels: none -> 27.4 us  [the longest x2 11.1 us: key_side(): pl.pallas_call(functools.partial(key_kernel, squares, begin, first_slot,...]
  transfers between devices with their start and end apart: 5 -> 23, of which waited for: 5 -> 12; matrix products, arithmetic and copies ran while one was open for 11% -> 0% of each run, Pallas kernels for 0% -> 14%
where the time goes in v2:
time: 122 us; the launch traced here: 121 us
  waiting for transfers between devices  50.9 us (42%)
  Pallas kernels  27.4 us (22%)
  starting transfers between devices  19.9 us (16%)
  blocking collectives  19.1 us (16%)
  local copies, waits for them, and re-layouts  2.87 us (2%)
    ppermute x23, waiting for transfers between devices, swap(): return lax.ppermute(array, 'seq', [(at, at ^ step) for at in range(size)])  50.9 us
    ppermute x23, starting transfers between devices, swap(): return lax.ppermute(array, 'seq', [(at, at ^ step) for at in range(size)])  19.9 us
    all_to_all x1, blocking collectives, square_body(): back = lax.all_to_all(renewed, 'seq', 0, 0, tiled=True)  19.1 us
    pallas_call x2, Pallas kernels, key_side(): pl.pallas_call(functools.partial(key_kernel, squares, begin, first_slot,...  11.1 us
    pallas_call x2, Pallas kernels, renew(): pl.pallas_call(functools.partial(renew_kernel, squares, first_slot), in_s...  7.84 us
    pallas_call x1, Pallas kernels, square_body(): pl.pallas_call(functools.partial(query_kernel, squares), grid=(heads,), i...  6 us
    unnamed x11, local copies, waits for them, and re-layouts  2.71 us
  transfers between devices with their start and end apart: 23, of which 12 were waited for; matrix products, arithmetic and copies ran while one was open for 0% of the time, Pallas kernels for 14%

profile of v2, /device:TPU:0, one launch (start us, length us, event | category | flops | bytes accessed | tf_op | source)
XLA Modules:
  0.0 121.3 jit_solution(8852356647724208243)
XLA Ops:
  0.7 1.1 copy.10
  1.8 0.0 copy-start.1
  1.8 0.0 copy-start.2
  1.8 0.1 dynamic-slice_bitcast_fusion.1
  1.8 0.0 copy-start
  1.9 4.0 %collective-permute-start.5 = (bf16[5,3,32,128]{3,2,1,0:T(8,128)(2,1)S(1)}, bf16[5,3,32,128]{3,2,1,0:T(8,128)(2,1)S(1)}, u32[]{:S(2)}, u32[]{:S(2)}) collective-permute-start(bf16[5,3,32,128]{3,2,1,0:T(8,128)(2,1)S(1)} %get-tuple-element.43), channel_id=1, source_target_pairs={{0,6},{1,7},{2,4},{3,5},{4,2},{5,3},{6,0},{7,1},{8,14},{9,15},{10,... | collective-permute-start | bytes 368648 | tf_op jit(solution)/shard_map/ppermute | solution.py:216
  5.9 0.4 collective-permute-start.4
  6.4 0.2 collective-permute-start.3
  6.5 3.5 %collective-permute-done.5 = bf16[5,3,32,128]{3,2,1,0:T(8,128)(2,1)S(1)} collective-permute-done((bf16[5,3,32,128]{3,2,1,0:T(8,128)(2,1)S(1)}, bf16[5,3,32,128]{3,2,1,0:T(8,128)(2,1)S(1)}, u32[]{:S(2)}, u32[]{:S(2)}) %collective-permute-start.5) | collective-permute-done | bytes 122912 | tf_op jit(solution)/shard_map/ppermute | solution.py:216
  10.1 2.0 %collective-permute-done.4 = bf16[5,3,32,128]{3,2,1,0:T(8,128)(2,1)S(1)} collective-permute-done((bf16[5,3,32,128]{3,2,1,0:T(8,128)(2,1)S(1)}, bf16[5,3,32,128]{3,2,1,0:T(8,128)(2,1)S(1)}, u32[]{:S(2)}, u32[]{:S(2)}) %collective-permute-start.4) | collective-permute-done | bytes 122912 | tf_op jit(solution)/shard_map/ppermute | solution.py:216
  12.0 2.7 %collective-permute-start.9 = (bf16[2,5,3,32,128]{4,3,2,1,0:T(8,128)(2,1)S(1)}, bf16[2,5,3,32,128]{4,3,2,1,0:T(8,128)(2,1)S(1)}, u32[]{:S(2)}, u32[]{:S(2)}) collective-permute-start(bf16[2,5,3,32,128]{4,3,2,1,0:T(8,128)(2,1)S(1)} %pad_maximum_fusion.2.refs_5_.refs_1_), channel_id=1, source_target_pairs={{0,8},{1,9},{2,10},{3,11},{4,12},{5,13},{6,14},{7,15},{8,0},{9,1},... | collective-permute-start | bytes 737288 | tf_op jit(solution)/shard_map/ppermute | solution.py:216
  14.7 0.4 collective-permute-start.8
  15.1 0.7 copy-done.3
  15.8 0.1 copy.9.rate_ref
  16.0 0.1 pad_add_fusion.where_ref.refs_12_
  16.0 1.1 split.1
  17.1 1.1 collective-permute-start
  18.2 1.6 %collective-permute-start.1 = (bf16[3,128,640]{2,1,0:T(8,128)(2,1)S(1)}, bf16[3,128,640]{2,1,0:T(8,128)(2,1)S(1)}, u32[]{:S(2)}, u32[]{:S(2)}) collective-permute-start(bf16[3,128,640]{2,1,0:T(8,128)(2,1)S(1)} %get-tuple-element.23), channel_id=1, source_target_pairs={{0,4},{1,5},{2,6},{3,7},{4,0},{5,1},{6,2},{7,3},{8,12},{9,13},{10,... | collective-permute-start | bytes 1474568 | tf_op jit(solution)/shard_map/ppermute | solution.py:216
  19.8 0.9 collective-permute-start.2
  20.7 11.0 %collective-permute-done.9.refs_9_.refs_5_ = bf16[2,5,3,32,128]{4,3,2,1,0:T(8,128)(2,1)S(1)} collective-permute-done((bf16[2,5,3,32,128]{4,3,2,1,0:T(8,128)(2,1)S(1)}, bf16[2,5,3,32,128]{4,3,2,1,0:T(8,128)(2,1)S(1)}, u32[]{:S(2)}, u32[]{:S(2)}) %collective-permute-start.9) | collective-permute-done | bytes 245792 | tf_op jit(solution)/shard_map/ppermute | solution.py:216
  31.6 0.0 collective-permute-start.7
  31.6 4.1 %collective-permute-done.8.refs_8_.refs_4_ = bf16[2,5,3,32,128]{4,3,2,1,0:T(8,128)(2,1)S(1)} collective-permute-done((bf16[2,5,3,32,128]{4,3,2,1,0:T(8,128)(2,1)S(1)}, bf16[2,5,3,32,128]{4,3,2,1,0:T(8,128)(2,1)S(1)}, u32[]{:S(2)}, u32[]{:S(2)}) %collective-permute-start.8) | collective-permute-done | bytes 245792 | tf_op jit(solution)/shard_map/ppermute | solution.py:216
  35.7 0.0 collective-permute-start.6
  35.7 0.0 collective-permute-done.7.refs_7_.refs_3_
  35.7 0.5 collective-permute-start.11
  36.3 1.0 collective-permute-done.6.refs_6_.refs_2_
  37.3 0.1 collective-permute-start.10
  37.4 0.0 collective-permute-done.refs_1_
  37.4 4.4 %collective-permute-done.1.refs_2_ = bf16[3,128,640]{2,1,0:T(8,128)(2,1)S(1)} collective-permute-done((bf16[3,128,640]{2,1,0:T(8,128)(2,1)S(1)}, bf16[3,128,640]{2,1,0:T(8,128)(2,1)S(1)}, u32[]{:S(2)}, u32[]{:S(2)}) %collective-permute-start.1) | collective-permute-done | bytes 491552 | tf_op jit(solution)/shard_map/ppermute | solution.py:216
  41.8 8.6 %collective-permute-done.2.refs_3_ = bf16[3,128,640]{2,1,0:T(8,128)(2,1)S(1)} collective-permute-done((bf16[3,128,640]{2,1,0:T(8,128)(2,1)S(1)}, bf16[3,128,640]{2,1,0:T(8,128)(2,1)S(1)}, u32[]{:S(2)}, u32[]{:S(2)}) %collective-permute-start.2) | collective-permute-done | bytes 491552 | tf_op jit(solution)/shard_map/ppermute | solution.py:216
  50.4 0.0 collective-permute-done.11.refs_11_.refs_7_
  50.4 0.0 collective-permute-done.10.refs_10_.refs_6_
  50.4 6.1 %key_side.2 = (f32[2,2,512,128]{3,2,1,0:T(8,128)S(1)}, bf16[2,512,128]{2,1,0:T(8,128)(2,1)S(1)}, bf16[512,128]{1,0:T(8,128)(2,1)S(1)}, bf16[512,128]{1,0:T(8,128)(2,1)S(1)}, f32[1,512,128]{2,1,0:T(8,128)S(1)}) custom-call(s32[2]{0:T(128)S(1)} %pad_add_fusion.where_ref.refs_12_, bf16[3,128,640]{2,1,0:T(8,128)(2,1)S(1)} %get-tuple-element.21.refs_0_, ...), custom_call_target="tpu_custom_call" | custom-call | flops 1000000000 | bytes 4000000 | tf_op jit(solution)/shard_map/key_side/pallas_call | solution.py:261
  56.6 0.1 collective-permute-start.16
  56.6 0.5 collective-permute-start.17
  57.1 0.1 collective-permute-start.15
  57.2 5.0 %key_side.3 = (f32[2,2,512,128]{3,2,1,0:T(8,128)S(1)}, bf16[2,512,128]{2,1,0:T(8,128)(2,1)S(1)}, bf16[512,128]{1,0:T(8,128)(2,1)S(1)}, bf16[512,128]{1,0:T(8,128)(2,1)S(1)}, f32[1,512,128]{2,1,0:T(8,128)}) custom-call(s32[2]{0:T(128)S(1)} %pad_add_fusion.where_ref.refs_12_, bf16[3,128,640]{2,1,0:T(8,128)(2,1)S(1)} %get-tuple-element.21.refs_0_, ...), custom_call_target="tpu_custom_call" | custom-call | flops 1000000000 | bytes 4000000 | tf_op jit(solution)/shard_map/key_side/pallas_call | solution.py:261
  62.2 0.4 collective-permute-start.20
  62.6 0.1 collective-permute-start.21
  62.7 6.0 %query_side.1 = (bf16[128,640]{1,0:T(8,128)(2,1)S(1)}, bf16[128,640]{1,0:T(8,128)(2,1)S(1)}, bf16[128,640]{1,0:T(8,128)(2,1)S(1)}, bf16[128,640]{1,0:T(8,128)(2,1)S(1)}) custom-call(bf16[3,128,640]{2,1,0:T(8,128)(2,1)S(1)} %get-tuple-element.21.refs_0_, bf16[3,128,640]{2,1,0:T(8,128)(2,1)S(1)} %collective-permute-done.refs_1_, ...), custom_call_target="tpu_custom_call" | custom-call | flops 1000000000 | bytes 4000000 | tf_op jit(solution)/shard_map/query_side/pallas_call | solution.py:298
  68.7 0.0 collective-permute-done.16
  68.7 0.5 collective-permute-start.19
  69.2 0.0 collective-permute-done.17
  69.2 1.5 %collective-permute-start.12 = (bf16[128,640]{1,0:T(8,128)(2,1)S(1)}, bf16[128,640]{1,0:T(8,128)(2,1)S(1)}, u32[]{:S(2)}, u32[]{:S(2)}) collective-permute-start(bf16[128,640]{1,0:T(8,128)(2,1)S(1)} %get-tuple-element.26), channel_id=1, source_target_pairs={{0,2},{1,3},{2,0},{3,1},{4,6},{5,7},{6,4},{7,5},{8,10},{9,11},{10,... | collective-permute-start | bytes 491528 | tf_op jit(solution)/shard_map/ppermute | solution.py:216
  70.7 0.1 fusion.1
  70.7 0.0 collective-permute-done.20
  70.7 0.1 collective-permute-start.13
  70.8 3.6 %collective-permute-start.18 = (bf16[2,512,128]{2,1,0:T(8,128)(2,1)S(1)}, bf16[2,512,128]{2,1,0:T(8,128)(2,1)S(1)}, u32[]{:S(2)}, u32[]{:S(2)}) collective-permute-start(bf16[2,512,128]{2,1,0:T(8,128)(2,1)S(1)} %fusion.1), channel_id=1, source_target_pairs={{0,8},{1,9},{2,10},{3,11},{4,12},{5,13},{6,14},{7,15},{8,0},{9,1},... | collective-permute-start | bytes 786440 | tf_op jit(solution)/shard_map/ppermute | solution.py:216
  74.5 0.1 fusion
  74.5 0.8 collective-permute-done.12.refs_1_
  75.4 1.2 collective-permute-start.22
  76.6 3.5 %collective-permute-done.13.refs_2_ = bf16[128,640]{1,0:T(8,128)(2,1)S(1)} collective-permute-done((bf16[128,640]{1,0:T(8,128)(2,1)S(1)}, bf16[128,640]{1,0:T(8,128)(2,1)S(1)}, u32[]{:S(2)}, u32[]{:S(2)}) %collective-permute-start.13) | collective-permute-done | bytes 163872 | tf_op jit(solution)/shard_map/ppermute | solution.py:216
  80.1 0.0 collective-permute-start.14
  80.1 9.2 %collective-permute-done.14.refs_3_ = bf16[128,640]{1,0:T(8,128)(2,1)S(1)} collective-permute-done((bf16[128,640]{1,0:T(8,128)(2,1)S(1)}, bf16[128,640]{1,0:T(8,128)(2,1)S(1)}, u32[]{:S(2)}, u32[]{:S(2)}) %collective-permute-start.14) | collective-permute-done | bytes 163872 | tf_op jit(solution)/shard_map/ppermute | solution.py:216
  89.3 1.4 %join.1 = (bf16[128,2560]{1,0:T(8,128)(2,1)}, f32[8,128]{1,0:T(8,128)S(1)}) custom-call(s32[2]{0:T(128)S(1)} %pad_add_fusion.where_ref.refs_12_, bf16[128,640]{1,0:T(8,128)(2,1)S(1)} %get-tuple-element.25.refs_0_, bf16[128,640]{1,0:T(8,128)(2,1)S(1)} %collective-permute-done.12.refs_1_, bf16[128,640]{1,0:T(8,128)(2,1)S(1)} %collective-permute-done.13.refs_2_, ...), custom_call_target="tpu_custom_call" | custom-call | flops 10000000 | bytes 4000000 | tf_op jit(solution)/shard_map/join/pallas_call | solution.py:309
  90.8 0.0 collective-permute-done.15.near_ref
  90.8 2.1 %collective-permute-done.18.far_ref = bf16[2,512,128]{2,1,0:T(8,128)(2,1)S(1)} collective-permute-done((bf16[2,512,128]{2,1,0:T(8,128)(2,1)S(1)}, bf16[2,512,128]{2,1,0:T(8,128)(2,1)S(1)}, u32[]{:S(2)}, u32[]{:S(2)}) %collective-permute-start.18) | collective-permute-done | bytes 262176 | tf_op jit(solution)/shard_map/ppermute | solution.py:216
  92.9 3.9 %renew.2 = bf16[16,2,32,128]{3,2,1,0:T(8,128)(2,1)S(1)} custom-call(s32[2]{0:T(128)S(1)} %pad_add_fusion.where_ref.refs_12_, f32[2,2,512,128]{3,2,1,0:T(8,128)S(1)} %get-tuple-element.30.mine_ref, bf16[2,512,128]{2,1,0:T(8,128)(2,1)S(1)} %collective-permute-done.15.near_ref, bf16[2,512,128]{2,1,0:T(8,128)(2,1)S(1)} %collective-permute-done.18.far_ref, ...), custom_call_target="tpu_custom_call" | custom-call | flops 1000000000 | bytes 4000000 | tf_op jit(solution)/shard_map/renew/pallas_call | solution.py:321
  96.8 0.0 collective-permute-done.19.near_ref
  96.8 0.5 collective-permute-done.22.far_ref
  97.4 3.9 %renew.3 = bf16[16,2,32,128]{3,2,1,0:T(8,128)(2,1)S(1)} custom-call(s32[2]{0:T(128)S(1)} %pad_add_fusion.where_ref.refs_12_, f32[2,2,512,128]{3,2,1,0:T(8,128)S(1)} %get-tuple-element.35.mine_ref, bf16[2,512,128]{2,1,0:T(8,128)(2,1)S(1)} %collective-permute-done.19.near_ref, bf16[2,512,128]{2,1,0:T(8,128)(2,1)S(1)} %collective-permute-done.22.far_ref, ...), custom_call_target="tpu_custom_call" | custom-call | flops 1000000000 | bytes 4000000 | tf_op jit(solution)/shard_map/renew/pallas_call | solution.py:321
  101.3 19.1 %all_to_all.5 = bf16[16,4,32,128]{3,2,1,0:T(8,128)(2,1)S(1)} all-to-all(bf16[16,4,32,128]{3,2,1,0:T(8,128)(2,1)S(1)} %pad_maximum_fusion), channel_id=1, replica_groups=mesh['groups'=2,'seq'=16] {'seq'}, dimensions={0} | all-to-all | bytes 1048576 | tf_op jit(solution)/shard_map/all_to_all | solution.py:335
  120.4 0.1 copy.11
  120.5 0.8 copy.12
  (10 shorter events, 0.2 us)
Async XLA Ops:
  1.8 14.3 %copy-start.1 = (bf16[128,2560]{1,0:T(8,128)(2,1)S(1)}, bf16[128,2560]{1,0:T(8,128)(2,1)}, u32[]{:S(2)}) copy-start(bf16[128,2560]{1,0:T(8,128)(2,1)} %k_ref.1) | copy-start | bytes 1966084
  1.8 14.3 %copy-start.2 = (bf16[128,2560]{1,0:T(8,128)(2,1)S(1)}, bf16[128,2560]{1,0:T(8,128)(2,1)}, u32[]{:S(2)}) copy-start(bf16[128,2560]{1,0:T(8,128)(2,1)} %v_ref.1) | copy-start | bytes 1966084
  1.8 14.2 %copy-start = (bf16[128,2560]{1,0:T(8,128)(2,1)S(1)}, bf16[128,2560]{1,0:T(8,128)(2,1)}, u32[]{:S(2)}) copy-start(bf16[128,2560]{1,0:T(8,128)(2,1)} %q_ref.1) | copy-start | bytes 1966084
  1.9 8.2 %collective-permute-start.5 = (bf16[5,3,32,128]{3,2,1,0:T(8,128)(2,1)S(1)}, bf16[5,3,32,128]{3,2,1,0:T(8,128)(2,1)S(1)}, u32[]{:S(2)}, u32[]{:S(2)}) collective-permute-start(bf16[5,3,32,128]{3,2,1,0:T(8,128)(2,1)S(1)} %get-tuple-element.43), channel_id=1, source_target_pairs={{0,6},{1,7},{2,4},{3,5},{4,2},{5,3},{6,0},{7,1},{8,14},{9,15},{10,... | collective-permute-start | bytes 368648 | tf_op jit(solution)/shard_map/ppermute | solution.py:216
  5.9 6.1 %collective-permute-start.4 = (bf16[5,3,32,128]{3,2,1,0:T(8,128)(2,1)S(1)}, bf16[5,3,32,128]{3,2,1,0:T(8,128)(2,1)S(1)}, u32[]{:S(2)}, u32[]{:S(2)}) collective-permute-start(bf16[5,3,32,128]{3,2,1,0:T(8,128)(2,1)S(1)} %get-tuple-element.42), channel_id=1, source_target_pairs={{0,4},{1,5},{2,6},{3,7},{4,0},{5,1},{6,2},{7,3},{8,12},{9,13},{10,... | collective-permute-start | bytes 368648 | tf_op jit(solution)/shard_map/ppermute | solution.py:216
  6.4 8.4 %collective-permute-start.3 = (bf16[5,3,32,128]{3,2,1,0:T(8,128)(2,1)S(1)}, bf16[5,3,32,128]{3,2,1,0:T(8,128)(2,1)S(1)}, u32[]{:S(2)}, u32[]{:S(2)}) collective-permute-start(bf16[5,3,32,128]{3,2,1,0:T(8,128)(2,1)S(1)} %get-tuple-element.44), channel_id=1, source_target_pairs={{0,2},{1,3},{2,0},{3,1},{4,6},{5,7},{6,4},{7,5},{8,10},{9,11},{10,... | collective-permute-start | bytes 368648 | tf_op jit(solution)/shard_map/ppermute | solution.py:216
  12.0 19.6 %collective-permute-start.9 = (bf16[2,5,3,32,128]{4,3,2,1,0:T(8,128)(2,1)S(1)}, bf16[2,5,3,32,128]{4,3,2,1,0:T(8,128)(2,1)S(1)}, u32[]{:S(2)}, u32[]{:S(2)}) collective-permute-start(bf16[2,5,3,32,128]{4,3,2,1,0:T(8,128)(2,1)S(1)} %pad_maximum_fusion.2.refs_5_.refs_1_), channel_id=1, source_target_pairs={{0,8},{1,9},{2,10},{3,11},{4,12},{5,13},{6,14},{7,15},{8,0},{9,1},... | collective-permute-start | bytes 737288 | tf_op jit(solution)/shard_map/ppermute | solution.py:216
  14.7 21.0 %collective-permute-start.8 = (bf16[2,5,3,32,128]{4,3,2,1,0:T(8,128)(2,1)S(1)}, bf16[2,5,3,32,128]{4,3,2,1,0:T(8,128)(2,1)S(1)}, u32[]{:S(2)}, u32[]{:S(2)}) collective-permute-start(bf16[2,5,3,32,128]{4,3,2,1,0:T(8,128)(2,1)S(1)} %pad_maximum_fusion.1.refs_4_.refs_0_), channel_id=1, source_target_pairs={{0,8},{1,9},{2,10},{3,11},{4,12},{5,13},{6,14},{7,15},{8,0},{9,1},... | collective-permute-start | bytes 737288 | tf_op jit(solution)/shard_map/ppermute | solution.py:216
  15.1 0.7 copy-start.3
  17.1 20.3 %collective-permute-start = (bf16[3,128,640]{2,1,0:T(8,128)(2,1)S(1)}, bf16[3,128,640]{2,1,0:T(8,128)(2,1)S(1)}, u32[]{:S(2)}, u32[]{:S(2)}) collective-permute-start(bf16[3,128,640]{2,1,0:T(8,128)(2,1)S(1)} %get-tuple-element.22), channel_id=1, source_target_pairs={{0,2},{1,3},{2,0},{3,1},{4,6},{5,7},{6,4},{7,5},{8,10},{9,11},{10,... | collective-permute-start | bytes 1474568 | tf_op jit(solution)/shard_map/ppermute | solution.py:216
  18.2 23.6 %collective-permute-start.1 = (bf16[3,128,640]{2,1,0:T(8,128)(2,1)S(1)}, bf16[3,128,640]{2,1,0:T(8,128)(2,1)S(1)}, u32[]{:S(2)}, u32[]{:S(2)}) collective-permute-start(bf16[3,128,640]{2,1,0:T(8,128)(2,1)S(1)} %get-tuple-element.23), channel_id=1, source_target_pairs={{0,4},{1,5},{2,6},{3,7},{4,0},{5,1},{6,2},{7,3},{8,12},{9,13},{10,... | collective-permute-start | bytes 1474568 | tf_op jit(solution)/shard_map/ppermute | solution.py:216
  19.8 30.6 %collective-permute-start.2 = (bf16[3,128,640]{2,1,0:T(8,128)(2,1)S(1)}, bf16[3,128,640]{2,1,0:T(8,128)(2,1)S(1)}, u32[]{:S(2)}, u32[]{:S(2)}) collective-permute-start(bf16[3,128,640]{2,1,0:T(8,128)(2,1)S(1)} %get-tuple-element.24), channel_id=1, source_target_pairs={{0,6},{1,7},{2,4},{3,5},{4,2},{5,3},{6,0},{7,1},{8,14},{9,15},{10,... | collective-permute-start | bytes 1474568 | tf_op jit(solution)/shard_map/ppermute | solution.py:216
  31.6 4.1 %collective-permute-start.7 = (bf16[2,5,3,32,128]{4,3,2,1,0:T(8,128)(2,1)S(1)}, bf16[2,5,3,32,128]{4,3,2,1,0:T(8,128)(2,1)S(1)}, u32[]{:S(2)}, u32[]{:S(2)}) collective-permute-start(bf16[2,5,3,32,128]{4,3,2,1,0:T(8,128)(2,1)S(1)} %pad_maximum_fusion.2.refs_5_.refs_1_), channel_id=1, source_target_pairs={{0,1},{1,0},{2,3},{3,2},{4,5},{5,4},{6,7},{7,6},{8,9},{9,8},{10,11... | collective-permute-start | bytes 737288 | tf_op jit(solution)/shard_map/ppermute | solution.py:216
  35.7 1.5 %collective-permute-start.6 = (bf16[2,5,3,32,128]{4,3,2,1,0:T(8,128)(2,1)S(1)}, bf16[2,5,3,32,128]{4,3,2,1,0:T(8,128)(2,1)S(1)}, u32[]{:S(2)}, u32[]{:S(2)}) collective-permute-start(bf16[2,5,3,32,128]{4,3,2,1,0:T(8,128)(2,1)S(1)} %pad_maximum_fusion.1.refs_4_.refs_0_), channel_id=1, source_target_pairs={{0,1},{1,0},{2,3},{3,2},{4,5},{5,4},{6,7},{7,6},{8,9},{9,8},{10,11... | collective-permute-start | bytes 737288 | tf_op jit(solution)/shard_map/ppermute | solution.py:216
  35.7 14.7 %collective-permute-start.11 = (bf16[2,5,3,32,128]{4,3,2,1,0:T(8,128)(2,1)S(1)}, bf16[2,5,3,32,128]{4,3,2,1,0:T(8,128)(2,1)S(1)}, u32[]{:S(2)}, u32[]{:S(2)}) collective-permute-start(bf16[2,5,3,32,128]{4,3,2,1,0:T(8,128)(2,1)S(1)} %collective-permute-done.9.refs_9_.refs_5_), channel_id=1, source_target_pairs={{0,1},{1,0},{2,3},{3,2},{4,5},{5,4},{6,7},{7,6},{8,9},{9,8},{10,11... | collective-permute-start | bytes 737288 | tf_op jit(solution)/shard_map/ppermute | solution.py:216
  37.3 13.2 %collective-permute-start.10 = (bf16[2,5,3,32,128]{4,3,2,1,0:T(8,128)(2,1)S(1)}, bf16[2,5,3,32,128]{4,3,2,1,0:T(8,128)(2,1)S(1)}, u32[]{:S(2)}, u32[]{:S(2)}) collective-permute-start(bf16[2,5,3,32,128]{4,3,2,1,0:T(8,128)(2,1)S(1)} %collective-permute-done.8.refs_8_.refs_4_), channel_id=1, source_target_pairs={{0,1},{1,0},{2,3},{3,2},{4,5},{5,4},{6,7},{7,6},{8,9},{9,8},{10,11... | collective-permute-start | bytes 737288 | tf_op jit(solution)/shard_map/ppermute | solution.py:216
  56.6 12.1 %collective-permute-start.16 = (bf16[512,128]{1,0:T(8,128)(2,1)S(1)}, bf16[512,128]{1,0:T(8,128)(2,1)S(1)}, u32[]{:S(2)}, u32[]{:S(2)}) collective-permute-start(bf16[512,128]{1,0:T(8,128)(2,1)S(1)} %get-tuple-element.32), channel_id=1, source_target_pairs={{0,1},{1,0},{2,3},{3,2},{4,5},{5,4},{6,7},{7,6},{8,9},{9,8},{10,11... | collective-permute-start | bytes 393224 | tf_op jit(solution)/shard_map/ppermute | solution.py:216
  56.6 12.6 %collective-permute-start.17 = (bf16[512,128]{1,0:T(8,128)(2,1)S(1)}, bf16[512,128]{1,0:T(8,128)(2,1)S(1)}, u32[]{:S(2)}, u32[]{:S(2)}) collective-permute-start(bf16[512,128]{1,0:T(8,128)(2,1)S(1)} %get-tuple-element.33), channel_id=1, source_target_pairs={{0,1},{1,0},{2,3},{3,2},{4,5},{5,4},{6,7},{7,6},{8,9},{9,8},{10,11... | collective-permute-start | bytes 393224 | tf_op jit(solution)/shard_map/ppermute | solution.py:216
  57.1 33.6 %collective-permute-start.15 = (bf16[2,512,128]{2,1,0:T(8,128)(2,1)S(1)}, bf16[2,512,128]{2,1,0:T(8,128)(2,1)S(1)}, u32[]{:S(2)}, u32[]{:S(2)}) collective-permute-start(bf16[2,512,128]{2,1,0:T(8,128)(2,1)S(1)} %get-tuple-element.31), channel_id=1, source_target_pairs={{0,1},{1,0},{2,3},{3,2},{4,5},{5,4},{6,7},{7,6},{8,9},{9,8},{10,11... | collective-permute-start | bytes 786440 | tf_op jit(solution)/shard_map/ppermute | solution.py:216
  62.2 8.6 %collective-permute-start.20 = (bf16[512,128]{1,0:T(8,128)(2,1)S(1)}, bf16[512,128]{1,0:T(8,128)(2,1)S(1)}, u32[]{:S(2)}, u32[]{:S(2)}) collective-permute-start(bf16[512,128]{1,0:T(8,128)(2,1)S(1)} %get-tuple-element.37), channel_id=1, source_target_pairs={{0,1},{1,0},{2,3},{3,2},{4,5},{5,4},{6,7},{7,6},{8,9},{9,8},{10,11... | collective-permute-start | bytes 393224 | tf_op jit(solution)/shard_map/ppermute | solution.py:216
  62.6 8.2 %collective-permute-start.21 = (bf16[512,128]{1,0:T(8,128)(2,1)S(1)}, bf16[512,128]{1,0:T(8,128)(2,1)S(1)}, u32[]{:S(2)}, u32[]{:S(2)}) collective-permute-start(bf16[512,128]{1,0:T(8,128)(2,1)S(1)} %get-tuple-element.38), channel_id=1, source_target_pairs={{0,1},{1,0},{2,3},{3,2},{4,5},{5,4},{6,7},{7,6},{8,9},{9,8},{10,11... | collective-permute-start | bytes 393224 | tf_op jit(solution)/shard_map/ppermute | solution.py:216
  68.7 28.1 %collective-permute-start.19 = (bf16[2,512,128]{2,1,0:T(8,128)(2,1)S(1)}, bf16[2,512,128]{2,1,0:T(8,128)(2,1)S(1)}, u32[]{:S(2)}, u32[]{:S(2)}) collective-permute-start(bf16[2,512,128]{2,1,0:T(8,128)(2,1)S(1)} %get-tuple-element.36), channel_id=1, source_target_pairs={{0,1},{1,0},{2,3},{3,2},{4,5},{5,4},{6,7},{7,6},{8,9},{9,8},{10,11... | collective-permute-start | bytes 786440 | tf_op jit(solution)/shard_map/ppermute | solution.py:216
  69.2 6.2 %collective-permute-start.12 = (bf16[128,640]{1,0:T(8,128)(2,1)S(1)}, bf16[128,640]{1,0:T(8,128)(2,1)S(1)}, u32[]{:S(2)}, u32[]{:S(2)}) collective-permute-start(bf16[128,640]{1,0:T(8,128)(2,1)S(1)} %get-tuple-element.26), channel_id=1, source_target_pairs={{0,2},{1,3},{2,0},{3,1},{4,6},{5,7},{6,4},{7,5},{8,10},{9,11},{10,... | collective-permute-start | bytes 491528 | tf_op jit(solution)/shard_map/ppermute | solution.py:216
  70.7 9.3 %collective-permute-start.13 = (bf16[128,640]{1,0:T(8,128)(2,1)S(1)}, bf16[128,640]{1,0:T(8,128)(2,1)S(1)}, u32[]{:S(2)}, u32[]{:S(2)}) collective-permute-start(bf16[128,640]{1,0:T(8,128)(2,1)S(1)} %get-tuple-element.27), channel_id=1, source_target_pairs={{0,4},{1,5},{2,6},{3,7},{4,0},{5,1},{6,2},{7,3},{8,12},{9,13},{10,... | collective-permute-start | bytes 491528 | tf_op jit(solution)/shard_map/ppermute | solution.py:216
  70.8 22.0 %collective-permute-start.18 = (bf16[2,512,128]{2,1,0:T(8,128)(2,1)S(1)}, bf16[2,512,128]{2,1,0:T(8,128)(2,1)S(1)}, u32[]{:S(2)}, u32[]{:S(2)}) collective-permute-start(bf16[2,512,128]{2,1,0:T(8,128)(2,1)S(1)} %fusion.1), channel_id=1, source_target_pairs={{0,8},{1,9},{2,10},{3,11},{4,12},{5,13},{6,14},{7,15},{8,0},{9,1},... | collective-permute-start | bytes 786440 | tf_op jit(solution)/shard_map/ppermute | solution.py:216
  75.4 22.0 %collective-permute-start.22 = (bf16[2,512,128]{2,1,0:T(8,128)(2,1)S(1)}, bf16[2,512,128]{2,1,0:T(8,128)(2,1)S(1)}, u32[]{:S(2)}, u32[]{:S(2)}) collective-permute-start(bf16[2,512,128]{2,1,0:T(8,128)(2,1)S(1)} %fusion), channel_id=1, source_target_pairs={{0,8},{1,9},{2,10},{3,11},{4,12},{5,13},{6,14},{7,15},{8,0},{9,1},... | collective-permute-start | bytes 786440 | tf_op jit(solution)/shard_map/ppermute | solution.py:216
  80.1 9.2 %collective-permute-start.14 = (bf16[128,640]{1,0:T(8,128)(2,1)S(1)}, bf16[128,640]{1,0:T(8,128)(2,1)S(1)}, u32[]{:S(2)}, u32[]{:S(2)}) collective-permute-start(bf16[128,640]{1,0:T(8,128)(2,1)S(1)} %get-tuple-element.28), channel_id=1, source_target_pairs={{0,6},{1,7},{2,4},{3,5},{4,2},{5,3},{6,0},{7,1},{8,14},{9,15},{10,... | collective-permute-start | bytes 491528 | tf_op jit(solution)/shard_map/ppermute | solution.py:216

commit v3 on v2

--- a/solution.py
+++ b/solution.py
@@ -63,11 +63,9 @@
     )
 
 
-def key_kernel(squares, begin, first_slot, slots, last, where_ref, *refs):
-    pairs, w_refs, carried = refs[:squares], refs[squares : squares + 8], refs[squares + 8]
-    keep_ref, near_ref = refs[squares + 9 : squares + 11]
-    far_refs = refs[squares + 11 : squares + 11 + slots]
-    carry_ref, terms = refs[-2:]
+def key_kernel(squares, heads, where_ref, *refs):
+    pairs, w_refs = refs[:squares], refs[squares : squares + 8]
+    keep_ref, near_ref, far_ref, terms = refs[squares + 8 :]
     spot, place = where_ref[0], where_ref[1]
     _, hid, head_size = terms.shape
     rows = hid // (PLACES * squares)
@@ -76,61 +74,55 @@
 
     def put(number, value):
         rel = (number % PLACES) ^ place
-        slot = number // PLACES - first_slot
-
-        @pl.when((rel % 2 == 0) & (slot < slots))
+        slot = number // PLACES
+
+        @pl.when(rel % 2 == 0)
         def _():
             keep_ref[rel // 2, slot] = value
 
-        @pl.when((rel == 1) & (slot < slots))
+        @pl.when(rel == 1)
         def _():
             near_ref[slot] = value.astype(near_ref.dtype)
 
-        for one in range(slots):
-
-            @pl.when((rel == 3) & (slot == one))
-            def _():
-                far_refs[one][...] = value.astype(far_refs[one].dtype)
-
-        if not last:
-
-            @pl.when(slot >= slots)
-            def _():
-                carry_ref[number - PLACES * (first_slot + slots)] = value
+        @pl.when(rel == 3)
+        def _():
+            far_ref[slot] = value.astype(far_ref.dtype)
 
     @pl.when(step == 0)
     def _():
-        if first_slot:
-            for number in range(PLACES * first_slot, 3 * begin):
-                put(number, carried[number - PLACES * first_slot])
-        if last:
-            for number in range(3 * last, PLACES * (first_slot + slots)):
-                put(number, jnp.zeros((hid, head_size), jnp.float32))
+        for number in range(3 * heads, PLACES * keep_ref.shape[1]):
+            put(number, jnp.zeros((hid, head_size), jnp.float32))
 
     keys = jnp.concatenate([pair[0] for pair in pairs], axis=0)
     scaled = jnp.concatenate([pair[1] for pair in pairs], axis=0)
+    both_maps = jnp.concatenate(
+        [weight_rows(w_refs, rel, matrix) for matrix in range(2) for rel in range(PLACES)], axis=0
+    )
+    second = jnp.concatenate([weight_rows(w_refs, rel, 2) for rel in range(PLACES)], axis=0)
+    raw = dot(both_maps, keys, NT)
+    raw_third = raw[hid:]
+    back = dot(second, scaled, NT)
+    half_first = raw[:hid] * (0.5 * scale_in)
+    tanh = jnp.tanh(half_first)
+    act = half_first + half_first * tanh
+    hidden = (act * raw_third).astype(jnp.bfloat16)
+    grad_third = (back * act).astype(jnp.bfloat16)
+    twice_slope = (1.0 + tanh) + act * (1.0 - tanh)
+    grad_first = (back * raw_third * twice_slope).astype(jnp.bfloat16)
+    firsts = dot(jnp.concatenate([grad_first, grad_third], axis=0), keys, NN)
+    values = (
+        firsts[:hid] * (0.5 * scale_in * scale_in),
+        firsts[hid:] * scale_in,
+        dot(hidden, scaled, NN) * scale_in,
+    )
     for rel in range(PLACES):
-        raw_first = dot(weight_rows(w_refs, rel, 0), keys, NT)
-        raw_third = dot(weight_rows(w_refs, rel, 1), keys, NT)
-        back = dot(weight_rows(w_refs, rel, 2), scaled, NT)
-        first = raw_first * scale_in
-        sig = 0.5 * jnp.tanh(0.5 * first) + 0.5
-        act = first * sig
-        hidden = (act * raw_third).astype(jnp.bfloat16)
-        grad_third = (back * act).astype(jnp.bfloat16)
-        slope = sig + act * (1.0 - sig)
-        grad_first = (back * raw_third * slope).astype(jnp.bfloat16)
-        values = (
-            dot(grad_first, keys, NN) * (scale_in * scale_in),
-            dot(grad_third, keys, NN) * scale_in,
-            dot(hidden, scaled, NN) * scale_in,
-        )
         for apart in range(squares):
+            at = (rel * squares + apart) * rows
             to = pl.multiple_of(((place ^ rel) * squares + (spot ^ apart)) * rows, rows)
             for matrix in range(3):
-                terms[matrix, pl.ds(to, rows), :] = values[matrix][apart * rows : (apart + 1) * rows]
+                terms[matrix, pl.ds(to, rows), :] = values[matrix][at : at + rows]
     for matrix in range(3):
-        put(3 * (begin + step) + matrix, terms[matrix])
+        put(3 * step + matrix, terms[matrix])
 
 
 def query_kernel(squares, *refs):
@@ -141,22 +133,31 @@
         jnp.concatenate([weight_rows(w_refs, rel, matrix) for rel in range(PLACES)], axis=0)
         for matrix in range(3)
     )
-    for q_ref, out_ref in zip(ins, outs):
-        queries = q_ref[0]
-        first = dot(queries, first_map, NT) * scale_in
-        third = dot(queries, third_map, NT) * scale_in
-        sig = 0.5 * jnp.tanh(0.5 * first) + 0.5
-        hidden = (first * sig * third).astype(jnp.bfloat16)
-        out_ref[...] = (dot(hidden, second, NN) * scale_out).astype(out_ref.dtype)
-
-
-def renew_kernel(squares, first_slot, where_ref, mine_ref, near_ref, far_ref, *refs):
+    queries = jnp.concatenate([q_ref[0] for q_ref in ins], axis=0)
+    half_first = dot(queries, first_map, NT) * (0.5 * scale_in)
+    third = dot(queries, third_map, NT)
+    hidden = ((half_first + half_first * jnp.tanh(half_first)) * third).astype(jnp.bfloat16)
+    out = (dot(hidden, second, NN) * (scale_in * scale_out)).astype(jnp.bfloat16)
+    rows = outs[0].shape[0]
+    for rel, out_ref in enumerate(outs):
+        out_ref[...] = out[rel * rows : (rel + 1) * rows]
+
+
+def halves(array):
+    high = array.astype(jnp.bfloat16)
+    return high, (array - high.astype(jnp.float32)).astype(jnp.bfloat16)
+
+
+def dot_halves(a, b, dims):
+    return dot(a[0], b[0], dims) + (dot(a[0], b[1], dims) + dot(a[1], b[0], dims))
+
+
+def renew_kernel(squares, where_ref, mine_ref, near_ref, far_ref, *refs):
     w_refs, (out_ref, updates) = refs[:8], refs[-2:]
     spot, place = where_ref[0], where_ref[1]
     slots, hid, head_size = far_ref.shape
     heads = w_refs[0].shape[1]
     rows = out_ref.shape[2]
-    exact = lax.Precision.HIGHEST
     eye = (
         lax.broadcasted_iota(jnp.int32, (head_size, head_size), 0)
         == lax.broadcasted_iota(jnp.int32, (head_size, head_size), 1)
@@ -167,19 +168,36 @@
         + far_ref[slot].astype(jnp.float32)
         for slot in range(slots)
     ]
-    grams = [dot(grad, grad, TN, exact) for grad in grads]
-    factors = [eye * (1.0 / (jnp.sqrt(jnp.sum(gram * eye)) + 1e-07)) for gram in grams]
-    for _ in range(NS_STEPS):
-        inner = [dot(gram, factor, NN, exact) for gram, factor in zip(grams, factors)]
-        square = [dot(factor, term, NN, exact) for factor, term in zip(factors, inner)]
-        mixed = [coef_b * term + coef_c * dot(term, term, NN, exact) for term in square]
+    grads = [halves(grad) for grad in grads]
+    grams = []
+    for high, low in grads:
+        cross = dot(high, low, TN)
+        grams.append(dot(high, high, TN) + (cross + cross.T))
+    scales = [1.0 / (jnp.sqrt(jnp.sum(gram * eye)) + 1e-07) for gram in grams]
+    factors = []
+    for gram, scale in zip(grams, scales):
+        square = (scale * scale) * gram
+        parts = halves(square)
+        factors.append(
+            scale * (coef_a * eye + coef_b * square + coef_c * dot_halves(parts, parts, NN))
+        )
+    grams = [halves(gram) for gram in grams]
+    for _ in range(NS_STEPS - 1):
+        parts = [halves(factor) for factor in factors]
+        inner = [dot_halves(gram, part, NN) for gram, part in zip(grams, parts)]
+        squares_of = [dot_halves(part, halves(term), NN) for part, term in zip(parts, inner)]
+        mixed = []
+        for square in squares_of:
+            term = halves(square)
+            mixed.append(coef_b * square + coef_c * dot_halves(term, term, NN))
         factors = [
-            coef_a * factor + dot(term, factor, NN, exact) for term, factor in zip(mixed, factors)
+            coef_a * factor + dot_halves(halves(term), part, NN)
+            for term, factor, part in zip(mixed, factors, parts)
         ]
     for slot in range(slots):
-        updates[slot] = math.sqrt(HID) * dot(grads[slot], factors[slot], NT, exact)
+        updates[slot] = math.sqrt(HID) * dot_halves(grads[slot], halves(factors[slot]), NT)
     for slot in range(slots):
-        number = jnp.minimum(PLACES * (first_slot + slot) + place, 3 * heads - 1)
+        number = jnp.minimum(PLACES * slot + place, 3 * heads - 1)
         head, matrix = number // 3, number % 3
         for rel in range(PLACES):
             owner = place ^ rel
@@ -248,58 +266,38 @@
     weights = [own, [swap(w, 1) for w in own], other, [swap(w, 1) for w in other]]
     weights = [w for pair in weights for w in pair]
 
-    def weight_spec(begin=0):
-        return pl.BlockSpec((cut, 1, 3, own_rows, head_size), lambda h: (0, h + begin, 0, 0, 0))
-
-    def key_side(begin, end, first_slot, slots, carry_count, carried):
-        keep_shape = (2, slots, hid, head_size)
-        carry_shape = (max(carry_count, 1), hid, head_size)
-
-        def whole(shape):
-            return pl.BlockSpec(shape, lambda h: (0,) * len(shape))
-
-        return pl.pallas_call(
-            functools.partial(
-                key_kernel, squares, begin, first_slot, slots, heads if end == heads else 0
-            ),
-            grid=(end - begin,),
-            in_specs=[
-                smem,
-                *[pl.BlockSpec((2, row_count, head_size), lambda h: (0, 0, h + begin))] * squares,
-                *[weight_spec(begin)] * 8,
-                whole(carried.shape) if begin else smem,
-            ],
-            out_specs=[whole(keep_shape), whole(keep_shape[1:])]
-            + [whole(keep_shape[2:])] * slots
-            + [whole(carry_shape)],
-            out_shape=[jax.ShapeDtypeStruct(keep_shape, jnp.float32), bf16(*keep_shape[1:])]
-            + [bf16(*keep_shape[2:])] * slots
-            + [jax.ShapeDtypeStruct(carry_shape, jnp.float32)],
-            scratch_shapes=[VMEM((3, hid, head_size), jnp.float32)],
-            compiler_params=params,
-            cost_estimate=cost(1000),
-            name="key_side",
-        )(where, *moved, *weights, carried)
-
-    def add_up(keep, near, *far):
-        got = jnp.stack([swap(one, 1) for one in far])
-        other = (keep[1] + got.astype(jnp.float32)).astype(jnp.bfloat16)
-        return keep, swap(near, 1), swap(other, half)
-
-    middle = -(-heads // 2)
-    slots_all = -(-3 * heads // PLACES)
-    slots_one = 3 * middle // PLACES
-    *sums_one, carry = key_side(0, middle, 0, slots_one, 3 * middle - PLACES * slots_one, where)
-    sums_one = add_up(*sums_one)
-    *sums_two, _ = key_side(middle, heads, slots_one, slots_all - slots_one, 0, carry)
-    sums_two = add_up(*sums_two)
+    weight_spec = pl.BlockSpec((cut, 1, 3, own_rows, head_size), lambda h: (0, h, 0, 0, 0))
+
+    slots = -(-3 * heads // PLACES)
+    sums_shape = (slots, hid, head_size)
+    keep, near, far = pl.pallas_call(
+        functools.partial(key_kernel, squares, heads),
+        grid=(heads,),
+        in_specs=[smem]
+        + [pl.BlockSpec((2, row_count, head_size), lambda h: (0, 0, h))] * squares
+        + [weight_spec] * 8,
+        out_specs=[pl.BlockSpec((2, *sums_shape), lambda h: (0, 0, 0, 0))]
+        + [pl.BlockSpec(sums_shape, lambda h: (0, 0, 0))] * 2,
+        out_shape=[
+            jax.ShapeDtypeStruct((2, *sums_shape), jnp.float32),
+            bf16(*sums_shape),
+            bf16(*sums_shape),
+        ],
+        scratch_shapes=[VMEM((3, hid, head_size), jnp.float32)],
+        compiler_params=params,
+        cost_estimate=cost(2000),
+        name="key_side",
+    )(where, *moved, *weights)
+
+    near = swap(near, 1)
+    far = swap((keep[1] + swap(far, 1).astype(jnp.float32)).astype(jnp.bfloat16), half)
 
     columns = pl.BlockSpec((row_count, head_size), lambda h: (0, h))
     parts = pl.pallas_call(
         functools.partial(query_kernel, squares),
         grid=(heads,),
         in_specs=[pl.BlockSpec((1, row_count, head_size), lambda h: (2, 0, h))] * squares
-        + [weight_spec()] * 8,
+        + [weight_spec] * 8,
         out_specs=[columns] * squares,
         out_shape=[bf16(row_count, width)] * squares,
         compiler_params=params,
@@ -316,25 +314,19 @@
         name="join",
     )(where, *across(parts))
 
-    def renew(keep, near, far, first_slot, before):
-        slots = far.shape[0]
-        return pl.pallas_call(
-            functools.partial(renew_kernel, squares, first_slot),
-            in_specs=[smem] + [vmem] * (11 + len(before)),
-            out_specs=vmem,
-            out_shape=bf16(size, slots, own_rows, head_size),
-            scratch_shapes=[VMEM((slots, hid, head_size), jnp.float32)],
-            compiler_params=params,
-            cost_estimate=cost(1000),
-            name="renew",
-        )(where, keep, near, far, *weights, *before)
-
-    renewed = jnp.concatenate(
-        [renew(*sums_one, 0, ()), renew(*sums_two, slots_one, (joined,))], axis=1
-    )
+    renewed = pl.pallas_call(
+        functools.partial(renew_kernel, squares),
+        in_specs=[smem] + [vmem] * 12,
+        out_specs=vmem,
+        out_shape=bf16(size, slots, own_rows, head_size),
+        scratch_shapes=[VMEM(sums_shape, jnp.float32)],
+        compiler_params=params,
+        cost_estimate=cost(2000),
+        name="renew",
+    )(where, keep, near, far, *weights, joined)
     back = lax.all_to_all(renewed, "seq", 0, 0, tiled=True)
-    back = back.reshape(2, squares, 2, slots_all, own_rows, head_size).transpose(1, 3, 0, 2, 4, 5)
-    back = back.reshape(squares, PLACES * slots_all, own_rows, head_size)[:, : 3 * heads]
+    back = back.reshape(2, squares, 2, slots, own_rows, head_size).transpose(1, 3, 0, 2, 4, 5)
+    back = back.reshape(squares, PLACES * slots, own_rows, head_size)[:, : 3 * heads]
     renewed_out = (
         back.reshape(squares, heads, 3, own_rows, head_size)
         .transpose(3, 2, 0, 1, 4)

time: 122 us -> 111 us (0.910)
  Pallas kernels: 27.4 us -> 17 us
  waiting for transfers between devices: 50.9 us -> 54.1 us
  blocking collectives: 19.1 us -> 17.6 us
    pallas_call x4 -> x2, Pallas kernels: 18.9 us -> 10.4 us  [the longest x1 7.52 us: square_body(): pl.pallas_call(functools.partial(key_kernel, squares, heads), grid=(heads...]
    ppermute x23 -> x18, waiting for transfers between devices: 50.9 us -> 54.1 us  [swap(): return lax.ppermute(array, 'seq', [(at, at ^ step) for at in range(size)])]
    pallas_call x1, Pallas kernels: 6 us -> 4.06 us  [square_body(): pl.pallas_call(functools.partial(query_kernel, squares), grid=(heads,), i...]
    all_to_all x1, blocking collectives: 19.1 us -> 17.6 us  [square_body(): back = lax.all_to_all(renewed, 'seq', 0, 0, tiled=True)]
    ppermute x23 -> x18, starting transfers between devices: 19.9 us -> 18.7 us  [swap(): return lax.ppermute(array, 'seq', [(at, at ^ step) for at in range(size)])]
  transfers between devices with their start and end apart: 23 -> 18, of which waited for: 12 -> 11; matrix products, arithmetic and copies ran while one was open for 0% -> 0% of each run, Pallas kernels for 14% -> 6%
where the time goes in v3:
time: 111 us
  waiting for transfers between devices  54.1 us (49%)
  starting transfers between devices  18.7 us (17%)
  blocking collectives  17.6 us (16%)
  Pallas kernels  17 us (15%)
  local copies, waits for them, and re-layouts  2.29 us (2%)
    ppermute x18, waiting for transfers between devices, swap(): return lax.ppermute(array, 'seq', [(at, at ^ step) for at in range(size)])  54.1 us
    ppermute x18, starting transfers between devices, swap(): return lax.ppermute(array, 'seq', [(at, at ^ step) for at in range(size)])  18.7 us
    all_to_all x1, blocking collectives, square_body(): back = lax.all_to_all(renewed, 'seq', 0, 0, tiled=True)  17.6 us
    pallas_call x1, Pallas kernels, square_body(): pl.pallas_call(functools.partial(key_kernel, squares, heads), grid=(heads...  7.52 us
    pallas_call x1, Pallas kernels, square_body(): pl.pallas_call(functools.partial(query_kernel, squares), grid=(heads,), i...  4.06 us
    pallas_call x1, Pallas kernels, square_body(): pl.pallas_call(functools.partial(renew_kernel, squares), in_specs=[smem]...  2.9 us
  transfers between devices with their start and end apart: 18, of which 11 were waited for; matrix products, arithmetic and copies ran while one was open for 0% of the time, Pallas kernels for 6%

profile of v3, /device:TPU:0, one launch (start us, length us, event | category | flops | bytes accessed | tf_op | source)
XLA Modules:
  0.0 110.8 jit_solution(1373757668753222140)
XLA Ops:
  0.6 0.0 copy-start.3
  0.6 0.0 copy-start
  0.7 0.0 copy-start.1
  0.7 0.0 copy-start.2
  0.7 1.2 %copy.10 = bf16[32,3,20,128]{3,0,1,2:T(8,128)(2,1)S(1)} copy(bf16[32,3,20,128]{3,0,2,1:T(8,128)(2,1)} %param.9) | data formatting | bytes 983040 | tf_op args[4]
  1.9 0.1 dynamic-slice_bitcast_fusion.1
  2.0 4.0 %collective-permute-start.5 = (bf16[5,3,32,128]{3,2,1,0:T(8,128)(2,1)S(1)}, bf16[5,3,32,128]{3,2,1,0:T(8,128)(2,1)S(1)}, u32[]{:S(2)}, u32[]{:S(2)}) collective-permute-start(bf16[5,3,32,128]{3,2,1,0:T(8,128)(2,1)S(1)} %get-tuple-element.31), channel_id=1, source_target_pairs={{0,6},{1,7},{2,4},{3,5},{4,2},{5,3},{6,0},{7,1},{8,14},{9,15},{10,... | collective-permute-start | bytes 368648 | tf_op jit(solution)/shard_map/ppermute | solution.py:234
  6.0 0.4 collective-permute-start.4
  6.5 0.2 collective-permute-start.3
  6.7 3.5 %collective-permute-done.5 = bf16[5,3,32,128]{3,2,1,0:T(8,128)(2,1)S(1)} collective-permute-done((bf16[5,3,32,128]{3,2,1,0:T(8,128)(2,1)S(1)}, bf16[5,3,32,128]{3,2,1,0:T(8,128)(2,1)S(1)}, u32[]{:S(2)}, u32[]{:S(2)}) %collective-permute-start.5) | collective-permute-done | bytes 122912 | tf_op jit(solution)/shard_map/ppermute | solution.py:234
  10.2 2.0 %collective-permute-done.4 = bf16[5,3,32,128]{3,2,1,0:T(8,128)(2,1)S(1)} collective-permute-done((bf16[5,3,32,128]{3,2,1,0:T(8,128)(2,1)S(1)}, bf16[5,3,32,128]{3,2,1,0:T(8,128)(2,1)S(1)}, u32[]{:S(2)}, u32[]{:S(2)}) %collective-permute-start.4) | collective-permute-done | bytes 122912 | tf_op jit(solution)/shard_map/ppermute | solution.py:234
  12.2 2.7 %collective-permute-start.9 = (bf16[2,5,3,32,128]{4,3,2,1,0:T(8,128)(2,1)S(1)}, bf16[2,5,3,32,128]{4,3,2,1,0:T(8,128)(2,1)S(1)}, u32[]{:S(2)}, u32[]{:S(2)}) collective-permute-start(bf16[2,5,3,32,128]{4,3,2,1,0:T(8,128)(2,1)S(1)} %pad_maximum_fusion.1.refs_5_.refs_1_), channel_id=1, source_target_pairs={{0,8},{1,9},{2,10},{3,11},{4,12},{5,13},{6,14},{7,15},{8,0},{9,1},... | collective-permute-start | bytes 737288 | tf_op jit(solution)/shard_map/ppermute | solution.py:234
  14.8 0.0 collective-permute-done.3
  14.9 0.4 collective-permute-start.8
  15.3 0.0 copy-done.3
  15.3 0.1 copy.9.rate_ref
  15.4 0.1 pad_add_fusion.where_ref
  15.5 0.0 copy-done
  15.5 0.0 copy-done.1
  15.5 0.0 copy-done.2
  15.5 1.1 split.1
  16.6 1.1 collective-permute-start
  17.7 1.6 %collective-permute-start.1 = (bf16[3,128,640]{2,1,0:T(8,128)(2,1)S(1)}, bf16[3,128,640]{2,1,0:T(8,128)(2,1)S(1)}, u32[]{:S(2)}, u32[]{:S(2)}) collective-permute-start(bf16[3,128,640]{2,1,0:T(8,128)(2,1)S(1)} %get-tuple-element.17), channel_id=1, source_target_pairs={{0,4},{1,5},{2,6},{3,7},{4,0},{5,1},{6,2},{7,3},{8,12},{9,13},{10,... | collective-permute-start | bytes 1474568 | tf_op jit(solution)/shard_map/ppermute | solution.py:234
  19.2 0.9 collective-permute-start.2
  20.1 11.7 %collective-permute-done.9.refs_9_.refs_5_ = bf16[2,5,3,32,128]{4,3,2,1,0:T(8,128)(2,1)S(1)} collective-permute-done((bf16[2,5,3,32,128]{4,3,2,1,0:T(8,128)(2,1)S(1)}, bf16[2,5,3,32,128]{4,3,2,1,0:T(8,128)(2,1)S(1)}, u32[]{:S(2)}, u32[]{:S(2)}) %collective-permute-start.9) | collective-permute-done | bytes 245792 | tf_op jit(solution)/shard_map/ppermute | solution.py:234
  31.8 0.0 collective-permute-start.7
  31.8 4.1 %collective-permute-done.8.refs_8_.refs_4_ = bf16[2,5,3,32,128]{4,3,2,1,0:T(8,128)(2,1)S(1)} collective-permute-done((bf16[2,5,3,32,128]{4,3,2,1,0:T(8,128)(2,1)S(1)}, bf16[2,5,3,32,128]{4,3,2,1,0:T(8,128)(2,1)S(1)}, u32[]{:S(2)}, u32[]{:S(2)}) %collective-permute-start.8) | collective-permute-done | bytes 245792 | tf_op jit(solution)/shard_map/ppermute | solution.py:234
  35.9 0.0 collective-permute-start.6
  35.9 0.0 collective-permute-done.7.refs_7_.refs_3_
  35.9 0.5 collective-permute-start.11
  36.4 1.0 collective-permute-done.6.refs_6_.refs_2_
  37.4 0.1 collective-permute-start.10
  37.5 0.0 collective-permute-done.refs_1_
  37.5 3.7 %collective-permute-done.1.refs_2_ = bf16[3,128,640]{2,1,0:T(8,128)(2,1)S(1)} collective-permute-done((bf16[3,128,640]{2,1,0:T(8,128)(2,1)S(1)}, bf16[3,128,640]{2,1,0:T(8,128)(2,1)S(1)}, u32[]{:S(2)}, u32[]{:S(2)}) %collective-permute-start.1) | collective-permute-done | bytes 491552 | tf_op jit(solution)/shard_map/ppermute | solution.py:234
  41.2 8.6 %collective-permute-done.2.refs_3_ = bf16[3,128,640]{2,1,0:T(8,128)(2,1)S(1)} collective-permute-done((bf16[3,128,640]{2,1,0:T(8,128)(2,1)S(1)}, bf16[3,128,640]{2,1,0:T(8,128)(2,1)S(1)}, u32[]{:S(2)}, u32[]{:S(2)}) %collective-permute-start.2) | collective-permute-done | bytes 491552 | tf_op jit(solution)/shard_map/ppermute | solution.py:234
  49.9 0.0 collective-permute-done.11.refs_11_.refs_7_
  49.9 0.0 collective-permute-done.10.refs_10_.refs_6_
  49.9 7.5 %key_side.1 = (f32[2,4,512,128]{3,2,1,0:T(8,128)S(1)}, bf16[4,512,128]{2,1,0:T(8,128)(2,1)S(1)}, bf16[4,512,128]{2,1,0:T(8,128)(2,1)S(1)}) custom-call(s32[2]{0:T(128)S(1)} %pad_add_fusion.where_ref, bf16[3,128,640]{2,1,0:T(8,128)(2,1)S(1)} %get-tuple-element.15.refs_0_, bf16[3,128,640]{2,1,0:T(8,128)(2,1)S(1)} %collective-permute-done.refs_1_, ...), custom_call_target="tpu_custom_call" | custom-call | flops 2000000000 | bytes 4000000 | tf_op jit(solution)/shard_map/key_side/pallas_call | solution.py:273
  57.4 0.1 collective-permute-start.16
  57.5 0.5 collective-permute-start.15
  58.0 1.4 %collective-permute-done.16 = bf16[4,512,128]{2,1,0:T(8,128)(2,1)S(1)} collective-permute-done((bf16[4,512,128]{2,1,0:T(8,128)(2,1)S(1)}, bf16[4,512,128]{2,1,0:T(8,128)(2,1)S(1)}, u32[]{:S(2)}, u32[]{:S(2)}) %collective-permute-start.16) | collective-permute-done | bytes 524320 | tf_op jit(solution)/shard_map/ppermute | solution.py:234
  59.4 0.1 fusion
  59.5 1.2 %collective-permute-start.17 = (bf16[4,512,128]{2,1,0:T(8,128)(2,1)S(1)}, bf16[4,512,128]{2,1,0:T(8,128)(2,1)S(1)}, u32[]{:S(2)}, u32[]{:S(2)}) collective-permute-start(bf16[4,512,128]{2,1,0:T(8,128)(2,1)S(1)} %fusion), channel_id=1, source_target_pairs={{0,8},{1,9},{2,10},{3,11},{4,12},{5,13},{6,14},{7,15},{8,0},{9,1},... | collective-permute-start | bytes 1572872 | tf_op jit(solution)/shard_map/ppermute | solution.py:234
  60.7 4.1 %query_side.1 = (bf16[128,640]{1,0:T(8,128)(2,1)S(1)}, bf16[128,640]{1,0:T(8,128)(2,1)S(1)}, bf16[128,640]{1,0:T(8,128)(2,1)S(1)}, bf16[128,640]{1,0:T(8,128)(2,1)S(1)}) custom-call(bf16[3,128,640]{2,1,0:T(8,128)(2,1)S(1)} %get-tuple-element.15.refs_0_, bf16[3,128,640]{2,1,0:T(8,128)(2,1)S(1)} %collective-permute-done.refs_1_, ...), custom_call_target="tpu_custom_call" | custom-call | flops 1000000000 | bytes 4000000 | tf_op jit(solution)/shard_map/query_side/pallas_call | solution.py:296
  64.8 1.6 %collective-permute-start.12 = (bf16[128,640]{1,0:T(8,128)(2,1)S(1)}, bf16[128,640]{1,0:T(8,128)(2,1)S(1)}, u32[]{:S(2)}, u32[]{:S(2)}) collective-permute-start(bf16[128,640]{1,0:T(8,128)(2,1)S(1)} %get-tuple-element.20), channel_id=1, source_target_pairs={{0,2},{1,3},{2,0},{3,1},{4,6},{5,7},{6,4},{7,5},{8,10},{9,11},{10,... | collective-permute-start | bytes 491528 | tf_op jit(solution)/shard_map/ppermute | solution.py:234
  66.4 2.4 %collective-permute-start.13 = (bf16[128,640]{1,0:T(8,128)(2,1)S(1)}, bf16[128,640]{1,0:T(8,128)(2,1)S(1)}, u32[]{:S(2)}, u32[]{:S(2)}) collective-permute-start(bf16[128,640]{1,0:T(8,128)(2,1)S(1)} %get-tuple-element.21), channel_id=1, source_target_pairs={{0,4},{1,5},{2,6},{3,7},{4,0},{5,1},{6,2},{7,3},{8,12},{9,13},{10,... | collective-permute-start | bytes 491528 | tf_op jit(solution)/shard_map/ppermute | solution.py:234
  68.8 1.0 collective-permute-start.14
  69.8 1.1 collective-permute-done.12.refs_1_
  70.8 5.7 %collective-permute-done.13.refs_2_ = bf16[128,640]{1,0:T(8,128)(2,1)S(1)} collective-permute-done((bf16[128,640]{1,0:T(8,128)(2,1)S(1)}, bf16[128,640]{1,0:T(8,128)(2,1)S(1)}, u32[]{:S(2)}, u32[]{:S(2)}) %collective-permute-start.13) | collective-permute-done | bytes 163872 | tf_op jit(solution)/shard_map/ppermute | solution.py:234
  76.6 11.3 %collective-permute-done.14.refs_3_ = bf16[128,640]{1,0:T(8,128)(2,1)S(1)} collective-permute-done((bf16[128,640]{1,0:T(8,128)(2,1)S(1)}, bf16[128,640]{1,0:T(8,128)(2,1)S(1)}, u32[]{:S(2)}, u32[]{:S(2)}) %collective-permute-start.14) | collective-permute-done | bytes 163872 | tf_op jit(solution)/shard_map/ppermute | solution.py:234
  87.9 1.4 %join.1 = (bf16[128,2560]{1,0:T(8,128)(2,1)}, f32[8,128]{1,0:T(8,128)S(1)}) custom-call(s32[2]{0:T(128)S(1)} %pad_add_fusion.where_ref, bf16[128,640]{1,0:T(8,128)(2,1)S(1)} %get-tuple-element.19.refs_0_, bf16[128,640]{1,0:T(8,128)(2,1)S(1)} %collective-permute-done.12.refs_1_, bf16[128,640]{1,0:T(8,128)(2,1)S(1)} %collective-permute-done.13.refs_2_, ...), custom_call_target="tpu_custom_call" | custom-call | flops 10000000 | bytes 4000000 | tf_op jit(solution)/shard_map/join/pallas_call | solution.py:307
  89.3 0.0 collective-permute-done.15.near_ref
  89.3 0.0 collective-permute-done.17.far_ref
  89.3 2.9 %renew.1 = bf16[16,4,32,128]{3,2,1,0:T(8,128)(2,1)S(1)} custom-call(s32[2]{0:T(128)S(1)} %pad_add_fusion.where_ref, f32[2,4,512,128]{3,2,1,0:T(8,128)S(1)} %get-tuple-element.24.mine_ref, bf16[4,512,128]{2,1,0:T(8,128)(2,1)S(1)} %collective-permute-done.15.near_ref, bf16[4,512,128]{2,1,0:T(8,128)(2,1)S(1)} %collective-permute-done.17.far_ref, ...), custom_call_target="tpu_custom_call" | custom-call | flops 2000000000 | bytes 4000000 | tf_op jit(solution)/shard_map/renew/pallas_call | solution.py:317
  92.2 17.6 %all_to_all.5 = bf16[16,4,32,128]{3,2,1,0:T(8,128)(2,1)S(1)} all-to-all(bf16[16,4,32,128]{3,2,1,0:T(8,128)(2,1)S(1)} %renew.1), channel_id=1, replica_groups=mesh['groups'=2,'seq'=16] {'seq'}, dimensions={0} | all-to-all | bytes 1048576 | tf_op jit(solution)/shard_map/all_to_all | solution.py:327
  109.8 0.1 copy.11
  109.9 0.8 copy.12
  (3 shorter events, 0.1 us)
Async XLA Ops:
  0.6 14.6 %copy-start.3 = (f32[128,20]{0,1:T(8,128)S(1)}, f32[128,20]{0,1:T(8,128)}, u32[]{:S(2)}) copy-start(f32[128,20]{0,1:T(8,128)} %param.8) | copy-start | bytes 30724
  0.6 14.8 %copy-start = (bf16[128,2560]{1,0:T(8,128)(2,1)S(1)}, bf16[128,2560]{1,0:T(8,128)(2,1)}, u32[]{:S(2)}) copy-start(bf16[128,2560]{1,0:T(8,128)(2,1)} %q_ref.1) | copy-start | bytes 1966084
  0.7 14.8 %copy-start.1 = (bf16[128,2560]{1,0:T(8,128)(2,1)S(1)}, bf16[128,2560]{1,0:T(8,128)(2,1)}, u32[]{:S(2)}) copy-start(bf16[128,2560]{1,0:T(8,128)(2,1)} %k_ref.1) | copy-start | bytes 1966084
  0.7 14.8 %copy-start.2 = (bf16[128,2560]{1,0:T(8,128)(2,1)S(1)}, bf16[128,2560]{1,0:T(8,128)(2,1)}, u32[]{:S(2)}) copy-start(bf16[128,2560]{1,0:T(8,128)(2,1)} %v_ref.1) | copy-start | bytes 1966084
  2.0 8.2 %collective-permute-start.5 = (bf16[5,3,32,128]{3,2,1,0:T(8,128)(2,1)S(1)}, bf16[5,3,32,128]{3,2,1,0:T(8,128)(2,1)S(1)}, u32[]{:S(2)}, u32[]{:S(2)}) collective-permute-start(bf16[5,3,32,128]{3,2,1,0:T(8,128)(2,1)S(1)} %get-tuple-element.31), channel_id=1, source_target_pairs={{0,6},{1,7},{2,4},{3,5},{4,2},{5,3},{6,0},{7,1},{8,14},{9,15},{10,... | collective-permute-start | bytes 368648 | tf_op jit(solution)/shard_map/ppermute | solution.py:234
  6.0 6.1 %collective-permute-start.4 = (bf16[5,3,32,128]{3,2,1,0:T(8,128)(2,1)S(1)}, bf16[5,3,32,128]{3,2,1,0:T(8,128)(2,1)S(1)}, u32[]{:S(2)}, u32[]{:S(2)}) collective-permute-start(bf16[5,3,32,128]{3,2,1,0:T(8,128)(2,1)S(1)} %get-tuple-element.30), channel_id=1, source_target_pairs={{0,4},{1,5},{2,6},{3,7},{4,0},{5,1},{6,2},{7,3},{8,12},{9,13},{10,... | collective-permute-start | bytes 368648 | tf_op jit(solution)/shard_map/ppermute | solution.py:234
  6.5 8.4 %collective-permute-start.3 = (bf16[5,3,32,128]{3,2,1,0:T(8,128)(2,1)S(1)}, bf16[5,3,32,128]{3,2,1,0:T(8,128)(2,1)S(1)}, u32[]{:S(2)}, u32[]{:S(2)}) collective-permute-start(bf16[5,3,32,128]{3,2,1,0:T(8,128)(2,1)S(1)} %get-tuple-element.32), channel_id=1, source_target_pairs={{0,2},{1,3},{2,0},{3,1},{4,6},{5,7},{6,4},{7,5},{8,10},{9,11},{10,... | collective-permute-start | bytes 368648 | tf_op jit(solution)/shard_map/ppermute | solution.py:234
  12.2 19.6 %collective-permute-start.9 = (bf16[2,5,3,32,128]{4,3,2,1,0:T(8,128)(2,1)S(1)}, bf16[2,5,3,32,128]{4,3,2,1,0:T(8,128)(2,1)S(1)}, u32[]{:S(2)}, u32[]{:S(2)}) collective-permute-start(bf16[2,5,3,32,128]{4,3,2,1,0:T(8,128)(2,1)S(1)} %pad_maximum_fusion.1.refs_5_.refs_1_), channel_id=1, source_target_pairs={{0,8},{1,9},{2,10},{3,11},{4,12},{5,13},{6,14},{7,15},{8,0},{9,1},... | collective-permute-start | bytes 737288 | tf_op jit(solution)/shard_map/ppermute | solution.py:234
  14.9 21.0 %collective-permute-start.8 = (bf16[2,5,3,32,128]{4,3,2,1,0:T(8,128)(2,1)S(1)}, bf16[2,5,3,32,128]{4,3,2,1,0:T(8,128)(2,1)S(1)}, u32[]{:S(2)}, u32[]{:S(2)}) collective-permute-start(bf16[2,5,3,32,128]{4,3,2,1,0:T(8,128)(2,1)S(1)} %pad_maximum_fusion.refs_4_.refs_0_), channel_id=1, source_target_pairs={{0,8},{1,9},{2,10},{3,11},{4,12},{5,13},{6,14},{7,15},{8,0},{9,1},... | collective-permute-start | bytes 737288 | tf_op jit(solution)/shard_map/ppermute | solution.py:234
  16.6 21.0 %collective-permute-start = (bf16[3,128,640]{2,1,0:T(8,128)(2,1)S(1)}, bf16[3,128,640]{2,1,0:T(8,128)(2,1)S(1)}, u32[]{:S(2)}, u32[]{:S(2)}) collective-permute-start(bf16[3,128,640]{2,1,0:T(8,128)(2,1)S(1)} %get-tuple-element.16), channel_id=1, source_target_pairs={{0,2},{1,3},{2,0},{3,1},{4,6},{5,7},{6,4},{7,5},{8,10},{9,11},{10,... | collective-permute-start | bytes 1474568 | tf_op jit(solution)/shard_map/ppermute | solution.py:234
  17.7 23.6 %collective-permute-start.1 = (bf16[3,128,640]{2,1,0:T(8,128)(2,1)S(1)}, bf16[3,128,640]{2,1,0:T(8,128)(2,1)S(1)}, u32[]{:S(2)}, u32[]{:S(2)}) collective-permute-start(bf16[3,128,640]{2,1,0:T(8,128)(2,1)S(1)} %get-tuple-element.17), channel_id=1, source_target_pairs={{0,4},{1,5},{2,6},{3,7},{4,0},{5,1},{6,2},{7,3},{8,12},{9,13},{10,... | collective-permute-start | bytes 1474568 | tf_op jit(solution)/shard_map/ppermute | solution.py:234
  19.2 30.6 %collective-permute-start.2 = (bf16[3,128,640]{2,1,0:T(8,128)(2,1)S(1)}, bf16[3,128,640]{2,1,0:T(8,128)(2,1)S(1)}, u32[]{:S(2)}, u32[]{:S(2)}) collective-permute-start(bf16[3,128,640]{2,1,0:T(8,128)(2,1)S(1)} %get-tuple-element.18), channel_id=1, source_target_pairs={{0,6},{1,7},{2,4},{3,5},{4,2},{5,3},{6,0},{7,1},{8,14},{9,15},{10,... | collective-permute-start | bytes 1474568 | tf_op jit(solution)/shard_map/ppermute | solution.py:234
  31.8 4.1 %collective-permute-start.7 = (bf16[2,5,3,32,128]{4,3,2,1,0:T(8,128)(2,1)S(1)}, bf16[2,5,3,32,128]{4,3,2,1,0:T(8,128)(2,1)S(1)}, u32[]{:S(2)}, u32[]{:S(2)}) collective-permute-start(bf16[2,5,3,32,128]{4,3,2,1,0:T(8,128)(2,1)S(1)} %pad_maximum_fusion.1.refs_5_.refs_1_), channel_id=1, source_target_pairs={{0,1},{1,0},{2,3},{3,2},{4,5},{5,4},{6,7},{7,6},{8,9},{9,8},{10,11... | collective-permute-start | bytes 737288 | tf_op jit(solution)/shard_map/ppermute | solution.py:234
  35.9 1.5 %collective-permute-start.6 = (bf16[2,5,3,32,128]{4,3,2,1,0:T(8,128)(2,1)S(1)}, bf16[2,5,3,32,128]{4,3,2,1,0:T(8,128)(2,1)S(1)}, u32[]{:S(2)}, u32[]{:S(2)}) collective-permute-start(bf16[2,5,3,32,128]{4,3,2,1,0:T(8,128)(2,1)S(1)} %pad_maximum_fusion.refs_4_.refs_0_), channel_id=1, source_target_pairs={{0,1},{1,0},{2,3},{3,2},{4,5},{5,4},{6,7},{7,6},{8,9},{9,8},{10,11... | collective-permute-start | bytes 737288 | tf_op jit(solution)/shard_map/ppermute | solution.py:234
  35.9 14.0 %collective-permute-start.11 = (bf16[2,5,3,32,128]{4,3,2,1,0:T(8,128)(2,1)S(1)}, bf16[2,5,3,32,128]{4,3,2,1,0:T(8,128)(2,1)S(1)}, u32[]{:S(2)}, u32[]{:S(2)}) collective-permute-start(bf16[2,5,3,32,128]{4,3,2,1,0:T(8,128)(2,1)S(1)} %collective-permute-done.9.refs_9_.refs_5_), channel_id=1, source_target_pairs={{0,1},{1,0},{2,3},{3,2},{4,5},{5,4},{6,7},{7,6},{8,9},{9,8},{10,11... | collective-permute-start | bytes 737288 | tf_op jit(solution)/shard_map/ppermute | solution.py:234
  37.4 12.5 %collective-permute-start.10 = (bf16[2,5,3,32,128]{4,3,2,1,0:T(8,128)(2,1)S(1)}, bf16[2,5,3,32,128]{4,3,2,1,0:T(8,128)(2,1)S(1)}, u32[]{:S(2)}, u32[]{:S(2)}) collective-permute-start(bf16[2,5,3,32,128]{4,3,2,1,0:T(8,128)(2,1)S(1)} %collective-permute-done.8.refs_8_.refs_4_), channel_id=1, source_target_pairs={{0,1},{1,0},{2,3},{3,2},{4,5},{5,4},{6,7},{7,6},{8,9},{9,8},{10,11... | collective-permute-start | bytes 737288 | tf_op jit(solution)/shard_map/ppermute | solution.py:234
  57.4 2.0 %collective-permute-start.16 = (bf16[4,512,128]{2,1,0:T(8,128)(2,1)S(1)}, bf16[4,512,128]{2,1,0:T(8,128)(2,1)S(1)}, u32[]{:S(2)}, u32[]{:S(2)}) collective-permute-start(bf16[4,512,128]{2,1,0:T(8,128)(2,1)S(1)} %get-tuple-element.26), channel_id=1, source_target_pairs={{0,1},{1,0},{2,3},{3,2},{4,5},{5,4},{6,7},{7,6},{8,9},{9,8},{10,11... | collective-permute-start | bytes 1572872 | tf_op jit(solution)/shard_map/ppermute | solution.py:234
  57.5 31.9 %collective-permute-start.15 = (bf16[4,512,128]{2,1,0:T(8,128)(2,1)S(1)}, bf16[4,512,128]{2,1,0:T(8,128)(2,1)S(1)}, u32[]{:S(2)}, u32[]{:S(2)}) collective-permute-start(bf16[4,512,128]{2,1,0:T(8,128)(2,1)S(1)} %get-tuple-element.25), channel_id=1, source_target_pairs={{0,1},{1,0},{2,3},{3,2},{4,5},{5,4},{6,7},{7,6},{8,9},{9,8},{10,11... | collective-permute-start | bytes 1572872 | tf_op jit(solution)/shard_map/ppermute | solution.py:234
  59.5 29.8 %collective-permute-start.17 = (bf16[4,512,128]{2,1,0:T(8,128)(2,1)S(1)}, bf16[4,512,128]{2,1,0:T(8,128)(2,1)S(1)}, u32[]{:S(2)}, u32[]{:S(2)}) collective-permute-start(bf16[4,512,128]{2,1,0:T(8,128)(2,1)S(1)} %fusion), channel_id=1, source_target_pairs={{0,8},{1,9},{2,10},{3,11},{4,12},{5,13},{6,14},{7,15},{8,0},{9,1},... | collective-permute-start | bytes 1572872 | tf_op jit(solution)/shard_map/ppermute | solution.py:234
  64.8 6.0 %collective-permute-start.12 = (bf16[128,640]{1,0:T(8,128)(2,1)S(1)}, bf16[128,640]{1,0:T(8,128)(2,1)S(1)}, u32[]{:S(2)}, u32[]{:S(2)}) collective-permute-start(bf16[128,640]{1,0:T(8,128)(2,1)S(1)} %get-tuple-element.20), channel_id=1, source_target_pairs={{0,2},{1,3},{2,0},{3,1},{4,6},{5,7},{6,4},{7,5},{8,10},{9,11},{10,... | collective-permute-start | bytes 491528 | tf_op jit(solution)/shard_map/ppermute | solution.py:234
  66.4 10.2 %collective-permute-start.13 = (bf16[128,640]{1,0:T(8,128)(2,1)S(1)}, bf16[128,640]{1,0:T(8,128)(2,1)S(1)}, u32[]{:S(2)}, u32[]{:S(2)}) collective-permute-start(bf16[128,640]{1,0:T(8,128)(2,1)S(1)} %get-tuple-element.21), channel_id=1, source_target_pairs={{0,4},{1,5},{2,6},{3,7},{4,0},{5,1},{6,2},{7,3},{8,12},{9,13},{10,... | collective-permute-start | bytes 491528 | tf_op jit(solution)/shard_map/ppermute | solution.py:234
  68.8 19.1 %collective-permute-start.14 = (bf16[128,640]{1,0:T(8,128)(2,1)S(1)}, bf16[128,640]{1,0:T(8,128)(2,1)S(1)}, u32[]{:S(2)}, u32[]{:S(2)}) collective-permute-start(bf16[128,640]{1,0:T(8,128)(2,1)S(1)} %get-tuple-element.22), channel_id=1, source_target_pairs={{0,6},{1,7},{2,4},{3,5},{4,2},{5,3},{6,0},{7,1},{8,14},{9,15},{10,... | collective-permute-start | bytes 491528 | tf_op jit(solution)/shard_map/ppermute | solution.py:234

commit v4 on v3

--- a/solution.py
+++ b/solution.py
@@ -47,13 +47,12 @@
 
 
 def join_kernel(where_ref, *refs):
-    ins, (out_ref, done_ref) = refs[:-2], refs[-2:]
+    ins, out_ref = refs[:-1], refs[-1]
     spot = where_ref[0]
     width = ins[0].shape[1]
     for rel, in_ref in enumerate(ins):
         at = pl.multiple_of((spot ^ rel) * width, width)
         out_ref[:, pl.ds(at, width)] = in_ref[...]
-    done_ref[...] = jnp.zeros_like(done_ref)
 
 
 def weight_rows(w_refs, rel, matrix):
@@ -100,20 +99,20 @@
     )
     second = jnp.concatenate([weight_rows(w_refs, rel, 2) for rel in range(PLACES)], axis=0)
     raw = dot(both_maps, keys, NT)
-    raw_third = raw[hid:]
+    third = raw[hid:] * scale_in
     back = dot(second, scaled, NT)
     half_first = raw[:hid] * (0.5 * scale_in)
     tanh = jnp.tanh(half_first)
     act = half_first + half_first * tanh
-    hidden = (act * raw_third).astype(jnp.bfloat16)
+    hidden = (act * third).astype(jnp.bfloat16)
     grad_third = (back * act).astype(jnp.bfloat16)
     twice_slope = (1.0 + tanh) + act * (1.0 - tanh)
-    grad_first = (back * raw_third * twice_slope).astype(jnp.bfloat16)
+    grad_first = (back * third * twice_slope).astype(jnp.bfloat16)
     firsts = dot(jnp.concatenate([grad_first, grad_third], axis=0), keys, NN)
     values = (
-        firsts[:hid] * (0.5 * scale_in * scale_in),
+        firsts[:hid] * (0.5 * scale_in),
         firsts[hid:] * scale_in,
-        dot(hidden, scaled, NN) * scale_in,
+        dot(hidden, scaled, NN),
     )
     for rel in range(PLACES):
         for apart in range(squares):
@@ -135,9 +134,9 @@
     )
     queries = jnp.concatenate([q_ref[0] for q_ref in ins], axis=0)
     half_first = dot(queries, first_map, NT) * (0.5 * scale_in)
-    third = dot(queries, third_map, NT)
+    third = dot(queries, third_map, NT) * scale_in
     hidden = ((half_first + half_first * jnp.tanh(half_first)) * third).astype(jnp.bfloat16)
-    out = (dot(hidden, second, NN) * (scale_in * scale_out)).astype(jnp.bfloat16)
+    out = (dot(hidden, second, NN) * scale_out).astype(jnp.bfloat16)
     rows = outs[0].shape[0]
     for rel, out_ref in enumerate(outs):
         out_ref[...] = out[rel * rows : (rel + 1) * rows]
@@ -239,8 +238,6 @@
     def bf16(*shape):
         return jax.ShapeDtypeStruct(shape, jnp.bfloat16)
 
-    token = jax.ShapeDtypeStruct((8, 128), jnp.float32)
-
     moved = across(
         pl.pallas_call(
             split_kernel,
@@ -262,8 +259,10 @@
         ]
     )
     own = [jnp.stack(pieces[:cut]), jnp.stack(pieces[cut:])]
+    own = list(lax.optimization_barrier(own))
     other = [swap(w, half) for w in own]
-    weights = [own, [swap(w, 1) for w in own], other, [swap(w, 1) for w in other]]
+    late, moved[2:] = lax.optimization_barrier((other, moved[2:]))
+    weights = [own, [swap(w, 1) for w in own], other, [swap(w, 1) for w in late]]
     weights = [w for pair in weights for w in pair]
 
     weight_spec = pl.BlockSpec((cut, 1, 3, own_rows, head_size), lambda h: (0, h, 0, 0, 0))
@@ -304,26 +303,28 @@
         cost_estimate=cost(1000),
         name="query_side",
     )(*moved, *weights)
-    applied, joined = pl.pallas_call(
+    parts = across(parts)
+    far, parts[2:] = lax.optimization_barrier((far, parts[2:]))
+    applied = pl.pallas_call(
         join_kernel,
         in_specs=[smem] + [vmem] * squares,
-        out_specs=[vmem] * 2,
-        out_shape=[bf16(row_count, num_heads * head_size), token],
+        out_specs=vmem,
+        out_shape=bf16(row_count, num_heads * head_size),
         compiler_params=params,
         cost_estimate=cost(10),
         name="join",
-    )(where, *across(parts))
+    )(where, *parts)
 
     renewed = pl.pallas_call(
         functools.partial(renew_kernel, squares),
-        in_specs=[smem] + [vmem] * 12,
+        in_specs=[smem] + [vmem] * 11,
         out_specs=vmem,
         out_shape=bf16(size, slots, own_rows, head_size),
         scratch_shapes=[VMEM(sums_shape, jnp.float32)],
         compiler_params=params,
         cost_estimate=cost(2000),
         name="renew",
-    )(where, keep, near, far, *weights, joined)
+    )(where, keep, near, far, *weights)
     back = lax.all_to_all(renewed, "seq", 0, 0, tiled=True)
     back = back.reshape(2, squares, 2, slots, own_rows, head_size).transpose(1, 3, 0, 2, 4, 5)
     back = back.reshape(squares, PLACES * slots, own_rows, head_size)[:, : 3 * heads]

time: 111 us -> 107 us (0.964)
  blocking collectives: 17.6 us -> 0 us
  starting transfers between devices: 18.7 us -> 26 us
  waiting for transfers between devices: 54.1 us -> 59.3 us
    all_to_all x1 -> x0, blocking collectives: 17.6 us -> none  [square_body(): back = lax.all_to_all(renewed, 'seq', 0, 0, tiled=True)]
    all_to_all x0 -> x1, starting transfers between devices: none -> 5.85 us  [square_body(): back = lax.all_to_all(renewed, 'seq', 0, 0, tiled=True)]
    ppermute x18, waiting for transfers between devices: 54.1 us -> 57.2 us  [swap(): return lax.ppermute(array, 'seq', [(at, at ^ step) for at in range(size)])]
    all_to_all x0 -> x1, waiting for transfers between devices: none -> 2.12 us  [square_body(): back = lax.all_to_all(renewed, 'seq', 0, 0, tiled=True)]
    ppermute x18, starting transfers between devices: 18.7 us -> 20.2 us  [swap(): return lax.ppermute(array, 'seq', [(at, at ^ step) for at in range(size)])]
  transfers between devices with their start and end apart: 18 -> 19, of which waited for: 11 -> 13; matrix products, arithmetic and copies ran while one was open for 0% -> 0% of each run, Pallas kernels for 6% -> 6%
where the time goes in v4:
time: 107 us
  waiting for transfers between devices  59.3 us (55%)
  starting transfers between devices  26 us (24%)
  Pallas kernels  18.1 us (17%)
  local copies, waits for them, and re-layouts  2.28 us (2%)
    ppermute x18, waiting for transfers between devices, swap(): return lax.ppermute(array, 'seq', [(at, at ^ step) for at in range(size)])  57.2 us
    ppermute x18, starting transfers between devices, swap(): return lax.ppermute(array, 'seq', [(at, at ^ step) for at in range(size)])  20.2 us
    pallas_call x1, Pallas kernels, square_body(): pl.pallas_call(functools.partial(key_kernel, squares, heads), grid=(heads...  7.8 us
    all_to_all x1, starting transfers between devices, square_body(): back = lax.all_to_all(renewed, 'seq', 0, 0, tiled=True)  5.85 us
    pallas_call x1, Pallas kernels, square_body(): pl.pallas_call(functools.partial(query_kernel, squares), grid=(heads,), i...  4.06 us
    pallas_call x1, Pallas kernels, square_body(): pl.pallas_call(functools.partial(renew_kernel, squares), in_specs=[smem]...  3.7 us
  transfers between devices with their start and end apart: 19, of which 13 were waited for; matrix products, arithmetic and copies ran while one was open for 0% of the time, Pallas kernels for 6%

profile of v4, /device:TPU:0, one launch (start us, length us, event | category | flops | bytes accessed | tf_op | source)
XLA Modules:
  0.0 106.7 jit_solution(15238841211119048394)
XLA Ops:
  0.6 0.0 copy-start.3
  0.6 0.0 copy-start.2
  0.7 0.0 copy-start.1
  0.7 0.0 copy-start
  0.7 1.2 %copy.10 = bf16[32,3,20,128]{3,0,1,2:T(8,128)(2,1)S(1)} copy(bf16[32,3,20,128]{3,0,2,1:T(8,128)(2,1)} %param.9) | data formatting | bytes 983040 | tf_op args[4]
  1.9 0.1 dynamic-slice_bitcast_fusion.1
  2.0 3.1 %collective-permute-start.2 = (bf16[5,3,32,128]{3,2,1,0:T(8,128)(2,1)S(1)}, bf16[5,3,32,128]{3,2,1,0:T(8,128)(2,1)S(1)}, u32[]{:S(2)}, u32[]{:S(2)}) collective-permute-start(bf16[5,3,32,128]{3,2,1,0:T(8,128)(2,1)S(1)} %get-tuple-element.44), channel_id=1, source_target_pairs={{0,4},{1,5},{2,6},{3,7},{4,0},{5,1},{6,2},{7,3},{8,12},{9,13},{10,... | collective-permute-start | bytes 368648 | tf_op jit(solution)/shard_map/ppermute | solution.py:233
  5.1 1.4 %collective-permute-start.3 = (bf16[5,3,32,128]{3,2,1,0:T(8,128)(2,1)S(1)}, bf16[5,3,32,128]{3,2,1,0:T(8,128)(2,1)S(1)}, u32[]{:S(2)}, u32[]{:S(2)}) collective-permute-start(bf16[5,3,32,128]{3,2,1,0:T(8,128)(2,1)S(1)} %get-tuple-element.45), channel_id=1, source_target_pairs={{0,6},{1,7},{2,4},{3,5},{4,2},{5,3},{6,0},{7,1},{8,14},{9,15},{10,... | collective-permute-start | bytes 368648 | tf_op jit(solution)/shard_map/ppermute | solution.py:233
  6.5 0.0 copy-done.3
  6.5 0.1 copy.9.rate_ref
  6.6 0.1 pad_add_fusion.where_ref
  6.7 0.0 copy-done.2
  6.7 0.0 copy-done.1
  6.7 0.0 copy-done
  6.7 1.1 %split.1 = (bf16[3,128,640]{2,1,0:T(8,128)(2,1)S(1)}, bf16[3,128,640]{2,1,0:T(8,128)(2,1)S(1)}, bf16[3,128,640]{2,1,0:T(8,128)(2,1)S(1)}, bf16[3,128,640]{2,1,0:T(8,128)(2,1)S(1)}) custom-call(s32[2]{0:T(128)S(1)} %pad_add_fusion.where_ref, bf16[128,2560]{1,0:T(8,128)(2,1)S(1)} %copy-done, bf16[128,2560]{1,0:T(8,128)(2,1)S(1)} %copy-done.1, ...), custom_call_target="tpu_custom_call" | custom-call | flops 10000000 | bytes 4000000 | tf_op jit(solution)/shard_map/split/pallas_call | solution.py:242
  7.8 1.6 %collective-permute-start.6 = (bf16[3,128,640]{2,1,0:T(8,128)(2,1)S(1)}, bf16[3,128,640]{2,1,0:T(8,128)(2,1)S(1)}, u32[]{:S(2)}, u32[]{:S(2)}) collective-permute-start(bf16[3,128,640]{2,1,0:T(8,128)(2,1)S(1)} %get-tuple-element.26), channel_id=1, source_target_pairs={{0,4},{1,5},{2,6},{3,7},{4,0},{5,1},{6,2},{7,3},{8,12},{9,13},{10,... | collective-permute-start | bytes 1474568 | tf_op jit(solution)/shard_map/ppermute | solution.py:233
  9.4 0.0 collective-permute-start.7
  9.4 1.9 %collective-permute-start.1 = (bf16[5,3,32,128]{3,2,1,0:T(8,128)(2,1)S(1)}, bf16[5,3,32,128]{3,2,1,0:T(8,128)(2,1)S(1)}, u32[]{:S(2)}, u32[]{:S(2)}) collective-permute-start(bf16[5,3,32,128]{3,2,1,0:T(8,128)(2,1)S(1)} %get-tuple-element.46), channel_id=1, source_target_pairs={{0,2},{1,3},{2,0},{3,1},{4,6},{5,7},{6,4},{7,5},{8,10},{9,11},{10,... | collective-permute-start | bytes 368648 | tf_op jit(solution)/shard_map/ppermute | solution.py:233
  11.3 0.0 collective-permute-done.2
  11.3 2.0 %collective-permute-done.3 = bf16[5,3,32,128]{3,2,1,0:T(8,128)(2,1)S(1)} collective-permute-done((bf16[5,3,32,128]{3,2,1,0:T(8,128)(2,1)S(1)}, bf16[5,3,32,128]{3,2,1,0:T(8,128)(2,1)S(1)}, u32[]{:S(2)}, u32[]{:S(2)}) %collective-permute-start.3) | collective-permute-done | bytes 122912 | tf_op jit(solution)/shard_map/ppermute | solution.py:233
  13.3 1.5 %collective-permute-done.1 = bf16[5,3,32,128]{3,2,1,0:T(8,128)(2,1)S(1)} collective-permute-done((bf16[5,3,32,128]{3,2,1,0:T(8,128)(2,1)S(1)}, bf16[5,3,32,128]{3,2,1,0:T(8,128)(2,1)S(1)}, u32[]{:S(2)}, u32[]{:S(2)}) %collective-permute-start.1) | collective-permute-done | bytes 122912 | tf_op jit(solution)/shard_map/ppermute | solution.py:233
  14.8 2.7 %collective-permute-start.4 = (bf16[2,5,3,32,128]{4,3,2,1,0:T(8,128)(2,1)S(1)}, bf16[2,5,3,32,128]{4,3,2,1,0:T(8,128)(2,1)S(1)}, u32[]{:S(2)}, u32[]{:S(2)}) collective-permute-start(bf16[2,5,3,32,128]{4,3,2,1,0:T(8,128)(2,1)S(1)} %pad_maximum_fusion.refs_4_.refs_0_), channel_id=1, source_target_pairs={{0,8},{1,9},{2,10},{3,11},{4,12},{5,13},{6,14},{7,15},{8,0},{9,1},... | collective-permute-start | bytes 737288 | tf_op jit(solution)/shard_map/ppermute | solution.py:233
  17.5 0.3 collective-permute-start.5
  17.8 1.4 %collective-permute-start = (bf16[3,128,640]{2,1,0:T(8,128)(2,1)S(1)}, bf16[3,128,640]{2,1,0:T(8,128)(2,1)S(1)}, u32[]{:S(2)}, u32[]{:S(2)}) collective-permute-start(bf16[3,128,640]{2,1,0:T(8,128)(2,1)S(1)} %get-tuple-element.23), channel_id=1, source_target_pairs={{0,2},{1,3},{2,0},{3,1},{4,6},{5,7},{6,4},{7,5},{8,10},{9,11},{10,... | collective-permute-start | bytes 1474568 | tf_op jit(solution)/shard_map/ppermute | solution.py:233
  19.2 18.6 %collective-permute-done.4.refs_8_.refs_4_ = bf16[2,5,3,32,128]{4,3,2,1,0:T(8,128)(2,1)S(1)} collective-permute-done((bf16[2,5,3,32,128]{4,3,2,1,0:T(8,128)(2,1)S(1)}, bf16[2,5,3,32,128]{4,3,2,1,0:T(8,128)(2,1)S(1)}, u32[]{:S(2)}, u32[]{:S(2)}) %collective-permute-start.4) | collective-permute-done | bytes 245792 | tf_op jit(solution)/shard_map/ppermute | solution.py:233
  37.8 0.0 collective-permute-start.8
  37.8 4.1 %collective-permute-done.5.refs_9_.refs_5_ = bf16[2,5,3,32,128]{4,3,2,1,0:T(8,128)(2,1)S(1)} collective-permute-done((bf16[2,5,3,32,128]{4,3,2,1,0:T(8,128)(2,1)S(1)}, bf16[2,5,3,32,128]{4,3,2,1,0:T(8,128)(2,1)S(1)}, u32[]{:S(2)}, u32[]{:S(2)}) %collective-permute-start.5) | collective-permute-done | bytes 245792 | tf_op jit(solution)/shard_map/ppermute | solution.py:233
  41.9 0.0 collective-permute-start.9
  41.9 0.0 collective-permute-done.6.refs_2_
  41.9 1.8 %collective-permute-done.7.refs_3_ = bf16[3,128,640]{2,1,0:T(8,128)(2,1)S(1)} collective-permute-done((bf16[3,128,640]{2,1,0:T(8,128)(2,1)S(1)}, bf16[3,128,640]{2,1,0:T(8,128)(2,1)S(1)}, u32[]{:S(2)}, u32[]{:S(2)}) %collective-permute-start.7) | collective-permute-done | bytes 491552 | tf_op jit(solution)/shard_map/ppermute | solution.py:233
  43.8 0.0 collective-permute-start.10
  43.8 0.5 collective-permute-start.11
  44.3 0.0 collective-permute-done.8.refs_6_.refs_2_
  44.3 0.0 collective-permute-done.9.refs_7_.refs_3_
  44.3 0.0 collective-permute-done.refs_1_
  44.3 1.0 collective-permute-done.10.refs_10_.refs_6_
  45.3 0.4 collective-permute-done.11.refs_11_.refs_7_
  45.6 7.8 %key_side.1 = (f32[2,4,512,128]{3,2,1,0:T(8,128)S(1)}, bf16[4,512,128]{2,1,0:T(8,128)(2,1)S(1)}, bf16[4,512,128]{2,1,0:T(8,128)(2,1)S(1)}) custom-call(s32[2]{0:T(128)S(1)} %pad_add_fusion.where_ref, bf16[3,128,640]{2,1,0:T(8,128)(2,1)S(1)} %get-tuple-element.22.refs_0_, bf16[3,128,640]{2,1,0:T(8,128)(2,1)S(1)} %collective-permute-done.refs_1_, ...), custom_call_target="tpu_custom_call" | custom-call | flops 2000000000 | bytes 4000000 | tf_op jit(solution)/shard_map/key_side/pallas_call | solution.py:272
  53.4 0.2 collective-permute-start.13
  53.6 1.7 %collective-permute-done.13 = bf16[4,512,128]{2,1,0:T(8,128)(2,1)S(1)} collective-permute-done((bf16[4,512,128]{2,1,0:T(8,128)(2,1)S(1)}, bf16[4,512,128]{2,1,0:T(8,128)(2,1)S(1)}, u32[]{:S(2)}, u32[]{:S(2)}) %collective-permute-start.13) | collective-permute-done | bytes 524320 | tf_op jit(solution)/shard_map/ppermute | solution.py:233
  55.4 0.1 fusion
  55.5 2.0 %collective-permute-start.14 = (bf16[4,512,128]{2,1,0:T(8,128)(2,1)S(1)}, bf16[4,512,128]{2,1,0:T(8,128)(2,1)S(1)}, u32[]{:S(2)}, u32[]{:S(2)}) collective-permute-start(bf16[4,512,128]{2,1,0:T(8,128)(2,1)S(1)} %fusion), channel_id=1, source_target_pairs={{0,8},{1,9},{2,10},{3,11},{4,12},{5,13},{6,14},{7,15},{8,0},{9,1},... | collective-permute-start | bytes 1572872 | tf_op jit(solution)/shard_map/ppermute | solution.py:233
  57.5 0.0 collective-permute-start.17
  57.5 4.1 %query_side.1 = (bf16[128,640]{1,0:T(8,128)(2,1)S(1)}, bf16[128,640]{1,0:T(8,128)(2,1)S(1)}, bf16[128,640]{1,0:T(8,128)(2,1)S(1)}, bf16[128,640]{1,0:T(8,128)(2,1)S(1)}) custom-call(bf16[3,128,640]{2,1,0:T(8,128)(2,1)S(1)} %get-tuple-element.22.refs_0_, bf16[3,128,640]{2,1,0:T(8,128)(2,1)S(1)} %collective-permute-done.refs_1_, ...), custom_call_target="tpu_custom_call" | custom-call | flops 1000000000 | bytes 4000000 | tf_op jit(solution)/shard_map/query_side/pallas_call | solution.py:295
  61.6 2.3 %collective-permute-start.15 = (bf16[128,640]{1,0:T(8,128)(2,1)S(1)}, bf16[128,640]{1,0:T(8,128)(2,1)S(1)}, u32[]{:S(2)}, u32[]{:S(2)}) collective-permute-start(bf16[128,640]{1,0:T(8,128)(2,1)S(1)} %get-tuple-element.36), channel_id=1, source_target_pairs={{0,4},{1,5},{2,6},{3,7},{4,0},{5,1},{6,2},{7,3},{8,12},{9,13},{10,... | collective-permute-start | bytes 491528 | tf_op jit(solution)/shard_map/ppermute | solution.py:233
  63.9 0.7 collective-permute-start.16
  64.6 8.7 %collective-permute-done.15.refs_2_ = bf16[128,640]{1,0:T(8,128)(2,1)S(1)} collective-permute-done((bf16[128,640]{1,0:T(8,128)(2,1)S(1)}, bf16[128,640]{1,0:T(8,128)(2,1)S(1)}, u32[]{:S(2)}, u32[]{:S(2)}) %collective-permute-start.15) | collective-permute-done | bytes 163872 | tf_op jit(solution)/shard_map/ppermute | solution.py:233
  73.3 2.7 %collective-permute-done.16.refs_3_ = bf16[128,640]{1,0:T(8,128)(2,1)S(1)} collective-permute-done((bf16[128,640]{1,0:T(8,128)(2,1)S(1)}, bf16[128,640]{1,0:T(8,128)(2,1)S(1)}, u32[]{:S(2)}, u32[]{:S(2)}) %collective-permute-start.16) | collective-permute-done | bytes 163872 | tf_op jit(solution)/shard_map/ppermute | solution.py:233
  76.1 5.7 %collective-permute-done.14.far_ref = bf16[4,512,128]{2,1,0:T(8,128)(2,1)S(1)} collective-permute-done((bf16[4,512,128]{2,1,0:T(8,128)(2,1)S(1)}, bf16[4,512,128]{2,1,0:T(8,128)(2,1)S(1)}, u32[]{:S(2)}, u32[]{:S(2)}) %collective-permute-start.14) | collective-permute-done | bytes 524320 | tf_op jit(solution)/shard_map/ppermute | solution.py:233
  81.8 0.0 collective-permute-done.17.near_ref
  81.8 3.7 %renew.1 = bf16[16,4,32,128]{3,2,1,0:T(8,128)(2,1)} custom-call(s32[2]{0:T(128)S(1)} %pad_add_fusion.where_ref, f32[2,4,512,128]{3,2,1,0:T(8,128)S(1)} %get-tuple-element.34.mine_ref, bf16[4,512,128]{2,1,0:T(8,128)(2,1)S(1)} %collective-permute-done.17.near_ref, bf16[4,512,128]{2,1,0:T(8,128)(2,1)S(1)} %collective-permute-done.14.far_ref, ...), custom_call_target="tpu_custom_call" | custom-call | flops 2000000000 | bytes 4000000 | tf_op jit(solution)/shard_map/renew/pallas_call | solution.py:318
  85.5 5.8 %all-to-all-start = ((bf16[16,4,32,128]{3,2,1,0:T(8,128)(2,1)}), bf16[16,4,32,128]{3,2,1,0:T(8,128)(2,1)S(1)}, u32[]{:S(2)}, u32[]{:S(2)}) async-start(bf16[16,4,32,128]{3,2,1,0:T(8,128)(2,1)} %renew.1), calls=%async_computation | async-start | bytes 1048576 | tf_op jit(solution)/shard_map/all_to_all | solution.py:328
  91.3 1.9 %collective-permute-start.12 = (bf16[128,640]{1,0:T(8,128)(2,1)S(1)}, bf16[128,640]{1,0:T(8,128)(2,1)S(1)}, u32[]{:S(2)}, u32[]{:S(2)}) collective-permute-start(bf16[128,640]{1,0:T(8,128)(2,1)S(1)} %get-tuple-element.33), channel_id=1, source_target_pairs={{0,2},{1,3},{2,0},{3,1},{4,6},{5,7},{6,4},{7,5},{8,10},{9,11},{10,... | collective-permute-start | bytes 491528 | tf_op jit(solution)/shard_map/ppermute | solution.py:233
  93.3 9.0 %collective-permute-done.12.refs_1_ = bf16[128,640]{1,0:T(8,128)(2,1)S(1)} collective-permute-done((bf16[128,640]{1,0:T(8,128)(2,1)S(1)}, bf16[128,640]{1,0:T(8,128)(2,1)S(1)}, u32[]{:S(2)}, u32[]{:S(2)}) %collective-permute-start.12) | collective-permute-done | bytes 163872 | tf_op jit(solution)/shard_map/ppermute | solution.py:233
  102.3 1.4 %join.1 = bf16[128,2560]{1,0:T(8,128)(2,1)} custom-call(s32[2]{0:T(128)S(1)} %pad_add_fusion.where_ref, bf16[128,640]{1,0:T(8,128)(2,1)S(1)} %get-tuple-element.32.refs_0_, bf16[128,640]{1,0:T(8,128)(2,1)S(1)} %collective-permute-done.12.refs_1_, bf16[128,640]{1,0:T(8,128)(2,1)S(1)} %collective-permute-done.15.refs_2_, ...), custom_call_target="tpu_custom_call" | custom-call | flops 10000000 | bytes 4000000 | tf_op jit(solution)/shard_map/join/pallas_call | solution.py:308
  103.7 2.1 %all-to-all-done = bf16[16,4,32,128]{3,2,1,0:T(8,128)(2,1)S(1)} async-done(((bf16[16,4,32,128]{3,2,1,0:T(8,128)(2,1)}), bf16[16,4,32,128]{3,2,1,0:T(8,128)(2,1)S(1)}, u32[]{:S(2)}, u32[]{:S(2)}) %all-to-all-start) | async-done | bytes 524320 | tf_op jit(solution)/shard_map/all_to_all | solution.py:328
  105.9 0.8 copy.12
  (4 shorter events, 0.1 us)
Async XLA Ops:
  0.6 5.9 %copy-start.3 = (f32[128,20]{0,1:T(8,128)S(1)}, f32[128,20]{0,1:T(8,128)}, u32[]{:S(2)}) copy-start(f32[128,20]{0,1:T(8,128)} %param.8) | copy-start | bytes 30724
  0.6 6.0 %copy-start.2 = (bf16[128,2560]{1,0:T(8,128)(2,1)S(1)}, bf16[128,2560]{1,0:T(8,128)(2,1)}, u32[]{:S(2)}) copy-start(bf16[128,2560]{1,0:T(8,128)(2,1)} %v_ref.1) | copy-start | bytes 1966084
  0.7 6.0 %copy-start.1 = (bf16[128,2560]{1,0:T(8,128)(2,1)S(1)}, bf16[128,2560]{1,0:T(8,128)(2,1)}, u32[]{:S(2)}) copy-start(bf16[128,2560]{1,0:T(8,128)(2,1)} %k_ref.1) | copy-start | bytes 1966084
  0.7 6.0 %copy-start = (bf16[128,2560]{1,0:T(8,128)(2,1)S(1)}, bf16[128,2560]{1,0:T(8,128)(2,1)}, u32[]{:S(2)}) copy-start(bf16[128,2560]{1,0:T(8,128)(2,1)} %q_ref.1) | copy-start | bytes 1966084
  2.0 9.3 %collective-permute-start.2 = (bf16[5,3,32,128]{3,2,1,0:T(8,128)(2,1)S(1)}, bf16[5,3,32,128]{3,2,1,0:T(8,128)(2,1)S(1)}, u32[]{:S(2)}, u32[]{:S(2)}) collective-permute-start(bf16[5,3,32,128]{3,2,1,0:T(8,128)(2,1)S(1)} %get-tuple-element.44), channel_id=1, source_target_pairs={{0,4},{1,5},{2,6},{3,7},{4,0},{5,1},{6,2},{7,3},{8,12},{9,13},{10,... | collective-permute-start | bytes 368648 | tf_op jit(solution)/shard_map/ppermute | solution.py:233
  5.1 8.2 %collective-permute-start.3 = (bf16[5,3,32,128]{3,2,1,0:T(8,128)(2,1)S(1)}, bf16[5,3,32,128]{3,2,1,0:T(8,128)(2,1)S(1)}, u32[]{:S(2)}, u32[]{:S(2)}) collective-permute-start(bf16[5,3,32,128]{3,2,1,0:T(8,128)(2,1)S(1)} %get-tuple-element.45), channel_id=1, source_target_pairs={{0,6},{1,7},{2,4},{3,5},{4,2},{5,3},{6,0},{7,1},{8,14},{9,15},{10,... | collective-permute-start | bytes 368648 | tf_op jit(solution)/shard_map/ppermute | solution.py:233
  7.8 34.2 %collective-permute-start.6 = (bf16[3,128,640]{2,1,0:T(8,128)(2,1)S(1)}, bf16[3,128,640]{2,1,0:T(8,128)(2,1)S(1)}, u32[]{:S(2)}, u32[]{:S(2)}) collective-permute-start(bf16[3,128,640]{2,1,0:T(8,128)(2,1)S(1)} %get-tuple-element.26), channel_id=1, source_target_pairs={{0,4},{1,5},{2,6},{3,7},{4,0},{5,1},{6,2},{7,3},{8,12},{9,13},{10,... | collective-permute-start | bytes 1474568 | tf_op jit(solution)/shard_map/ppermute | solution.py:233
  9.4 34.3 %collective-permute-start.7 = (bf16[3,128,640]{2,1,0:T(8,128)(2,1)S(1)}, bf16[3,128,640]{2,1,0:T(8,128)(2,1)S(1)}, u32[]{:S(2)}, u32[]{:S(2)}) collective-permute-start(bf16[3,128,640]{2,1,0:T(8,128)(2,1)S(1)} %get-tuple-element.27), channel_id=1, source_target_pairs={{0,6},{1,7},{2,4},{3,5},{4,2},{5,3},{6,0},{7,1},{8,14},{9,15},{10,... | collective-permute-start | bytes 1474568 | tf_op jit(solution)/shard_map/ppermute | solution.py:233
  9.4 5.4 %collective-permute-start.1 = (bf16[5,3,32,128]{3,2,1,0:T(8,128)(2,1)S(1)}, bf16[5,3,32,128]{3,2,1,0:T(8,128)(2,1)S(1)}, u32[]{:S(2)}, u32[]{:S(2)}) collective-permute-start(bf16[5,3,32,128]{3,2,1,0:T(8,128)(2,1)S(1)} %get-tuple-element.46), channel_id=1, source_target_pairs={{0,2},{1,3},{2,0},{3,1},{4,6},{5,7},{6,4},{7,5},{8,10},{9,11},{10,... | collective-permute-start | bytes 368648 | tf_op jit(solution)/shard_map/ppermute | solution.py:233
  14.8 23.0 %collective-permute-start.4 = (bf16[2,5,3,32,128]{4,3,2,1,0:T(8,128)(2,1)S(1)}, bf16[2,5,3,32,128]{4,3,2,1,0:T(8,128)(2,1)S(1)}, u32[]{:S(2)}, u32[]{:S(2)}) collective-permute-start(bf16[2,5,3,32,128]{4,3,2,1,0:T(8,128)(2,1)S(1)} %pad_maximum_fusion.refs_4_.refs_0_), channel_id=1, source_target_pairs={{0,8},{1,9},{2,10},{3,11},{4,12},{5,13},{6,14},{7,15},{8,0},{9,1},... | collective-permute-start | bytes 737288 | tf_op jit(solution)/shard_map/ppermute | solution.py:233
  17.5 24.4 %collective-permute-start.5 = (bf16[2,5,3,32,128]{4,3,2,1,0:T(8,128)(2,1)S(1)}, bf16[2,5,3,32,128]{4,3,2,1,0:T(8,128)(2,1)S(1)}, u32[]{:S(2)}, u32[]{:S(2)}) collective-permute-start(bf16[2,5,3,32,128]{4,3,2,1,0:T(8,128)(2,1)S(1)} %pad_maximum_fusion.1.refs_5_.refs_1_), channel_id=1, source_target_pairs={{0,8},{1,9},{2,10},{3,11},{4,12},{5,13},{6,14},{7,15},{8,0},{9,1},... | collective-permute-start | bytes 737288 | tf_op jit(solution)/shard_map/ppermute | solution.py:233
  17.8 26.5 %collective-permute-start = (bf16[3,128,640]{2,1,0:T(8,128)(2,1)S(1)}, bf16[3,128,640]{2,1,0:T(8,128)(2,1)S(1)}, u32[]{:S(2)}, u32[]{:S(2)}) collective-permute-start(bf16[3,128,640]{2,1,0:T(8,128)(2,1)S(1)} %get-tuple-element.23), channel_id=1, source_target_pairs={{0,2},{1,3},{2,0},{3,1},{4,6},{5,7},{6,4},{7,5},{8,10},{9,11},{10,... | collective-permute-start | bytes 1474568 | tf_op jit(solution)/shard_map/ppermute | solution.py:233
  37.8 6.5 %collective-permute-start.8 = (bf16[2,5,3,32,128]{4,3,2,1,0:T(8,128)(2,1)S(1)}, bf16[2,5,3,32,128]{4,3,2,1,0:T(8,128)(2,1)S(1)}, u32[]{:S(2)}, u32[]{:S(2)}) collective-permute-start(bf16[2,5,3,32,128]{4,3,2,1,0:T(8,128)(2,1)S(1)} %pad_maximum_fusion.refs_4_.refs_0_), channel_id=1, source_target_pairs={{0,1},{1,0},{2,3},{3,2},{4,5},{5,4},{6,7},{7,6},{8,9},{9,8},{10,11... | collective-permute-start | bytes 737288 | tf_op jit(solution)/shard_map/ppermute | solution.py:233
  41.9 2.3 %collective-permute-start.9 = (bf16[2,5,3,32,128]{4,3,2,1,0:T(8,128)(2,1)S(1)}, bf16[2,5,3,32,128]{4,3,2,1,0:T(8,128)(2,1)S(1)}, u32[]{:S(2)}, u32[]{:S(2)}) collective-permute-start(bf16[2,5,3,32,128]{4,3,2,1,0:T(8,128)(2,1)S(1)} %pad_maximum_fusion.1.refs_5_.refs_1_), channel_id=1, source_target_pairs={{0,1},{1,0},{2,3},{3,2},{4,5},{5,4},{6,7},{7,6},{8,9},{9,8},{10,11... | collective-permute-start | bytes 737288 | tf_op jit(solution)/shard_map/ppermute | solution.py:233
  43.8 1.5 %collective-permute-start.10 = (bf16[2,5,3,32,128]{4,3,2,1,0:T(8,128)(2,1)S(1)}, bf16[2,5,3,32,128]{4,3,2,1,0:T(8,128)(2,1)S(1)}, u32[]{:S(2)}, u32[]{:S(2)}) collective-permute-start(bf16[2,5,3,32,128]{4,3,2,1,0:T(8,128)(2,1)S(1)} %collective-permute-done.4.refs_8_.refs_4_), channel_id=1, source_target_pairs={{0,1},{1,0},{2,3},{3,2},{4,5},{5,4},{6,7},{7,6},{8,9},{9,8},{10,11... | collective-permute-start | bytes 737288 | tf_op jit(solution)/shard_map/ppermute | solution.py:233
  43.8 1.9 %collective-permute-start.11 = (bf16[2,5,3,32,128]{4,3,2,1,0:T(8,128)(2,1)S(1)}, bf16[2,5,3,32,128]{4,3,2,1,0:T(8,128)(2,1)S(1)}, u32[]{:S(2)}, u32[]{:S(2)}) collective-permute-start(bf16[2,5,3,32,128]{4,3,2,1,0:T(8,128)(2,1)S(1)} %collective-permute-done.5.refs_9_.refs_5_), channel_id=1, source_target_pairs={{0,1},{1,0},{2,3},{3,2},{4,5},{5,4},{6,7},{7,6},{8,9},{9,8},{10,11... | collective-permute-start | bytes 737288 | tf_op jit(solution)/shard_map/ppermute | solution.py:233
  53.4 2.0 %collective-permute-start.13 = (bf16[4,512,128]{2,1,0:T(8,128)(2,1)S(1)}, bf16[4,512,128]{2,1,0:T(8,128)(2,1)S(1)}, u32[]{:S(2)}, u32[]{:S(2)}) collective-permute-start(bf16[4,512,128]{2,1,0:T(8,128)(2,1)S(1)} %get-tuple-element.35), channel_id=1, source_target_pairs={{0,1},{1,0},{2,3},{3,2},{4,5},{5,4},{6,7},{7,6},{8,9},{9,8},{10,11... | collective-permute-start | bytes 1572872 | tf_op jit(solution)/shard_map/ppermute | solution.py:233
  55.5 26.3 %collective-permute-start.14 = (bf16[4,512,128]{2,1,0:T(8,128)(2,1)S(1)}, bf16[4,512,128]{2,1,0:T(8,128)(2,1)S(1)}, u32[]{:S(2)}, u32[]{:S(2)}) collective-permute-start(bf16[4,512,128]{2,1,0:T(8,128)(2,1)S(1)} %fusion), channel_id=1, source_target_pairs={{0,8},{1,9},{2,10},{3,11},{4,12},{5,13},{6,14},{7,15},{8,0},{9,1},... | collective-permute-start | bytes 1572872 | tf_op jit(solution)/shard_map/ppermute | solution.py:233
  57.5 24.3 %collective-permute-start.17 = (bf16[4,512,128]{2,1,0:T(8,128)(2,1)S(1)}, bf16[4,512,128]{2,1,0:T(8,128)(2,1)S(1)}, u32[]{:S(2)}, u32[]{:S(2)}) collective-permute-start(bf16[4,512,128]{2,1,0:T(8,128)(2,1)S(1)} %get-tuple-element.40), channel_id=1, source_target_pairs={{0,1},{1,0},{2,3},{3,2},{4,5},{5,4},{6,7},{7,6},{8,9},{9,8},{10,11... | collective-permute-start | bytes 1572872 | tf_op jit(solution)/shard_map/ppermute | solution.py:233
  61.6 11.8 %collective-permute-start.15 = (bf16[128,640]{1,0:T(8,128)(2,1)S(1)}, bf16[128,640]{1,0:T(8,128)(2,1)S(1)}, u32[]{:S(2)}, u32[]{:S(2)}) collective-permute-start(bf16[128,640]{1,0:T(8,128)(2,1)S(1)} %get-tuple-element.36), channel_id=1, source_target_pairs={{0,4},{1,5},{2,6},{3,7},{4,0},{5,1},{6,2},{7,3},{8,12},{9,13},{10,... | collective-permute-start | bytes 491528 | tf_op jit(solution)/shard_map/ppermute | solution.py:233
  63.9 12.2 %collective-permute-start.16 = (bf16[128,640]{1,0:T(8,128)(2,1)S(1)}, bf16[128,640]{1,0:T(8,128)(2,1)S(1)}, u32[]{:S(2)}, u32[]{:S(2)}) collective-permute-start(bf16[128,640]{1,0:T(8,128)(2,1)S(1)} %get-tuple-element.37), channel_id=1, source_target_pairs={{0,6},{1,7},{2,4},{3,5},{4,2},{5,3},{6,0},{7,1},{8,14},{9,15},{10,... | collective-permute-start | bytes 491528 | tf_op jit(solution)/shard_map/ppermute | solution.py:233
  85.5 20.3 %all-to-all-start = ((bf16[16,4,32,128]{3,2,1,0:T(8,128)(2,1)}), bf16[16,4,32,128]{3,2,1,0:T(8,128)(2,1)S(1)}, u32[]{:S(2)}, u32[]{:S(2)}) async-start(bf16[16,4,32,128]{3,2,1,0:T(8,128)(2,1)} %renew.1), calls=%async_computation | async-start | bytes 1048576 | tf_op jit(solution)/shard_map/all_to_all | solution.py:328
  91.3 10.9 %collective-permute-start.12 = (bf16[128,640]{1,0:T(8,128)(2,1)S(1)}, bf16[128,640]{1,0:T(8,128)(2,1)S(1)}, u32[]{:S(2)}, u32[]{:S(2)}) collective-permute-start(bf16[128,640]{1,0:T(8,128)(2,1)S(1)} %get-tuple-element.33), channel_id=1, source_target_pairs={{0,2},{1,3},{2,0},{3,1},{4,6},{5,7},{6,4},{7,5},{8,10},{9,11},{10,... | collective-permute-start | bytes 491528 | tf_op jit(solution)/shard_map/ppermute | solution.py:233

commit v5 on v4

--- a/solution.py
+++ b/solution.py
@@ -30,6 +30,7 @@
 def split_kernel(where_ref, q_ref, k_ref, v_ref, rate_ref, *refs):
     outs, scaled = refs[:-1], refs[-1]
     spot = where_ref[0]
+    squares = len(outs) // 2
     width = outs[0].shape[2]
     num_heads = rate_ref.shape[1]
     head_size = k_ref.shape[1] // num_heads
@@ -39,11 +40,11 @@
         scaled[:, at] = (rates[:, head : head + 1] * v_ref[:, at].astype(jnp.float32)).astype(
             jnp.bfloat16
         )
-    for rel, out_ref in enumerate(outs):
+    for rel in range(squares):
         at = pl.multiple_of((spot ^ rel) * width, width)
-        out_ref[0] = k_ref[:, pl.ds(at, width)]
-        out_ref[1] = scaled[:, pl.ds(at, width)]
-        out_ref[2] = q_ref[:, pl.ds(at, width)]
+        outs[rel][0] = k_ref[:, pl.ds(at, width)]
+        outs[rel][1] = scaled[:, pl.ds(at, width)]
+        outs[squares + rel][...] = q_ref[:, pl.ds(at, width)]
 
 
 def join_kernel(where_ref, *refs):
@@ -64,7 +65,7 @@
 
 def key_kernel(squares, heads, where_ref, *refs):
     pairs, w_refs = refs[:squares], refs[squares : squares + 8]
-    keep_ref, near_ref, far_ref, terms = refs[squares + 8 :]
+    keep_ref, near_ref, *far_refs, terms = refs[squares + 8 :]
     spot, place = where_ref[0], where_ref[1]
     _, hid, head_size = terms.shape
     rows = hid // (PLACES * squares)
@@ -83,9 +84,11 @@
         def _():
             near_ref[slot] = value.astype(near_ref.dtype)
 
-        @pl.when(rel == 3)
-        def _():
-            far_ref[slot] = value.astype(far_ref.dtype)
+        for one, far_ref in enumerate(far_refs):
+
+            @pl.when((rel == 3) & (slot == one))
+            def _():
+                far_ref[...] = value.astype(far_ref.dtype)
 
     @pl.when(step == 0)
     def _():
@@ -126,13 +129,13 @@
 
 def query_kernel(squares, *refs):
     ins, w_refs, outs = refs[:squares], refs[squares : squares + 8], refs[-squares:]
-    scale_in = 1.0 / math.sqrt(ins[0].shape[2])
+    scale_in = 1.0 / math.sqrt(ins[0].shape[1])
     scale_out = 1.0 / math.sqrt(HID)
     first_map, third_map, second = (
         jnp.concatenate([weight_rows(w_refs, rel, matrix) for rel in range(PLACES)], axis=0)
         for matrix in range(3)
     )
-    queries = jnp.concatenate([q_ref[0] for q_ref in ins], axis=0)
+    queries = jnp.concatenate([q_ref[...] for q_ref in ins], axis=0)
     half_first = dot(queries, first_map, NT) * (0.5 * scale_in)
     third = dot(queries, third_map, NT) * scale_in
     hidden = ((half_first + half_first * jnp.tanh(half_first)) * third).astype(jnp.bfloat16)
@@ -238,18 +241,17 @@
     def bf16(*shape):
         return jax.ShapeDtypeStruct(shape, jnp.bfloat16)
 
-    moved = across(
-        pl.pallas_call(
-            split_kernel,
-            in_specs=[smem] + [vmem] * 4,
-            out_specs=[vmem] * squares,
-            out_shape=[bf16(3, row_count, width)] * squares,
-            scratch_shapes=[VMEM((row_count, num_heads * head_size), jnp.bfloat16)],
-            compiler_params=params,
-            cost_estimate=cost(10),
-            name="split",
-        )(where, queries, key_vectors, value_vectors, token_rates)
-    )
+    pieces = pl.pallas_call(
+        split_kernel,
+        in_specs=[smem] + [vmem] * 4,
+        out_specs=[vmem] * (2 * squares),
+        out_shape=[bf16(2, row_count, width)] * squares + [bf16(row_count, width)] * squares,
+        scratch_shapes=[VMEM((row_count, num_heads * head_size), jnp.bfloat16)],
+        compiler_params=params,
+        cost_estimate=cost(10),
+        name="split",
+    )(where, queries, key_vectors, value_vectors, token_rates)
+    moved, asking = across(pieces[:squares]), pieces[squares:]
 
     by_spot = fast_weights.reshape(own_rows, 3, squares, heads, head_size).transpose(2, 3, 1, 0, 4)
     pieces = across(
@@ -262,6 +264,8 @@
     own = list(lax.optimization_barrier(own))
     other = [swap(w, half) for w in own]
     late, moved[2:] = lax.optimization_barrier((other, moved[2:]))
+    other, asking = lax.optimization_barrier((other, asking))
+    asking = across(asking)
     weights = [own, [swap(w, 1) for w in own], other, [swap(w, 1) for w in late]]
     weights = [w for pair in weights for w in pair]
 
@@ -269,18 +273,19 @@
 
     slots = -(-3 * heads // PLACES)
     sums_shape = (slots, hid, head_size)
-    keep, near, far = pl.pallas_call(
+    keep, near, *far = pl.pallas_call(
         functools.partial(key_kernel, squares, heads),
         grid=(heads,),
         in_specs=[smem]
         + [pl.BlockSpec((2, row_count, head_size), lambda h: (0, 0, h))] * squares
         + [weight_spec] * 8,
         out_specs=[pl.BlockSpec((2, *sums_shape), lambda h: (0, 0, 0, 0))]
-        + [pl.BlockSpec(sums_shape, lambda h: (0, 0, 0))] * 2,
+        + [pl.BlockSpec(sums_shape, lambda h: (0, 0, 0))]
+        + [pl.BlockSpec(sums_shape[1:], lambda h: (0, 0))] * slots,
         out_shape=[
             jax.ShapeDtypeStruct((2, *sums_shape), jnp.float32),
             bf16(*sums_shape),
-            bf16(*sums_shape),
+            *[bf16(*sums_shape[1:])] * slots,
         ],
         scratch_shapes=[VMEM((3, hid, head_size), jnp.float32)],
         compiler_params=params,
@@ -289,20 +294,23 @@
     )(where, *moved, *weights)
 
     near = swap(near, 1)
-    far = swap((keep[1] + swap(far, 1).astype(jnp.float32)).astype(jnp.bfloat16), half)
+    far = [swap(one, 1) for one in far]
+    far, asking = lax.optimization_barrier((far, asking))
+    far = jnp.stack(far).astype(jnp.float32)
+    far = swap((keep[1] + far).astype(jnp.bfloat16), half)
 
     columns = pl.BlockSpec((row_count, head_size), lambda h: (0, h))
     parts = pl.pallas_call(
         functools.partial(query_kernel, squares),
         grid=(heads,),
-        in_specs=[pl.BlockSpec((1, row_count, head_size), lambda h: (2, 0, h))] * squares
+        in_specs=[columns] * squares
         + [weight_spec] * 8,
         out_specs=[columns] * squares,
         out_shape=[bf16(row_count, width)] * squares,
         compiler_params=params,
         cost_estimate=cost(1000),
         name="query_side",
-    )(*moved, *weights)
+    )(*asking, *weights)
     parts = across(parts)
     far, parts[2:] = lax.optimization_barrier((far, parts[2:]))
     applied = pl.pallas_call(

time: 107 us -> 102 us (0.953)
  waiting for transfers between devices: 59.3 us -> 51.7 us
  starting transfers between devices: 26 us -> 28.6 us
    ppermute x18 -> x24, waiting for transfers between devices: 57.2 us -> 49.6 us  [swap(): return lax.ppermute(array, 'seq', [(at, at ^ step) for at in range(size)])]
    ppermute x18 -> x24, starting transfers between devices: 20.2 us -> 23.3 us  [swap(): return lax.ppermute(array, 'seq', [(at, at ^ step) for at in range(size)])]
  transfers between devices with their start and end apart: 19 -> 25, of which waited for: 13 -> 13; matrix products, arithmetic and copies ran while one was open for 0% -> 0% of each run, Pallas kernels for 6% -> 14%
where the time goes in v5:
time: 102 us
  waiting for transfers between devices  51.7 us (51%)
  starting transfers between devices  28.6 us (28%)
  Pallas kernels  18.3 us (18%)
  local copies, waits for them, and re-layouts  2.28 us (2%)
    ppermute x24, waiting for transfers between devices, swap(): return lax.ppermute(array, 'seq', [(at, at ^ step) for at in range(size)])  49.6 us
    ppermute x24, starting transfers between devices, swap(): return lax.ppermute(array, 'seq', [(at, at ^ step) for at in range(size)])  23.3 us
    pallas_call x1, Pallas kernels, square_body(): pl.pallas_call(functools.partial(key_kernel, squares, heads), grid=(heads...  8.07 us
    all_to_all x1, starting transfers between devices, square_body(): back = lax.all_to_all(renewed, 'seq', 0, 0, tiled=True)  5.31 us
    pallas_call x1, Pallas kernels, square_body(): pl.pallas_call(functools.partial(query_kernel, squares), grid=(heads,), i...  4.06 us
    pallas_call x1, Pallas kernels, square_body(): pl.pallas_call(functools.partial(renew_kernel, squares), in_specs=[smem]...  3.67 us
    unnamed x11, local copies, waits for them, and re-layouts  2.13 us
    all_to_all x1, waiting for transfers between devices, square_body(): back = lax.all_to_all(renewed, 'seq', 0, 0, tiled=True)  2.12 us
  transfers between devices with their start and end apart: 25, of which 13 were waited for; matrix products, arithmetic and copies ran while one was open for 0% of the time, Pallas kernels for 14%

profile of v5, /device:TPU:0, one launch (start us, length us, event | category | flops | bytes accessed | tf_op | source)
XLA Modules:
  0.0 102.0 jit_solution(7974384783305233836)
XLA Ops:
  0.6 0.0 copy-start.3
  0.6 0.0 copy-start.2
  0.7 1.2 %copy.10 = bf16[32,3,20,128]{3,0,1,2:T(8,128)(2,1)S(1)} copy(bf16[32,3,20,128]{3,0,2,1:T(8,128)(2,1)} %param.9) | data formatting | bytes 983040 | tf_op args[4]
  1.9 0.1 dynamic-slice_bitcast_fusion.1
  2.0 3.1 %collective-permute-start.2 = (bf16[5,3,32,128]{3,2,1,0:T(8,128)(2,1)S(1)}, bf16[5,3,32,128]{3,2,1,0:T(8,128)(2,1)S(1)}, u32[]{:S(2)}, u32[]{:S(2)}) collective-permute-start(bf16[5,3,32,128]{3,2,1,0:T(8,128)(2,1)S(1)} %get-tuple-element.86), channel_id=1, source_target_pairs={{0,4},{1,5},{2,6},{3,7},{4,0},{5,1},{6,2},{7,3},{8,12},{9,13},{10,... | collective-permute-start | bytes 368648 | tf_op jit(solution)/shard_map/ppermute | solution.py:236
  5.1 1.4 %collective-permute-start.3 = (bf16[5,3,32,128]{3,2,1,0:T(8,128)(2,1)S(1)}, bf16[5,3,32,128]{3,2,1,0:T(8,128)(2,1)S(1)}, u32[]{:S(2)}, u32[]{:S(2)}) collective-permute-start(bf16[5,3,32,128]{3,2,1,0:T(8,128)(2,1)S(1)} %get-tuple-element.87), channel_id=1, source_target_pairs={{0,6},{1,7},{2,4},{3,5},{4,2},{5,3},{6,0},{7,1},{8,14},{9,15},{10,... | collective-permute-start | bytes 368648 | tf_op jit(solution)/shard_map/ppermute | solution.py:236
  6.5 0.1 collective-permute-start.1
  6.6 0.1 pad_add_fusion.where_ref
  6.7 0.1 copy.9.rate_ref
  6.8 1.1 %split.1 = (bf16[2,128,640]{2,1,0:T(8,128)(2,1)S(1)}, bf16[2,128,640]{2,1,0:T(8,128)(2,1)S(1)}, bf16[2,128,640]{2,1,0:T(8,128)(2,1)S(1)}, bf16[2,128,640]{2,1,0:...) custom-call(s32[2]{0:T(128)S(1)} %pad_add_fusion.where_ref, ...), custom_call_target="tpu_custom_call" | custom-call | flops 10000000 | bytes 4000000 | tf_op jit(solution)/shard_map/split/pallas_call | solution.py:244
  7.9 2.0 %collective-permute-start.6 = (bf16[2,128,640]{2,1,0:T(8,128)(2,1)S(1)}, bf16[2,128,640]{2,1,0:T(8,128)(2,1)S(1)}, u32[]{:S(2)}, u32[]{:S(2)}) collective-permute-start(bf16[2,128,640]{2,1,0:T(8,128)(2,1)S(1)} %get-tuple-element.47), channel_id=1, source_target_pairs={{0,4},{1,5},{2,6},{3,7},{4,0},{5,1},{6,2},{7,3},{8,12},{9,13},{10,... | collective-permute-start | bytes 983048 | tf_op jit(solution)/shard_map/ppermute | solution.py:236
  9.9 1.4 %collective-permute-start.7 = (bf16[2,128,640]{2,1,0:T(8,128)(2,1)S(1)}, bf16[2,128,640]{2,1,0:T(8,128)(2,1)S(1)}, u32[]{:S(2)}, u32[]{:S(2)}) collective-permute-start(bf16[2,128,640]{2,1,0:T(8,128)(2,1)S(1)} %get-tuple-element.48), channel_id=1, source_target_pairs={{0,6},{1,7},{2,4},{3,5},{4,2},{5,3},{6,0},{7,1},{8,14},{9,15},{10,... | collective-permute-start | bytes 983048 | tf_op jit(solution)/shard_map/ppermute | solution.py:236
  11.3 0.0 collective-permute-done.2
  11.3 2.0 %collective-permute-done.3 = bf16[5,3,32,128]{3,2,1,0:T(8,128)(2,1)S(1)} collective-permute-done((bf16[5,3,32,128]{3,2,1,0:T(8,128)(2,1)S(1)}, bf16[5,3,32,128]{3,2,1,0:T(8,128)(2,1)S(1)}, u32[]{:S(2)}, u32[]{:S(2)}) %collective-permute-start.3) | collective-permute-done | bytes 122912 | tf_op jit(solution)/shard_map/ppermute | solution.py:236
  13.3 0.3 collective-permute-done.1
  13.6 2.7 %collective-permute-start.4 = (bf16[2,5,3,32,128]{4,3,2,1,0:T(8,128)(2,1)S(1)}, bf16[2,5,3,32,128]{4,3,2,1,0:T(8,128)(2,1)S(1)}, u32[]{:S(2)}, u32[]{:S(2)}) collective-permute-start(bf16[2,5,3,32,128]{4,3,2,1,0:T(8,128)(2,1)S(1)} %pad_maximum_fusion.refs_4_.refs_0_), channel_id=1, source_target_pairs={{0,8},{1,9},{2,10},{3,11},{4,12},{5,13},{6,14},{7,15},{8,0},{9,1},... | collective-permute-start | bytes 737288 | tf_op jit(solution)/shard_map/ppermute | solution.py:236
  16.3 0.3 collective-permute-start.5
  16.6 0.4 collective-permute-start
  17.1 12.8 %collective-permute-done.6.refs_2_ = bf16[2,128,640]{2,1,0:T(8,128)(2,1)S(1)} collective-permute-done((bf16[2,128,640]{2,1,0:T(8,128)(2,1)S(1)}, bf16[2,128,640]{2,1,0:T(8,128)(2,1)S(1)}, u32[]{:S(2)}, u32[]{:S(2)}) %collective-permute-start.6) | collective-permute-done | bytes 327712 | tf_op jit(solution)/shard_map/ppermute | solution.py:236
  29.8 0.0 collective-permute-start.8
  29.8 6.9 %collective-permute-done.7.refs_3_ = bf16[2,128,640]{2,1,0:T(8,128)(2,1)S(1)} collective-permute-done((bf16[2,128,640]{2,1,0:T(8,128)(2,1)S(1)}, bf16[2,128,640]{2,1,0:T(8,128)(2,1)S(1)}, u32[]{:S(2)}, u32[]{:S(2)}) %collective-permute-start.7) | collective-permute-done | bytes 327712 | tf_op jit(solution)/shard_map/ppermute | solution.py:236
  36.7 0.0 collective-permute-start.9
  36.7 0.0 collective-permute-done.4.refs_8_.refs_4_
  36.7 0.0 collective-permute-done.5.refs_9_.refs_5_
  36.7 0.5 collective-permute-start.10
  37.2 0.1 collective-permute-start.11
  37.3 0.0 collective-permute-done.refs_1_
  37.3 0.4 collective-permute-start.16
  37.7 0.0 collective-permute-done.8.refs_6_.refs_2_
  37.7 2.7 %collective-permute-start.17 = (bf16[128,640]{1,0:T(8,128)(2,1)S(1)}, bf16[128,640]{1,0:T(8,128)(2,1)S(1)}, u32[]{:S(2)}, u32[]{:S(2)}) collective-permute-start(bf16[128,640]{1,0:T(8,128)(2,1)S(1)} %get-tuple-element.65), channel_id=1, source_target_pairs={{0,4},{1,5},{2,6},{3,7},{4,0},{5,1},{6,2},{7,3},{8,12},{9,13},{10,... | collective-permute-start | bytes 491528 | tf_op jit(solution)/shard_map/ppermute | solution.py:236
  40.4 0.0 collective-permute-done.9.refs_7_.refs_3_
  40.5 0.4 collective-permute-start.18
  40.8 0.0 collective-permute-done.10.refs_10_.refs_6_
  40.8 0.0 collective-permute-done.11.refs_11_.refs_7_
  40.8 8.1 %key_side.1 = (f32[2,4,512,128]{3,2,1,0:T(8,128)S(1)}, bf16[4,512,128]{2,1,0:T(8,128)(2,1)S(1)}, bf16[512,128]{1,0:T(8,128)(2,1)S(1)}, bf16[512,128]{1,0:T(8,128...) custom-call(s32[2]{0:T(128)S(1)} %pad_add_fusion.where_ref, ...), custom_call_target="tpu_custom_call" | custom-call | flops 2000000000 | bytes 4000000 | tf_op jit(solution)/shard_map/key_side/pallas_call | solution.py:276
  48.9 0.1 collective-permute-start.12
  49.0 0.5 collective-permute-start.13
  49.5 0.0 collective-permute-done.16.refs_1_
  49.5 0.1 collective-permute-start.14
  49.6 0.0 collective-permute-done.17.refs_2_
  49.6 0.4 collective-permute-start.15
  50.0 0.0 collective-permute-done.18.refs_3_
  50.0 0.3 collective-permute-done.12
  50.3 0.2 collective-permute-done.13
  50.5 0.3 collective-permute-done.14
  50.8 0.2 collective-permute-done.15
  51.0 0.1 fusion
  51.2 2.4 %collective-permute-start.20 = (bf16[4,512,128]{2,1,0:T(8,128)(2,1)S(1)}, bf16[4,512,128]{2,1,0:T(8,128)(2,1)S(1)}, u32[]{:S(2)}, u32[]{:S(2)}) collective-permute-start(bf16[4,512,128]{2,1,0:T(8,128)(2,1)S(1)} %fusion), channel_id=1, source_target_pairs={{0,8},{1,9},{2,10},{3,11},{4,12},{5,13},{6,14},{7,15},{8,0},{9,1},... | collective-permute-start | bytes 1572872 | tf_op jit(solution)/shard_map/ppermute | solution.py:236
  53.5 0.0 collective-permute-start.23
  53.6 4.1 %query_side.1 = (bf16[128,640]{1,0:T(8,128)(2,1)S(1)}, bf16[128,640]{1,0:T(8,128)(2,1)S(1)}, bf16[128,640]{1,0:T(8,128)(2,1)S(1)}, bf16[128,640]{1,0:T(8,128)(2,1)S(1)}) custom-call(bf16[128,640]{1,0:T(8,128)(2,1)S(1)} %get-tuple-element.67.refs_0_, bf16[128,640]{1,0:T(8,128)(2,1)S(1)} %collective-permute-done.16.refs_1_, ...), custom_call_target="tpu_custom_call" | custom-call | flops 1000000000 | bytes 4000000 | tf_op jit(solution)/shard_map/query_side/pallas_call | solution.py:303
  57.6 2.0 %collective-permute-start.21 = (bf16[128,640]{1,0:T(8,128)(2,1)S(1)}, bf16[128,640]{1,0:T(8,128)(2,1)S(1)}, u32[]{:S(2)}, u32[]{:S(2)}) collective-permute-start(bf16[128,640]{1,0:T(8,128)(2,1)S(1)} %get-tuple-element.78), channel_id=1, source_target_pairs={{0,4},{1,5},{2,6},{3,7},{4,0},{5,1},{6,2},{7,3},{8,12},{9,13},{10,... | collective-permute-start | bytes 491528 | tf_op jit(solution)/shard_map/ppermute | solution.py:236
  59.7 0.3 collective-permute-start.22
  60.0 9.3 %collective-permute-done.21.refs_2_ = bf16[128,640]{1,0:T(8,128)(2,1)S(1)} collective-permute-done((bf16[128,640]{1,0:T(8,128)(2,1)S(1)}, bf16[128,640]{1,0:T(8,128)(2,1)S(1)}, u32[]{:S(2)}, u32[]{:S(2)}) %collective-permute-start.21) | collective-permute-done | bytes 163872 | tf_op jit(solution)/shard_map/ppermute | solution.py:236
  69.3 2.9 %collective-permute-done.22.refs_3_ = bf16[128,640]{1,0:T(8,128)(2,1)S(1)} collective-permute-done((bf16[128,640]{1,0:T(8,128)(2,1)S(1)}, bf16[128,640]{1,0:T(8,128)(2,1)S(1)}, u32[]{:S(2)}, u32[]{:S(2)}) %collective-permute-start.22) | collective-permute-done | bytes 163872 | tf_op jit(solution)/shard_map/ppermute | solution.py:236
  72.3 5.4 %collective-permute-done.20.far_ref = bf16[4,512,128]{2,1,0:T(8,128)(2,1)S(1)} collective-permute-done((bf16[4,512,128]{2,1,0:T(8,128)(2,1)S(1)}, bf16[4,512,128]{2,1,0:T(8,128)(2,1)S(1)}, u32[]{:S(2)}, u32[]{:S(2)}) %collective-permute-start.20) | collective-permute-done | bytes 524320 | tf_op jit(solution)/shard_map/ppermute | solution.py:236
  77.6 0.0 collective-permute-done.23.near_ref
  77.6 3.7 %renew.1 = bf16[16,4,32,128]{3,2,1,0:T(8,128)(2,1)} custom-call(s32[2]{0:T(128)S(1)} %pad_add_fusion.where_ref, f32[2,4,512,128]{3,2,1,0:T(8,128)S(1)} %get-tuple-element.73.mine_ref, bf16[4,512,128]{2,1,0:T(8,128)(2,1)S(1)} %collective-permute-done.23.near_ref, bf16[4,512,128]{2,1,0:T(8,128)(2,1)S(1)} %collective-permute-done.20.far_ref, ...), custom_call_target="tpu_custom_call" | custom-call | flops 2000000000 | bytes 4000000 | tf_op jit(solution)/shard_map/renew/pallas_call | solution.py:326
  81.3 5.3 %all-to-all-start = ((bf16[16,4,32,128]{3,2,1,0:T(8,128)(2,1)}), bf16[16,4,32,128]{3,2,1,0:T(8,128)(2,1)S(1)}, u32[]{:S(2)}, u32[]{:S(2)}) async-start(bf16[16,4,32,128]{3,2,1,0:T(8,128)(2,1)} %renew.1), calls=%async_computation | async-start | bytes 1048576 | tf_op jit(solution)/shard_map/all_to_all | solution.py:336
  86.6 1.9 %collective-permute-start.19 = (bf16[128,640]{1,0:T(8,128)(2,1)S(1)}, bf16[128,640]{1,0:T(8,128)(2,1)S(1)}, u32[]{:S(2)}, u32[]{:S(2)}) collective-permute-start(bf16[128,640]{1,0:T(8,128)(2,1)S(1)} %get-tuple-element.72), channel_id=1, source_target_pairs={{0,2},{1,3},{2,0},{3,1},{4,6},{5,7},{6,4},{7,5},{8,10},{9,11},{10,... | collective-permute-start | bytes 491528 | tf_op jit(solution)/shard_map/ppermute | solution.py:236
  88.5 9.0 %collective-permute-done.19.refs_1_ = bf16[128,640]{1,0:T(8,128)(2,1)S(1)} collective-permute-done((bf16[128,640]{1,0:T(8,128)(2,1)S(1)}, bf16[128,640]{1,0:T(8,128)(2,1)S(1)}, u32[]{:S(2)}, u32[]{:S(2)}) %collective-permute-start.19) | collective-permute-done | bytes 163872 | tf_op jit(solution)/shard_map/ppermute | solution.py:236
  97.5 1.4 %join.1 = bf16[128,2560]{1,0:T(8,128)(2,1)} custom-call(s32[2]{0:T(128)S(1)} %pad_add_fusion.where_ref, bf16[128,640]{1,0:T(8,128)(2,1)S(1)} %get-tuple-element.71.refs_0_, bf16[128,640]{1,0:T(8,128)(2,1)S(1)} %collective-permute-done.19.refs_1_, bf16[128,640]{1,0:T(8,128)(2,1)S(1)} %collective-permute-done.21.refs_2_, ...), custom_call_target="tpu_custom_call" | custom-call | flops 10000000 | bytes 4000000 | tf_op jit(solution)/shard_map/join/pallas_call | solution.py:316
  99.0 2.1 %all-to-all-done = bf16[16,4,32,128]{3,2,1,0:T(8,128)(2,1)S(1)} async-done(((bf16[16,4,32,128]{3,2,1,0:T(8,128)(2,1)}), bf16[16,4,32,128]{3,2,1,0:T(8,128)(2,1)S(1)}, u32[]{:S(2)}, u32[]{:S(2)}) %all-to-all-start) | async-done | bytes 524320 | tf_op jit(solution)/shard_map/all_to_all | solution.py:336
  101.1 0.1 copy.11
  101.2 0.8 copy.12
  (9 shorter events, 0.1 us)
Async XLA Ops:
  0.6 6.1 %copy-start.3 = (f32[128,20]{0,1:T(8,128)S(1)}, f32[128,20]{0,1:T(8,128)}, u32[]{:S(2)}) copy-start(f32[128,20]{0,1:T(8,128)} %param.8) | copy-start | bytes 30724
  0.6 6.2 %copy-start.2 = (bf16[128,2560]{1,0:T(8,128)(2,1)S(1)}, bf16[128,2560]{1,0:T(8,128)(2,1)}, u32[]{:S(2)}) copy-start(bf16[128,2560]{1,0:T(8,128)(2,1)} %v_ref.1) | copy-start | bytes 1966084
  0.7 6.2 %copy-start.1 = (bf16[128,2560]{1,0:T(8,128)(2,1)S(1)}, bf16[128,2560]{1,0:T(8,128)(2,1)}, u32[]{:S(2)}) copy-start(bf16[128,2560]{1,0:T(8,128)(2,1)} %k_ref.1) | copy-start | bytes 1966084
  0.7 6.2 %copy-start = (bf16[128,2560]{1,0:T(8,128)(2,1)S(1)}, bf16[128,2560]{1,0:T(8,128)(2,1)}, u32[]{:S(2)}) copy-start(bf16[128,2560]{1,0:T(8,128)(2,1)} %q_ref.1) | copy-start | bytes 1966084
  2.0 9.4 %collective-permute-start.2 = (bf16[5,3,32,128]{3,2,1,0:T(8,128)(2,1)S(1)}, bf16[5,3,32,128]{3,2,1,0:T(8,128)(2,1)S(1)}, u32[]{:S(2)}, u32[]{:S(2)}) collective-permute-start(bf16[5,3,32,128]{3,2,1,0:T(8,128)(2,1)S(1)} %get-tuple-element.86), channel_id=1, source_target_pairs={{0,4},{1,5},{2,6},{3,7},{4,0},{5,1},{6,2},{7,3},{8,12},{9,13},{10,... | collective-permute-start | bytes 368648 | tf_op jit(solution)/shard_map/ppermute | solution.py:236
  5.1 8.2 %collective-permute-start.3 = (bf16[5,3,32,128]{3,2,1,0:T(8,128)(2,1)S(1)}, bf16[5,3,32,128]{3,2,1,0:T(8,128)(2,1)S(1)}, u32[]{:S(2)}, u32[]{:S(2)}) collective-permute-start(bf16[5,3,32,128]{3,2,1,0:T(8,128)(2,1)S(1)} %get-tuple-element.87), channel_id=1, source_target_pairs={{0,6},{1,7},{2,4},{3,5},{4,2},{5,3},{6,0},{7,1},{8,14},{9,15},{10,... | collective-permute-start | bytes 368648 | tf_op jit(solution)/shard_map/ppermute | solution.py:236
  6.5 7.1 %collective-permute-start.1 = (bf16[5,3,32,128]{3,2,1,0:T(8,128)(2,1)S(1)}, bf16[5,3,32,128]{3,2,1,0:T(8,128)(2,1)S(1)}, u32[]{:S(2)}, u32[]{:S(2)}) collective-permute-start(bf16[5,3,32,128]{3,2,1,0:T(8,128)(2,1)S(1)} %get-tuple-element.88), channel_id=1, source_target_pairs={{0,2},{1,3},{2,0},{3,1},{4,6},{5,7},{6,4},{7,5},{8,10},{9,11},{10,... | collective-permute-start | bytes 368648 | tf_op jit(solution)/shard_map/ppermute | solution.py:236
  7.9 21.9 %collective-permute-start.6 = (bf16[2,128,640]{2,1,0:T(8,128)(2,1)S(1)}, bf16[2,128,640]{2,1,0:T(8,128)(2,1)S(1)}, u32[]{:S(2)}, u32[]{:S(2)}) collective-permute-start(bf16[2,128,640]{2,1,0:T(8,128)(2,1)S(1)} %get-tuple-element.47), channel_id=1, source_target_pairs={{0,4},{1,5},{2,6},{3,7},{4,0},{5,1},{6,2},{7,3},{8,12},{9,13},{10,... | collective-permute-start | bytes 983048 | tf_op jit(solution)/shard_map/ppermute | solution.py:236
  9.9 26.8 %collective-permute-start.7 = (bf16[2,128,640]{2,1,0:T(8,128)(2,1)S(1)}, bf16[2,128,640]{2,1,0:T(8,128)(2,1)S(1)}, u32[]{:S(2)}, u32[]{:S(2)}) collective-permute-start(bf16[2,128,640]{2,1,0:T(8,128)(2,1)S(1)} %get-tuple-element.48), channel_id=1, source_target_pairs={{0,6},{1,7},{2,4},{3,5},{4,2},{5,3},{6,0},{7,1},{8,14},{9,15},{10,... | collective-permute-start | bytes 983048 | tf_op jit(solution)/shard_map/ppermute | solution.py:236
  13.6 23.1 %collective-permute-start.4 = (bf16[2,5,3,32,128]{4,3,2,1,0:T(8,128)(2,1)S(1)}, bf16[2,5,3,32,128]{4,3,2,1,0:T(8,128)(2,1)S(1)}, u32[]{:S(2)}, u32[]{:S(2)}) collective-permute-start(bf16[2,5,3,32,128]{4,3,2,1,0:T(8,128)(2,1)S(1)} %pad_maximum_fusion.refs_4_.refs_0_), channel_id=1, source_target_pairs={{0,8},{1,9},{2,10},{3,11},{4,12},{5,13},{6,14},{7,15},{8,0},{9,1},... | collective-permute-start | bytes 737288 | tf_op jit(solution)/shard_map/ppermute | solution.py:236
  16.3 20.4 %collective-permute-start.5 = (bf16[2,5,3,32,128]{4,3,2,1,0:T(8,128)(2,1)S(1)}, bf16[2,5,3,32,128]{4,3,2,1,0:T(8,128)(2,1)S(1)}, u32[]{:S(2)}, u32[]{:S(2)}) collective-permute-start(bf16[2,5,3,32,128]{4,3,2,1,0:T(8,128)(2,1)S(1)} %pad_maximum_fusion.1.refs_5_.refs_1_), channel_id=1, source_target_pairs={{0,8},{1,9},{2,10},{3,11},{4,12},{5,13},{6,14},{7,15},{8,0},{9,1},... | collective-permute-start | bytes 737288 | tf_op jit(solution)/shard_map/ppermute | solution.py:236
  16.6 20.7 %collective-permute-start = (bf16[2,128,640]{2,1,0:T(8,128)(2,1)S(1)}, bf16[2,128,640]{2,1,0:T(8,128)(2,1)S(1)}, u32[]{:S(2)}, u32[]{:S(2)}) collective-permute-start(bf16[2,128,640]{2,1,0:T(8,128)(2,1)S(1)} %get-tuple-element.44), channel_id=1, source_target_pairs={{0,2},{1,3},{2,0},{3,1},{4,6},{5,7},{6,4},{7,5},{8,10},{9,11},{10,... | collective-permute-start | bytes 983048 | tf_op jit(solution)/shard_map/ppermute | solution.py:236
  29.8 7.9 %collective-permute-start.8 = (bf16[2,5,3,32,128]{4,3,2,1,0:T(8,128)(2,1)S(1)}, bf16[2,5,3,32,128]{4,3,2,1,0:T(8,128)(2,1)S(1)}, u32[]{:S(2)}, u32[]{:S(2)}) collective-permute-start(bf16[2,5,3,32,128]{4,3,2,1,0:T(8,128)(2,1)S(1)} %pad_maximum_fusion.refs_4_.refs_0_), channel_id=1, source_target_pairs={{0,1},{1,0},{2,3},{3,2},{4,5},{5,4},{6,7},{7,6},{8,9},{9,8},{10,11... | collective-permute-start | bytes 737288 | tf_op jit(solution)/shard_map/ppermute | solution.py:236
  36.7 3.7 %collective-permute-start.9 = (bf16[2,5,3,32,128]{4,3,2,1,0:T(8,128)(2,1)S(1)}, bf16[2,5,3,32,128]{4,3,2,1,0:T(8,128)(2,1)S(1)}, u32[]{:S(2)}, u32[]{:S(2)}) collective-permute-start(bf16[2,5,3,32,128]{4,3,2,1,0:T(8,128)(2,1)S(1)} %pad_maximum_fusion.1.refs_5_.refs_1_), channel_id=1, source_target_pairs={{0,1},{1,0},{2,3},{3,2},{4,5},{5,4},{6,7},{7,6},{8,9},{9,8},{10,11... | collective-permute-start | bytes 737288 | tf_op jit(solution)/shard_map/ppermute | solution.py:236
  36.7 4.1 %collective-permute-start.10 = (bf16[2,5,3,32,128]{4,3,2,1,0:T(8,128)(2,1)S(1)}, bf16[2,5,3,32,128]{4,3,2,1,0:T(8,128)(2,1)S(1)}, u32[]{:S(2)}, u32[]{:S(2)}) collective-permute-start(bf16[2,5,3,32,128]{4,3,2,1,0:T(8,128)(2,1)S(1)} %collective-permute-done.4.refs_8_.refs_4_), channel_id=1, source_target_pairs={{0,1},{1,0},{2,3},{3,2},{4,5},{5,4},{6,7},{7,6},{8,9},{9,8},{10,11... | collective-permute-start | bytes 737288 | tf_op jit(solution)/shard_map/ppermute | solution.py:236
  37.2 3.6 %collective-permute-start.11 = (bf16[2,5,3,32,128]{4,3,2,1,0:T(8,128)(2,1)S(1)}, bf16[2,5,3,32,128]{4,3,2,1,0:T(8,128)(2,1)S(1)}, u32[]{:S(2)}, u32[]{:S(2)}) collective-permute-start(bf16[2,5,3,32,128]{4,3,2,1,0:T(8,128)(2,1)S(1)} %collective-permute-done.5.refs_9_.refs_5_), channel_id=1, source_target_pairs={{0,1},{1,0},{2,3},{3,2},{4,5},{5,4},{6,7},{7,6},{8,9},{9,8},{10,11... | collective-permute-start | bytes 737288 | tf_op jit(solution)/shard_map/ppermute | solution.py:236
  37.3 12.2 %collective-permute-start.16 = (bf16[128,640]{1,0:T(8,128)(2,1)S(1)}, bf16[128,640]{1,0:T(8,128)(2,1)S(1)}, u32[]{:S(2)}, u32[]{:S(2)}) collective-permute-start(bf16[128,640]{1,0:T(8,128)(2,1)S(1)} %get-tuple-element.64), channel_id=1, source_target_pairs={{0,2},{1,3},{2,0},{3,1},{4,6},{5,7},{6,4},{7,5},{8,10},{9,11},{10,... | collective-permute-start | bytes 491528 | tf_op jit(solution)/shard_map/ppermute | solution.py:236
  37.7 11.8 %collective-permute-start.17 = (bf16[128,640]{1,0:T(8,128)(2,1)S(1)}, bf16[128,640]{1,0:T(8,128)(2,1)S(1)}, u32[]{:S(2)}, u32[]{:S(2)}) collective-permute-start(bf16[128,640]{1,0:T(8,128)(2,1)S(1)} %get-tuple-element.65), channel_id=1, source_target_pairs={{0,4},{1,5},{2,6},{3,7},{4,0},{5,1},{6,2},{7,3},{8,12},{9,13},{10,... | collective-permute-start | bytes 491528 | tf_op jit(solution)/shard_map/ppermute | solution.py:236
  40.5 9.5 %collective-permute-start.18 = (bf16[128,640]{1,0:T(8,128)(2,1)S(1)}, bf16[128,640]{1,0:T(8,128)(2,1)S(1)}, u32[]{:S(2)}, u32[]{:S(2)}) collective-permute-start(bf16[128,640]{1,0:T(8,128)(2,1)S(1)} %get-tuple-element.66), channel_id=1, source_target_pairs={{0,6},{1,7},{2,4},{3,5},{4,2},{5,3},{6,0},{7,1},{8,14},{9,15},{10,... | collective-permute-start | bytes 491528 | tf_op jit(solution)/shard_map/ppermute | solution.py:236
  48.9 1.4 %collective-permute-start.12 = (bf16[512,128]{1,0:T(8,128)(2,1)S(1)}, bf16[512,128]{1,0:T(8,128)(2,1)S(1)}, u32[]{:S(2)}, u32[]{:S(2)}) collective-permute-start(bf16[512,128]{1,0:T(8,128)(2,1)S(1)} %get-tuple-element.59), channel_id=1, source_target_pairs={{0,1},{1,0},{2,3},{3,2},{4,5},{5,4},{6,7},{7,6},{8,9},{9,8},{10,11... | collective-permute-start | bytes 393224 | tf_op jit(solution)/shard_map/ppermute | solution.py:236
  49.0 1.5 %collective-permute-start.13 = (bf16[512,128]{1,0:T(8,128)(2,1)S(1)}, bf16[512,128]{1,0:T(8,128)(2,1)S(1)}, u32[]{:S(2)}, u32[]{:S(2)}) collective-permute-start(bf16[512,128]{1,0:T(8,128)(2,1)S(1)} %get-tuple-element.60), channel_id=1, source_target_pairs={{0,1},{1,0},{2,3},{3,2},{4,5},{5,4},{6,7},{7,6},{8,9},{9,8},{10,11... | collective-permute-start | bytes 393224 | tf_op jit(solution)/shard_map/ppermute | solution.py:236
  49.5 1.3 %collective-permute-start.14 = (bf16[512,128]{1,0:T(8,128)(2,1)S(1)}, bf16[512,128]{1,0:T(8,128)(2,1)S(1)}, u32[]{:S(2)}, u32[]{:S(2)}) collective-permute-start(bf16[512,128]{1,0:T(8,128)(2,1)S(1)} %get-tuple-element.61), channel_id=1, source_target_pairs={{0,1},{1,0},{2,3},{3,2},{4,5},{5,4},{6,7},{7,6},{8,9},{9,8},{10,11... | collective-permute-start | bytes 393224 | tf_op jit(solution)/shard_map/ppermute | solution.py:236
  49.6 1.5 %collective-permute-start.15 = (bf16[512,128]{1,0:T(8,128)(2,1)S(1)}, bf16[512,128]{1,0:T(8,128)(2,1)S(1)}, u32[]{:S(2)}, u32[]{:S(2)}) collective-permute-start(bf16[512,128]{1,0:T(8,128)(2,1)S(1)} %get-tuple-element.62), channel_id=1, source_target_pairs={{0,1},{1,0},{2,3},{3,2},{4,5},{5,4},{6,7},{7,6},{8,9},{9,8},{10,11... | collective-permute-start | bytes 393224 | tf_op jit(solution)/shard_map/ppermute | solution.py:236
  51.2 26.5 %collective-permute-start.20 = (bf16[4,512,128]{2,1,0:T(8,128)(2,1)S(1)}, bf16[4,512,128]{2,1,0:T(8,128)(2,1)S(1)}, u32[]{:S(2)}, u32[]{:S(2)}) collective-permute-start(bf16[4,512,128]{2,1,0:T(8,128)(2,1)S(1)} %fusion), channel_id=1, source_target_pairs={{0,8},{1,9},{2,10},{3,11},{4,12},{5,13},{6,14},{7,15},{8,0},{9,1},... | collective-permute-start | bytes 1572872 | tf_op jit(solution)/shard_map/ppermute | solution.py:236
  53.5 24.1 %collective-permute-start.23 = (bf16[4,512,128]{2,1,0:T(8,128)(2,1)S(1)}, bf16[4,512,128]{2,1,0:T(8,128)(2,1)S(1)}, u32[]{:S(2)}, u32[]{:S(2)}) collective-permute-start(bf16[4,512,128]{2,1,0:T(8,128)(2,1)S(1)} %get-tuple-element.82), channel_id=1, source_target_pairs={{0,1},{1,0},{2,3},{3,2},{4,5},{5,4},{6,7},{7,6},{8,9},{9,8},{10,11... | collective-permute-start | bytes 1572872 | tf_op jit(solution)/shard_map/ppermute | solution.py:236
  57.6 11.7 %collective-permute-start.21 = (bf16[128,640]{1,0:T(8,128)(2,1)S(1)}, bf16[128,640]{1,0:T(8,128)(2,1)S(1)}, u32[]{:S(2)}, u32[]{:S(2)}) collective-permute-start(bf16[128,640]{1,0:T(8,128)(2,1)S(1)} %get-tuple-element.78), channel_id=1, source_target_pairs={{0,4},{1,5},{2,6},{3,7},{4,0},{5,1},{6,2},{7,3},{8,12},{9,13},{10,... | collective-permute-start | bytes 491528 | tf_op jit(solution)/shard_map/ppermute | solution.py:236
  59.7 12.6 %collective-permute-start.22 = (bf16[128,640]{1,0:T(8,128)(2,1)S(1)}, bf16[128,640]{1,0:T(8,128)(2,1)S(1)}, u32[]{:S(2)}, u32[]{:S(2)}) collective-permute-start(bf16[128,640]{1,0:T(8,128)(2,1)S(1)} %get-tuple-element.79), channel_id=1, source_target_pairs={{0,6},{1,7},{2,4},{3,5},{4,2},{5,3},{6,0},{7,1},{8,14},{9,15},{10,... | collective-permute-start | bytes 491528 | tf_op jit(solution)/shard_map/ppermute | solution.py:236
  81.3 19.8 %all-to-all-start = ((bf16[16,4,32,128]{3,2,1,0:T(8,128)(2,1)}), bf16[16,4,32,128]{3,2,1,0:T(8,128)(2,1)S(1)}, u32[]{:S(2)}, u32[]{:S(2)}) async-start(bf16[16,4,32,128]{3,2,1,0:T(8,128)(2,1)} %renew.1), calls=%async_computation | async-start | bytes 1048576 | tf_op jit(solution)/shard_map/all_to_all | solution.py:336
  86.6 10.9 %collective-permute-start.19 = (bf16[128,640]{1,0:T(8,128)(2,1)S(1)}, bf16[128,640]{1,0:T(8,128)(2,1)S(1)}, u32[]{:S(2)}, u32[]{:S(2)}) collective-permute-start(bf16[128,640]{1,0:T(8,128)(2,1)S(1)} %get-tuple-element.72), channel_id=1, source_target_pairs={{0,2},{1,3},{2,0},{3,1},{4,6},{5,7},{6,4},{7,5},{8,10},{9,11},{10,... | collective-permute-start | bytes 491528 | tf_op jit(solution)/shard_map/ppermute | solution.py:236

commit v6 on v5

--- a/solution.py
+++ b/solution.py
@@ -65,7 +65,7 @@
 
 def key_kernel(squares, heads, where_ref, *refs):
     pairs, w_refs = refs[:squares], refs[squares : squares + 8]
-    keep_ref, near_ref, *far_refs, terms = refs[squares + 8 :]
+    mine_ref, sent_ref, near_ref, *far_refs, terms = refs[squares + 8 :]
     spot, place = where_ref[0], where_ref[1]
     _, hid, head_size = terms.shape
     rows = hid // (PLACES * squares)
@@ -76,9 +76,13 @@
         rel = (number % PLACES) ^ place
         slot = number // PLACES
 
-        @pl.when(rel % 2 == 0)
+        @pl.when(rel == 0)
         def _():
-            keep_ref[rel // 2, slot] = value
+            mine_ref[slot] = value
+
+        @pl.when(rel == 2)
+        def _():
+            sent_ref[slot] = value
 
         @pl.when(rel == 1)
         def _():
@@ -92,7 +96,7 @@
 
     @pl.when(step == 0)
     def _():
-        for number in range(3 * heads, PLACES * keep_ref.shape[1]):
+        for number in range(3 * heads, PLACES * mine_ref.shape[0]):
             put(number, jnp.zeros((hid, head_size), jnp.float32))
 
     keys = jnp.concatenate([pair[0] for pair in pairs], axis=0)
@@ -154,19 +158,29 @@
     return dot(a[0], b[0], dims) + (dot(a[0], b[1], dims) + dot(a[1], b[0], dims))
 
 
-def renew_kernel(squares, where_ref, mine_ref, near_ref, far_ref, *refs):
-    w_refs, (out_ref, updates) = refs[:8], refs[-2:]
+def pick_kernel(squares, where_ref, *refs):
+    w_refs, out_ref = refs[:8], refs[8]
     spot, place = where_ref[0], where_ref[1]
+    heads = w_refs[0].shape[1]
+    for slot in range(out_ref.shape[1]):
+        number = jnp.minimum(PLACES * slot + place, 3 * heads - 1)
+        for rel in range(PLACES):
+            owner = place ^ rel
+            for apart in range(squares):
+                w = w_refs[2 * rel + apart // (squares // 2)]
+                to = (owner // 2 * squares + (spot ^ apart)) * 2 + owner % 2
+                out_ref[to, slot] = w[apart % (squares // 2), number // 3, number % 3]
+
+
+def renew_kernel(squares, mine_ref, far_ref, old_ref, out_ref, updates):
     slots, hid, head_size = far_ref.shape
-    heads = w_refs[0].shape[1]
     rows = out_ref.shape[2]
     eye = (
         lax.broadcasted_iota(jnp.int32, (head_size, head_size), 0)
         == lax.broadcasted_iota(jnp.int32, (head_size, head_size), 1)
     ).astype(jnp.float32)
     grads = [
-        mine_ref[0, slot]
-        + near_ref[slot].astype(jnp.float32)
+        mine_ref[slot]
         + far_ref[slot].astype(jnp.float32)
         for slot in range(slots)
     ]
@@ -199,16 +213,12 @@
     for slot in range(slots):
         updates[slot] = math.sqrt(HID) * dot_halves(grads[slot], halves(factors[slot]), NT)
     for slot in range(slots):
-        number = jnp.minimum(PLACES * slot + place, 3 * heads - 1)
-        head, matrix = number // 3, number % 3
-        for rel in range(PLACES):
-            owner = place ^ rel
-            for apart in range(squares):
-                w = w_refs[2 * rel + apart // (squares // 2)]
-                at = pl.multiple_of((owner * squares + (spot ^ apart)) * rows, rows)
-                to = (owner // 2 * squares + (spot ^ apart)) * 2 + owner % 2
-                old = w[apart % (squares // 2), head, matrix].astype(jnp.float32)
-                out_ref[to, slot] = (old - updates[slot, pl.ds(at, rows), :]).astype(out_ref.dtype)
+        for owner in range(PLACES):
+            for at in range(squares):
+                to = (owner // 2 * squares + at) * 2 + owner % 2
+                rows_at = slice((owner * squares + at) * rows, (owner * squares + at + 1) * rows)
+                old = old_ref[to, slot].astype(jnp.float32)
+                out_ref[to, slot] = (old - updates[slot, rows_at, :]).astype(out_ref.dtype)
 
 
 def square_body(queries, key_vectors, value_vectors, token_rates, fast_weights, squares):
@@ -273,17 +283,17 @@
 
     slots = -(-3 * heads // PLACES)
     sums_shape = (slots, hid, head_size)
-    keep, near, *far = pl.pallas_call(
+    mine, sent, near, *far = pl.pallas_call(
         functools.partial(key_kernel, squares, heads),
         grid=(heads,),
         in_specs=[smem]
         + [pl.BlockSpec((2, row_count, head_size), lambda h: (0, 0, h))] * squares
         + [weight_spec] * 8,
-        out_specs=[pl.BlockSpec((2, *sums_shape), lambda h: (0, 0, 0, 0))]
-        + [pl.BlockSpec(sums_shape, lambda h: (0, 0, 0))]
+        out_specs=[pl.BlockSpec(sums_shape, lambda h: (0, 0, 0))] * 3
         + [pl.BlockSpec(sums_shape[1:], lambda h: (0, 0))] * slots,
         out_shape=[
-            jax.ShapeDtypeStruct((2, *sums_shape), jnp.float32),
+            jax.ShapeDtypeStruct(sums_shape, jnp.float32),
+            jax.ShapeDtypeStruct(sums_shape, jnp.float32),
             bf16(*sums_shape),
             *[bf16(*sums_shape[1:])] * slots,
         ],
@@ -294,10 +304,11 @@
     )(where, *moved, *weights)
 
     near = swap(near, 1)
+    mine = mine + near.astype(jnp.float32)
     far = [swap(one, 1) for one in far]
     far, asking = lax.optimization_barrier((far, asking))
     far = jnp.stack(far).astype(jnp.float32)
-    far = swap((keep[1] + far).astype(jnp.bfloat16), half)
+    far = swap((sent + far).astype(jnp.bfloat16), half)
 
     columns = pl.BlockSpec((row_count, head_size), lambda h: (0, h))
     parts = pl.pallas_call(
@@ -311,6 +322,7 @@
         cost_estimate=cost(1000),
         name="query_side",
     )(*asking, *weights)
+    parts, late_weights = lax.optimization_barrier((parts, weights))
     parts = across(parts)
     far, parts[2:] = lax.optimization_barrier((far, parts[2:]))
     applied = pl.pallas_call(
@@ -323,16 +335,25 @@
         name="join",
     )(where, *parts)
 
+    old = pl.pallas_call(
+        functools.partial(pick_kernel, squares),
+        in_specs=[smem] + [vmem] * 8,
+        out_specs=vmem,
+        out_shape=bf16(size, slots, own_rows, head_size),
+        compiler_params=params,
+        cost_estimate=cost(10),
+        name="pick",
+    )(where, *late_weights)
     renewed = pl.pallas_call(
         functools.partial(renew_kernel, squares),
-        in_specs=[smem] + [vmem] * 11,
+        in_specs=[vmem] * 3,
         out_specs=vmem,
         out_shape=bf16(size, slots, own_rows, head_size),
         scratch_shapes=[VMEM(sums_shape, jnp.float32)],
         compiler_params=params,
         cost_estimate=cost(2000),
         name="renew",
-    )(where, keep, near, far, *weights)
+    )(mine, far, old)
     back = lax.all_to_all(renewed, "seq", 0, 0, tiled=True)
     back = back.reshape(2, squares, 2, slots, own_rows, head_size).transpose(1, 3, 0, 2, 4, 5)
     back = back.reshape(squares, PLACES * slots, own_rows, head_size)[:, : 3 * heads]

time: 102 us -> 101 us (level)
  waiting for transfers between devices: 51.7 us -> 50.2 us
    ppermute x24, waiting for transfers between devices: 49.6 us -> 48.1 us  [swap(): return lax.ppermute(array, 'seq', [(at, at ^ step) for at in range(size)])]
    pallas_call x1 -> x2, Pallas kernels: 3.67 us -> 3.69 us  [the longest x1 3.04 us: square_body(): pl.pallas_call(functools.partial(renew_kernel, squares), in_specs=[vmem]...]
  transfers between devices with their start and end apart: 25 -> 25, of which waited for: 13 -> 13; matrix products, arithmetic and copies ran while one was open for 0% -> 0% of each run, Pallas kernels for 14% -> 15%
where the time goes in v6:
time: 101 us
  waiting for transfers between devices  50.2 us (50%)
  starting transfers between devices  28.4 us (28%)
  Pallas kernels  18.4 us (18%)
  local copies, waits for them, and re-layouts  2.88 us (3%)
    ppermute x24, waiting for transfers between devices, swap(): return lax.ppermute(array, 'seq', [(at, at ^ step) for at in range(size)])  48.1 us
    ppermute x24, starting transfers between devices, swap(): return lax.ppermute(array, 'seq', [(at, at ^ step) for at in range(size)])  23.6 us
    pallas_call x1, Pallas kernels, square_body(): pl.pallas_call(functools.partial(key_kernel, squares, heads), grid=(heads...  8.09 us
    all_to_all x1, starting transfers between devices, square_body(): back = lax.all_to_all(renewed, 'seq', 0, 0, tiled=True)  4.82 us
    pallas_call x1, Pallas kernels, square_body(): pl.pallas_call(functools.partial(query_kernel, squares), grid=(heads,), i...  4.06 us
    pallas_call x1, Pallas kernels, square_body(): pl.pallas_call(functools.partial(renew_kernel, squares), in_specs=[vmem]...  3.04 us
    unnamed x11, local copies, waits for them, and re-layouts  2.73 us
    all_to_all x1, waiting for transfers between devices, square_body(): back = lax.all_to_all(renewed, 'seq', 0, 0, tiled=True)  2.12 us
  transfers between devices with their start and end apart: 25, of which 13 were waited for; matrix products, arithmetic and copies ran while one was open for 0% of the time, Pallas kernels for 15%

profile of v6, /device:TPU:0, one launch (start us, length us, event | category | flops | bytes accessed | tf_op | source)
XLA Modules:
  0.0 101.1 jit_solution(5906492488761379442)
XLA Ops:
  0.7 1.2 %copy.10 = bf16[32,3,20,128]{3,0,1,2:T(8,128)(2,1)S(1)} copy(bf16[32,3,20,128]{3,0,2,1:T(8,128)(2,1)} %param.9) | data formatting | bytes 983040 | tf_op args[4]
  1.9 0.0 copy-start
  1.9 0.1 dynamic-slice_bitcast_fusion.1
  2.0 3.1 %collective-permute-start.2 = (bf16[5,3,32,128]{3,2,1,0:T(8,128)(2,1)S(1)}, bf16[5,3,32,128]{3,2,1,0:T(8,128)(2,1)S(1)}, u32[]{:S(2)}, u32[]{:S(2)}) collective-permute-start(bf16[5,3,32,128]{3,2,1,0:T(8,128)(2,1)S(1)} %get-tuple-element.112), channel_id=1, source_target_pairs={{0,4},{1,5},{2,6},{3,7},{4,0},{5,1},{6,2},{7,3},{8,12},{9,13},{10,... | collective-permute-start | bytes 368648 | tf_op jit(solution)/shard_map/ppermute | solution.py:246
  5.0 1.4 %collective-permute-start.3 = (bf16[5,3,32,128]{3,2,1,0:T(8,128)(2,1)S(1)}, bf16[5,3,32,128]{3,2,1,0:T(8,128)(2,1)S(1)}, u32[]{:S(2)}, u32[]{:S(2)}) collective-permute-start(bf16[5,3,32,128]{3,2,1,0:T(8,128)(2,1)S(1)} %get-tuple-element.113), channel_id=1, source_target_pairs={{0,6},{1,7},{2,4},{3,5},{4,2},{5,3},{6,0},{7,1},{8,14},{9,15},{10,... | collective-permute-start | bytes 368648 | tf_op jit(solution)/shard_map/ppermute | solution.py:246
  6.4 0.1 collective-permute-start.1
  6.6 0.1 pad_add_fusion.where_ref
  6.7 0.6 copy-done.3
  7.3 0.1 copy.9.rate_ref
  7.4 1.1 %split.1 = (bf16[2,128,640]{2,1,0:T(8,128)(2,1)S(1)}, bf16[2,128,640]{2,1,0:T(8,128)(2,1)S(1)}, bf16[2,128,640]{2,1,0:T(8,128)(2,1)S(1)}, bf16[2,128,640]{2,1,0:...) custom-call(s32[2]{0:T(128)S(1)} %pad_add_fusion.where_ref, ...), custom_call_target="tpu_custom_call" | custom-call | flops 10000000 | bytes 4000000 | tf_op jit(solution)/shard_map/split/pallas_call | solution.py:254
  8.5 2.0 %collective-permute-start.6 = (bf16[2,128,640]{2,1,0:T(8,128)(2,1)S(1)}, bf16[2,128,640]{2,1,0:T(8,128)(2,1)S(1)}, u32[]{:S(2)}, u32[]{:S(2)}) collective-permute-start(bf16[2,128,640]{2,1,0:T(8,128)(2,1)S(1)} %get-tuple-element.60), channel_id=1, source_target_pairs={{0,4},{1,5},{2,6},{3,7},{4,0},{5,1},{6,2},{7,3},{8,12},{9,13},{10,... | collective-permute-start | bytes 983048 | tf_op jit(solution)/shard_map/ppermute | solution.py:246
  10.5 1.4 %collective-permute-start.7 = (bf16[2,128,640]{2,1,0:T(8,128)(2,1)S(1)}, bf16[2,128,640]{2,1,0:T(8,128)(2,1)S(1)}, u32[]{:S(2)}, u32[]{:S(2)}) collective-permute-start(bf16[2,128,640]{2,1,0:T(8,128)(2,1)S(1)} %get-tuple-element.61), channel_id=1, source_target_pairs={{0,6},{1,7},{2,4},{3,5},{4,2},{5,3},{6,0},{7,1},{8,14},{9,15},{10,... | collective-permute-start | bytes 983048 | tf_op jit(solution)/shard_map/ppermute | solution.py:246
  11.9 0.0 collective-permute-done.2
  11.9 0.7 collective-permute-done.3
  12.7 0.9 collective-permute-done.1
  13.6 2.7 %collective-permute-start.4 = (bf16[2,5,3,32,128]{4,3,2,1,0:T(8,128)(2,1)S(1)}, bf16[2,5,3,32,128]{4,3,2,1,0:T(8,128)(2,1)S(1)}, u32[]{:S(2)}, u32[]{:S(2)}) collective-permute-start(bf16[2,5,3,32,128]{4,3,2,1,0:T(8,128)(2,1)S(1)} %pad_maximum_fusion.refs_4_.refs_0_), channel_id=1, source_target_pairs={{0,8},{1,9},{2,10},{3,11},{4,12},{5,13},{6,14},{7,15},{8,0},{9,1},... | collective-permute-start | bytes 737288 | tf_op jit(solution)/shard_map/ppermute | solution.py:246
  16.3 0.3 collective-permute-start.5
  16.6 0.4 collective-permute-start
  17.0 12.7 %collective-permute-done.6.refs_2_ = bf16[2,128,640]{2,1,0:T(8,128)(2,1)S(1)} collective-permute-done((bf16[2,128,640]{2,1,0:T(8,128)(2,1)S(1)}, bf16[2,128,640]{2,1,0:T(8,128)(2,1)S(1)}, u32[]{:S(2)}, u32[]{:S(2)}) %collective-permute-start.6) | collective-permute-done | bytes 327712 | tf_op jit(solution)/shard_map/ppermute | solution.py:246
  29.8 0.0 collective-permute-start.8
  29.8 6.9 %collective-permute-done.7.refs_3_ = bf16[2,128,640]{2,1,0:T(8,128)(2,1)S(1)} collective-permute-done((bf16[2,128,640]{2,1,0:T(8,128)(2,1)S(1)}, bf16[2,128,640]{2,1,0:T(8,128)(2,1)S(1)}, u32[]{:S(2)}, u32[]{:S(2)}) %collective-permute-start.7) | collective-permute-done | bytes 327712 | tf_op jit(solution)/shard_map/ppermute | solution.py:246
  36.7 0.0 collective-permute-start.9
  36.7 0.0 collective-permute-done.4.refs_8_.refs_4_
  36.7 0.0 collective-permute-done.5.refs_9_.refs_5_
  36.7 0.5 collective-permute-start.10
  37.2 0.1 collective-permute-start.11
  37.3 0.0 collective-permute-done.refs_1_
  37.3 0.4 collective-permute-start.16
  37.7 0.0 collective-permute-done.8.refs_6_.refs_2_
  37.7 2.7 %collective-permute-start.17 = (bf16[128,640]{1,0:T(8,128)(2,1)S(1)}, bf16[128,640]{1,0:T(8,128)(2,1)S(1)}, u32[]{:S(2)}, u32[]{:S(2)}) collective-permute-start(bf16[128,640]{1,0:T(8,128)(2,1)S(1)} %get-tuple-element.78), channel_id=1, source_target_pairs={{0,4},{1,5},{2,6},{3,7},{4,0},{5,1},{6,2},{7,3},{8,12},{9,13},{10,... | collective-permute-start | bytes 491528 | tf_op jit(solution)/shard_map/ppermute | solution.py:246
  40.4 0.0 collective-permute-done.9.refs_7_.refs_3_
  40.4 0.4 collective-permute-start.18
  40.8 0.0 collective-permute-done.10.refs_10_.refs_6_
  40.8 0.0 collective-permute-done.11.refs_11_.refs_7_
  40.8 8.1 %key_side.1 = (f32[4,512,128]{2,1,0:T(8,128)S(1)}, f32[4,512,128]{2,1,0:T(8,128)S(1)}, bf16[4,512,128]{2,1,0:T(8,128)(2,1)S(1)}, bf16[512,128]{1,0:T(8,128)(2,1)...) custom-call(s32[2]{0:T(128)S(1)} %pad_add_fusion.where_ref, ...), custom_call_target="tpu_custom_call" | custom-call | flops 2000000000 | bytes 4000000 | tf_op jit(solution)/shard_map/key_side/pallas_call | solution.py:286
  48.9 0.1 collective-permute-start.12
  49.0 0.5 collective-permute-start.13
  49.5 0.0 collective-permute-done.16.refs_1_
  49.5 0.1 collective-permute-start.14
  49.6 0.0 collective-permute-done.17.refs_2_
  49.6 0.4 collective-permute-start.15
  50.0 0.1 collective-permute-start.23
  50.1 0.2 collective-permute-done.12
  50.3 0.2 collective-permute-done.13
  50.5 0.3 collective-permute-done.14
  50.8 0.2 collective-permute-done.15
  51.0 0.1 add_convert_fusion
  51.2 2.9 %collective-permute-start.20 = (bf16[4,512,128]{2,1,0:T(8,128)(2,1)S(1)}, bf16[4,512,128]{2,1,0:T(8,128)(2,1)S(1)}, u32[]{:S(2)}, u32[]{:S(2)}) collective-permute-start(bf16[4,512,128]{2,1,0:T(8,128)(2,1)S(1)} %add_convert_fusion), channel_id=1, source_target_pairs={{0,8},{1,9},{2,10},{3,11},{4,12},{5,13},{6,14},{7,15},{8,0},{9,1},... | collective-permute-start | bytes 1572872 | tf_op jit(solution)/shard_map/ppermute | solution.py:246
  54.1 4.1 %query_side.1 = (bf16[128,640]{1,0:T(8,128)(2,1)S(1)}, bf16[128,640]{1,0:T(8,128)(2,1)S(1)}, bf16[128,640]{1,0:T(8,128)(2,1)S(1)}, bf16[128,640]{1,0:T(8,128)(2,1)S(1)}) custom-call(bf16[128,640]{1,0:T(8,128)(2,1)S(1)} %get-tuple-element.80.refs_0_, bf16[128,640]{1,0:T(8,128)(2,1)S(1)} %collective-permute-done.16.refs_1_, ...), custom_call_target="tpu_custom_call" | custom-call | flops 1000000000 | bytes 4000000 | tf_op jit(solution)/shard_map/query_side/pallas_call | solution.py:314
  58.2 2.0 %collective-permute-start.21 = (bf16[128,640]{1,0:T(8,128)(2,1)S(1)}, bf16[128,640]{1,0:T(8,128)(2,1)S(1)}, u32[]{:S(2)}, u32[]{:S(2)}) collective-permute-start(bf16[128,640]{1,0:T(8,128)(2,1)S(1)} %get-tuple-element.95), channel_id=1, source_target_pairs={{0,4},{1,5},{2,6},{3,7},{4,0},{5,1},{6,2},{7,3},{8,12},{9,13},{10,... | collective-permute-start | bytes 491528 | tf_op jit(solution)/shard_map/ppermute | solution.py:246
  60.2 0.0 collective-permute-start.22
  60.2 0.7 pick.1.old_ref
  60.9 0.0 collective-permute-done.23
  60.9 0.1 convert_add_fusion.mine_ref
  61.0 8.9 %collective-permute-done.21.refs_2_ = bf16[128,640]{1,0:T(8,128)(2,1)S(1)} collective-permute-done((bf16[128,640]{1,0:T(8,128)(2,1)S(1)}, bf16[128,640]{1,0:T(8,128)(2,1)S(1)}, u32[]{:S(2)}, u32[]{:S(2)}) %collective-permute-start.21) | collective-permute-done | bytes 163872 | tf_op jit(solution)/shard_map/ppermute | solution.py:246
  69.9 2.9 %collective-permute-done.22.refs_3_ = bf16[128,640]{1,0:T(8,128)(2,1)S(1)} collective-permute-done((bf16[128,640]{1,0:T(8,128)(2,1)S(1)}, bf16[128,640]{1,0:T(8,128)(2,1)S(1)}, u32[]{:S(2)}, u32[]{:S(2)}) %collective-permute-start.22) | collective-permute-done | bytes 163872 | tf_op jit(solution)/shard_map/ppermute | solution.py:246
  72.8 5.0 %collective-permute-done.20.far_ref = bf16[4,512,128]{2,1,0:T(8,128)(2,1)S(1)} collective-permute-done((bf16[4,512,128]{2,1,0:T(8,128)(2,1)S(1)}, bf16[4,512,128]{2,1,0:T(8,128)(2,1)S(1)}, u32[]{:S(2)}, u32[]{:S(2)}) %collective-permute-start.20) | collective-permute-done | bytes 524320 | tf_op jit(solution)/shard_map/ppermute | solution.py:246
  77.9 3.0 %renew.1 = bf16[16,4,32,128]{3,2,1,0:T(8,128)(2,1)} custom-call(f32[4,512,128]{2,1,0:T(8,128)S(1)} %convert_add_fusion.mine_ref, bf16[4,512,128]{2,1,0:T(8,128)(2,1)S(1)} %collective-permute-done.20.far_ref, bf16[16,4,32,128]{3,2,1,0:T(8,128)(2,1)S(1)} %pick.1.old_ref), custom_call_target="tpu_custom_call" | custom-call | flops 2000000000 | bytes 4000000 | tf_op jit(solution)/shard_map/renew/pallas_call | solution.py:347
  80.9 4.8 %all-to-all-start = ((bf16[16,4,32,128]{3,2,1,0:T(8,128)(2,1)}), bf16[16,4,32,128]{3,2,1,0:T(8,128)(2,1)S(1)}, u32[]{:S(2)}, u32[]{:S(2)}) async-start(bf16[16,4,32,128]{3,2,1,0:T(8,128)(2,1)} %renew.1), calls=%async_computation | async-start | bytes 1048576 | tf_op jit(solution)/shard_map/all_to_all | solution.py:357
  85.7 1.9 %collective-permute-start.19 = (bf16[128,640]{1,0:T(8,128)(2,1)S(1)}, bf16[128,640]{1,0:T(8,128)(2,1)S(1)}, u32[]{:S(2)}, u32[]{:S(2)}) collective-permute-start(bf16[128,640]{1,0:T(8,128)(2,1)S(1)} %get-tuple-element.89), channel_id=1, source_target_pairs={{0,2},{1,3},{2,0},{3,1},{4,6},{5,7},{6,4},{7,5},{8,10},{9,11},{10,... | collective-permute-start | bytes 491528 | tf_op jit(solution)/shard_map/ppermute | solution.py:246
  87.7 9.0 %collective-permute-done.19.refs_1_ = bf16[128,640]{1,0:T(8,128)(2,1)S(1)} collective-permute-done((bf16[128,640]{1,0:T(8,128)(2,1)S(1)}, bf16[128,640]{1,0:T(8,128)(2,1)S(1)}, u32[]{:S(2)}, u32[]{:S(2)}) %collective-permute-start.19) | collective-permute-done | bytes 163872 | tf_op jit(solution)/shard_map/ppermute | solution.py:246
  96.6 1.4 %join.1 = bf16[128,2560]{1,0:T(8,128)(2,1)} custom-call(s32[2]{0:T(128)S(1)} %pad_add_fusion.where_ref, bf16[128,640]{1,0:T(8,128)(2,1)S(1)} %get-tuple-element.88.refs_0_, bf16[128,640]{1,0:T(8,128)(2,1)S(1)} %collective-permute-done.19.refs_1_, bf16[128,640]{1,0:T(8,128)(2,1)S(1)} %collective-permute-done.21.refs_2_, ...), custom_call_target="tpu_custom_call" | custom-call | flops 10000000 | bytes 4000000 | tf_op jit(solution)/shard_map/join/pallas_call | solution.py:328
  98.1 2.1 %all-to-all-done = bf16[16,4,32,128]{3,2,1,0:T(8,128)(2,1)S(1)} async-done(((bf16[16,4,32,128]{3,2,1,0:T(8,128)(2,1)}), bf16[16,4,32,128]{3,2,1,0:T(8,128)(2,1)S(1)}, u32[]{:S(2)}, u32[]{:S(2)}) %all-to-all-start) | async-done | bytes 524320 | tf_op jit(solution)/shard_map/all_to_all | solution.py:357
  100.3 0.8 copy.12
  (11 shorter events, 0.2 us)
Async XLA Ops:
  0.7 6.7 %copy-start.1 = (bf16[128,2560]{1,0:T(8,128)(2,1)S(1)}, bf16[128,2560]{1,0:T(8,128)(2,1)}, u32[]{:S(2)}) copy-start(bf16[128,2560]{1,0:T(8,128)(2,1)} %k_ref.1) | copy-start | bytes 1966084
  0.7 6.7 %copy-start.2 = (bf16[128,2560]{1,0:T(8,128)(2,1)S(1)}, bf16[128,2560]{1,0:T(8,128)(2,1)}, u32[]{:S(2)}) copy-start(bf16[128,2560]{1,0:T(8,128)(2,1)} %v_ref.1) | copy-start | bytes 1966084
  1.9 5.5 %copy-start = (bf16[128,2560]{1,0:T(8,128)(2,1)S(1)}, bf16[128,2560]{1,0:T(8,128)(2,1)}, u32[]{:S(2)}) copy-start(bf16[128,2560]{1,0:T(8,128)(2,1)} %q_ref.1) | copy-start | bytes 1966084
  2.0 10.0 %collective-permute-start.2 = (bf16[5,3,32,128]{3,2,1,0:T(8,128)(2,1)S(1)}, bf16[5,3,32,128]{3,2,1,0:T(8,128)(2,1)S(1)}, u32[]{:S(2)}, u32[]{:S(2)}) collective-permute-start(bf16[5,3,32,128]{3,2,1,0:T(8,128)(2,1)S(1)} %get-tuple-element.112), channel_id=1, source_target_pairs={{0,4},{1,5},{2,6},{3,7},{4,0},{5,1},{6,2},{7,3},{8,12},{9,13},{10,... | collective-permute-start | bytes 368648 | tf_op jit(solution)/shard_map/ppermute | solution.py:246
  5.0 7.6 %collective-permute-start.3 = (bf16[5,3,32,128]{3,2,1,0:T(8,128)(2,1)S(1)}, bf16[5,3,32,128]{3,2,1,0:T(8,128)(2,1)S(1)}, u32[]{:S(2)}, u32[]{:S(2)}) collective-permute-start(bf16[5,3,32,128]{3,2,1,0:T(8,128)(2,1)S(1)} %get-tuple-element.113), channel_id=1, source_target_pairs={{0,6},{1,7},{2,4},{3,5},{4,2},{5,3},{6,0},{7,1},{8,14},{9,15},{10,... | collective-permute-start | bytes 368648 | tf_op jit(solution)/shard_map/ppermute | solution.py:246
  6.4 7.1 %collective-permute-start.1 = (bf16[5,3,32,128]{3,2,1,0:T(8,128)(2,1)S(1)}, bf16[5,3,32,128]{3,2,1,0:T(8,128)(2,1)S(1)}, u32[]{:S(2)}, u32[]{:S(2)}) collective-permute-start(bf16[5,3,32,128]{3,2,1,0:T(8,128)(2,1)S(1)} %get-tuple-element.114), channel_id=1, source_target_pairs={{0,2},{1,3},{2,0},{3,1},{4,6},{5,7},{6,4},{7,5},{8,10},{9,11},{10,... | collective-permute-start | bytes 368648 | tf_op jit(solution)/shard_map/ppermute | solution.py:246
  6.6 0.7 copy-start.3
  8.5 21.2 %collective-permute-start.6 = (bf16[2,128,640]{2,1,0:T(8,128)(2,1)S(1)}, bf16[2,128,640]{2,1,0:T(8,128)(2,1)S(1)}, u32[]{:S(2)}, u32[]{:S(2)}) collective-permute-start(bf16[2,128,640]{2,1,0:T(8,128)(2,1)S(1)} %get-tuple-element.60), channel_id=1, source_target_pairs={{0,4},{1,5},{2,6},{3,7},{4,0},{5,1},{6,2},{7,3},{8,12},{9,13},{10,... | collective-permute-start | bytes 983048 | tf_op jit(solution)/shard_map/ppermute | solution.py:246
  10.5 26.2 %collective-permute-start.7 = (bf16[2,128,640]{2,1,0:T(8,128)(2,1)S(1)}, bf16[2,128,640]{2,1,0:T(8,128)(2,1)S(1)}, u32[]{:S(2)}, u32[]{:S(2)}) collective-permute-start(bf16[2,128,640]{2,1,0:T(8,128)(2,1)S(1)} %get-tuple-element.61), channel_id=1, source_target_pairs={{0,6},{1,7},{2,4},{3,5},{4,2},{5,3},{6,0},{7,1},{8,14},{9,15},{10,... | collective-permute-start | bytes 983048 | tf_op jit(solution)/shard_map/ppermute | solution.py:246
  13.6 23.1 %collective-permute-start.4 = (bf16[2,5,3,32,128]{4,3,2,1,0:T(8,128)(2,1)S(1)}, bf16[2,5,3,32,128]{4,3,2,1,0:T(8,128)(2,1)S(1)}, u32[]{:S(2)}, u32[]{:S(2)}) collective-permute-start(bf16[2,5,3,32,128]{4,3,2,1,0:T(8,128)(2,1)S(1)} %pad_maximum_fusion.refs_4_.refs_0_), channel_id=1, source_target_pairs={{0,8},{1,9},{2,10},{3,11},{4,12},{5,13},{6,14},{7,15},{8,0},{9,1},... | collective-permute-start | bytes 737288 | tf_op jit(solution)/shard_map/ppermute | solution.py:246
  16.3 20.4 %collective-permute-start.5 = (bf16[2,5,3,32,128]{4,3,2,1,0:T(8,128)(2,1)S(1)}, bf16[2,5,3,32,128]{4,3,2,1,0:T(8,128)(2,1)S(1)}, u32[]{:S(2)}, u32[]{:S(2)}) collective-permute-start(bf16[2,5,3,32,128]{4,3,2,1,0:T(8,128)(2,1)S(1)} %pad_maximum_fusion.1.refs_5_.refs_1_), channel_id=1, source_target_pairs={{0,8},{1,9},{2,10},{3,11},{4,12},{5,13},{6,14},{7,15},{8,0},{9,1},... | collective-permute-start | bytes 737288 | tf_op jit(solution)/shard_map/ppermute | solution.py:246
  16.6 20.7 %collective-permute-start = (bf16[2,128,640]{2,1,0:T(8,128)(2,1)S(1)}, bf16[2,128,640]{2,1,0:T(8,128)(2,1)S(1)}, u32[]{:S(2)}, u32[]{:S(2)}) collective-permute-start(bf16[2,128,640]{2,1,0:T(8,128)(2,1)S(1)} %get-tuple-element.57), channel_id=1, source_target_pairs={{0,2},{1,3},{2,0},{3,1},{4,6},{5,7},{6,4},{7,5},{8,10},{9,11},{10,... | collective-permute-start | bytes 983048 | tf_op jit(solution)/shard_map/ppermute | solution.py:246
  29.8 7.9 %collective-permute-start.8 = (bf16[2,5,3,32,128]{4,3,2,1,0:T(8,128)(2,1)S(1)}, bf16[2,5,3,32,128]{4,3,2,1,0:T(8,128)(2,1)S(1)}, u32[]{:S(2)}, u32[]{:S(2)}) collective-permute-start(bf16[2,5,3,32,128]{4,3,2,1,0:T(8,128)(2,1)S(1)} %pad_maximum_fusion.refs_4_.refs_0_), channel_id=1, source_target_pairs={{0,1},{1,0},{2,3},{3,2},{4,5},{5,4},{6,7},{7,6},{8,9},{9,8},{10,11... | collective-permute-start | bytes 737288 | tf_op jit(solution)/shard_map/ppermute | solution.py:246
  36.7 3.7 %collective-permute-start.9 = (bf16[2,5,3,32,128]{4,3,2,1,0:T(8,128)(2,1)S(1)}, bf16[2,5,3,32,128]{4,3,2,1,0:T(8,128)(2,1)S(1)}, u32[]{:S(2)}, u32[]{:S(2)}) collective-permute-start(bf16[2,5,3,32,128]{4,3,2,1,0:T(8,128)(2,1)S(1)} %pad_maximum_fusion.1.refs_5_.refs_1_), channel_id=1, source_target_pairs={{0,1},{1,0},{2,3},{3,2},{4,5},{5,4},{6,7},{7,6},{8,9},{9,8},{10,11... | collective-permute-start | bytes 737288 | tf_op jit(solution)/shard_map/ppermute | solution.py:246
  36.7 4.1 %collective-permute-start.10 = (bf16[2,5,3,32,128]{4,3,2,1,0:T(8,128)(2,1)S(1)}, bf16[2,5,3,32,128]{4,3,2,1,0:T(8,128)(2,1)S(1)}, u32[]{:S(2)}, u32[]{:S(2)}) collective-permute-start(bf16[2,5,3,32,128]{4,3,2,1,0:T(8,128)(2,1)S(1)} %collective-permute-done.4.refs_8_.refs_4_), channel_id=1, source_target_pairs={{0,1},{1,0},{2,3},{3,2},{4,5},{5,4},{6,7},{7,6},{8,9},{9,8},{10,11... | collective-permute-start | bytes 737288 | tf_op jit(solution)/shard_map/ppermute | solution.py:246
  37.2 3.6 %collective-permute-start.11 = (bf16[2,5,3,32,128]{4,3,2,1,0:T(8,128)(2,1)S(1)}, bf16[2,5,3,32,128]{4,3,2,1,0:T(8,128)(2,1)S(1)}, u32[]{:S(2)}, u32[]{:S(2)}) collective-permute-start(bf16[2,5,3,32,128]{4,3,2,1,0:T(8,128)(2,1)S(1)} %collective-permute-done.5.refs_9_.refs_5_), channel_id=1, source_target_pairs={{0,1},{1,0},{2,3},{3,2},{4,5},{5,4},{6,7},{7,6},{8,9},{9,8},{10,11... | collective-permute-start | bytes 737288 | tf_op jit(solution)/shard_map/ppermute | solution.py:246
  37.3 12.2 %collective-permute-start.16 = (bf16[128,640]{1,0:T(8,128)(2,1)S(1)}, bf16[128,640]{1,0:T(8,128)(2,1)S(1)}, u32[]{:S(2)}, u32[]{:S(2)}) collective-permute-start(bf16[128,640]{1,0:T(8,128)(2,1)S(1)} %get-tuple-element.77), channel_id=1, source_target_pairs={{0,2},{1,3},{2,0},{3,1},{4,6},{5,7},{6,4},{7,5},{8,10},{9,11},{10,... | collective-permute-start | bytes 491528 | tf_op jit(solution)/shard_map/ppermute | solution.py:246
  37.7 11.9 %collective-permute-start.17 = (bf16[128,640]{1,0:T(8,128)(2,1)S(1)}, bf16[128,640]{1,0:T(8,128)(2,1)S(1)}, u32[]{:S(2)}, u32[]{:S(2)}) collective-permute-start(bf16[128,640]{1,0:T(8,128)(2,1)S(1)} %get-tuple-element.78), channel_id=1, source_target_pairs={{0,4},{1,5},{2,6},{3,7},{4,0},{5,1},{6,2},{7,3},{8,12},{9,13},{10,... | collective-permute-start | bytes 491528 | tf_op jit(solution)/shard_map/ppermute | solution.py:246
  40.4 9.6 %collective-permute-start.18 = (bf16[128,640]{1,0:T(8,128)(2,1)S(1)}, bf16[128,640]{1,0:T(8,128)(2,1)S(1)}, u32[]{:S(2)}, u32[]{:S(2)}) collective-permute-start(bf16[128,640]{1,0:T(8,128)(2,1)S(1)} %get-tuple-element.79), channel_id=1, source_target_pairs={{0,6},{1,7},{2,4},{3,5},{4,2},{5,3},{6,0},{7,1},{8,14},{9,15},{10,... | collective-permute-start | bytes 491528 | tf_op jit(solution)/shard_map/ppermute | solution.py:246
  48.9 1.4 %collective-permute-start.12 = (bf16[512,128]{1,0:T(8,128)(2,1)S(1)}, bf16[512,128]{1,0:T(8,128)(2,1)S(1)}, u32[]{:S(2)}, u32[]{:S(2)}) collective-permute-start(bf16[512,128]{1,0:T(8,128)(2,1)S(1)} %get-tuple-element.72), channel_id=1, source_target_pairs={{0,1},{1,0},{2,3},{3,2},{4,5},{5,4},{6,7},{7,6},{8,9},{9,8},{10,11... | collective-permute-start | bytes 393224 | tf_op jit(solution)/shard_map/ppermute | solution.py:246
  49.0 1.5 %collective-permute-start.13 = (bf16[512,128]{1,0:T(8,128)(2,1)S(1)}, bf16[512,128]{1,0:T(8,128)(2,1)S(1)}, u32[]{:S(2)}, u32[]{:S(2)}) collective-permute-start(bf16[512,128]{1,0:T(8,128)(2,1)S(1)} %get-tuple-element.73), channel_id=1, source_target_pairs={{0,1},{1,0},{2,3},{3,2},{4,5},{5,4},{6,7},{7,6},{8,9},{9,8},{10,11... | collective-permute-start | bytes 393224 | tf_op jit(solution)/shard_map/ppermute | solution.py:246
  49.5 1.3 %collective-permute-start.14 = (bf16[512,128]{1,0:T(8,128)(2,1)S(1)}, bf16[512,128]{1,0:T(8,128)(2,1)S(1)}, u32[]{:S(2)}, u32[]{:S(2)}) collective-permute-start(bf16[512,128]{1,0:T(8,128)(2,1)S(1)} %get-tuple-element.74), channel_id=1, source_target_pairs={{0,1},{1,0},{2,3},{3,2},{4,5},{5,4},{6,7},{7,6},{8,9},{9,8},{10,11... | collective-permute-start | bytes 393224 | tf_op jit(solution)/shard_map/ppermute | solution.py:246
  49.6 1.5 %collective-permute-start.15 = (bf16[512,128]{1,0:T(8,128)(2,1)S(1)}, bf16[512,128]{1,0:T(8,128)(2,1)S(1)}, u32[]{:S(2)}, u32[]{:S(2)}) collective-permute-start(bf16[512,128]{1,0:T(8,128)(2,1)S(1)} %get-tuple-element.75), channel_id=1, source_target_pairs={{0,1},{1,0},{2,3},{3,2},{4,5},{5,4},{6,7},{7,6},{8,9},{9,8},{10,11... | collective-permute-start | bytes 393224 | tf_op jit(solution)/shard_map/ppermute | solution.py:246
  50.0 10.9 %collective-permute-start.23 = (bf16[4,512,128]{2,1,0:T(8,128)(2,1)S(1)}, bf16[4,512,128]{2,1,0:T(8,128)(2,1)S(1)}, u32[]{:S(2)}, u32[]{:S(2)}) collective-permute-start(bf16[4,512,128]{2,1,0:T(8,128)(2,1)S(1)} %get-tuple-element.100), channel_id=1, source_target_pairs={{0,1},{1,0},{2,3},{3,2},{4,5},{5,4},{6,7},{7,6},{8,9},{9,8},{10,11... | collective-permute-start | bytes 1572872 | tf_op jit(solution)/shard_map/ppermute | solution.py:246
  51.2 26.7 %collective-permute-start.20 = (bf16[4,512,128]{2,1,0:T(8,128)(2,1)S(1)}, bf16[4,512,128]{2,1,0:T(8,128)(2,1)S(1)}, u32[]{:S(2)}, u32[]{:S(2)}) collective-permute-start(bf16[4,512,128]{2,1,0:T(8,128)(2,1)S(1)} %add_convert_fusion), channel_id=1, source_target_pairs={{0,8},{1,9},{2,10},{3,11},{4,12},{5,13},{6,14},{7,15},{8,0},{9,1},... | collective-permute-start | bytes 1572872 | tf_op jit(solution)/shard_map/ppermute | solution.py:246
  58.2 11.7 %collective-permute-start.21 = (bf16[128,640]{1,0:T(8,128)(2,1)S(1)}, bf16[128,640]{1,0:T(8,128)(2,1)S(1)}, u32[]{:S(2)}, u32[]{:S(2)}) collective-permute-start(bf16[128,640]{1,0:T(8,128)(2,1)S(1)} %get-tuple-element.95), channel_id=1, source_target_pairs={{0,4},{1,5},{2,6},{3,7},{4,0},{5,1},{6,2},{7,3},{8,12},{9,13},{10,... | collective-permute-start | bytes 491528 | tf_op jit(solution)/shard_map/ppermute | solution.py:246
  60.2 12.6 %collective-permute-start.22 = (bf16[128,640]{1,0:T(8,128)(2,1)S(1)}, bf16[128,640]{1,0:T(8,128)(2,1)S(1)}, u32[]{:S(2)}, u32[]{:S(2)}) collective-permute-start(bf16[128,640]{1,0:T(8,128)(2,1)S(1)} %get-tuple-element.96), channel_id=1, source_target_pairs={{0,6},{1,7},{2,4},{3,5},{4,2},{5,3},{6,0},{7,1},{8,14},{9,15},{10,... | collective-permute-start | bytes 491528 | tf_op jit(solution)/shard_map/ppermute | solution.py:246
  80.9 19.3 %all-to-all-start = ((bf16[16,4,32,128]{3,2,1,0:T(8,128)(2,1)}), bf16[16,4,32,128]{3,2,1,0:T(8,128)(2,1)S(1)}, u32[]{:S(2)}, u32[]{:S(2)}) async-start(bf16[16,4,32,128]{3,2,1,0:T(8,128)(2,1)} %renew.1), calls=%async_computation | async-start | bytes 1048576 | tf_op jit(solution)/shard_map/all_to_all | solution.py:357
  85.7 10.9 %collective-permute-start.19 = (bf16[128,640]{1,0:T(8,128)(2,1)S(1)}, bf16[128,640]{1,0:T(8,128)(2,1)S(1)}, u32[]{:S(2)}, u32[]{:S(2)}) collective-permute-start(bf16[128,640]{1,0:T(8,128)(2,1)S(1)} %get-tuple-element.89), channel_id=1, source_target_pairs={{0,2},{1,3},{2,0},{3,1},{4,6},{5,7},{6,4},{7,5},{8,10},{9,11},{10,... | collective-permute-start | bytes 491528 | tf_op jit(solution)/shard_map/ppermute | solution.py:246

commit v7 on v6

--- a/solution.py
+++ b/solution.py
@@ -168,8 +168,13 @@
             owner = place ^ rel
             for apart in range(squares):
                 w = w_refs[2 * rel + apart // (squares // 2)]
-                to = (owner // 2 * squares + (spot ^ apart)) * 2 + owner % 2
+                to = device_of(owner, spot ^ apart, squares)
                 out_ref[to, slot] = w[apart % (squares // 2), number // 3, number % 3]
+
+
+def device_of(place, spot, squares):
+    up = place // 2
+    return (up * squares + (spot ^ up * (squares // 2))) * 2 + place % 2
 
 
 def renew_kernel(squares, mine_ref, far_ref, old_ref, out_ref, updates):
@@ -215,7 +220,7 @@
     for slot in range(slots):
         for owner in range(PLACES):
             for at in range(squares):
-                to = (owner // 2 * squares + at) * 2 + owner % 2
+                to = device_of(owner, at, squares)
                 rows_at = slice((owner * squares + at) * rows, (owner * squares + at + 1) * rows)
                 old = old_ref[to, slot].astype(jnp.float32)
                 out_ref[to, slot] = (old - updates[slot, rows_at, :]).astype(out_ref.dtype)
@@ -231,8 +236,10 @@
     hid = size * own_rows
     cut = squares // 2
     position = lax.axis_index("seq").astype(jnp.int32)
-    spot = position % half // 2
+    turn = squares // 2
+    spot = position % half // 2 ^ turn * (position // half)
     where = jnp.stack([spot, 2 * (position // half) + position % 2])
+    partner = half + 2 * turn
     params = pltpu.CompilerParams(vmem_limit_bytes=40 * 2**20)
     smem = pl.BlockSpec(memory_space=SMEM)
     vmem = pl.BlockSpec(memory_space=VMEM)
@@ -272,7 +279,7 @@
     )
     own = [jnp.stack(pieces[:cut]), jnp.stack(pieces[cut:])]
     own = list(lax.optimization_barrier(own))
-    other = [swap(w, half) for w in own]
+    other = [swap(w, partner) for w in own]
     late, moved[2:] = lax.optimization_barrier((other, moved[2:]))
     other, asking = lax.optimization_barrier((other, asking))
     asking = across(asking)
@@ -308,7 +315,7 @@
     far = [swap(one, 1) for one in far]
     far, asking = lax.optimization_barrier((far, asking))
     far = jnp.stack(far).astype(jnp.float32)
-    far = swap((sent + far).astype(jnp.bfloat16), half)
+    far = swap((sent + far).astype(jnp.bfloat16), partner)
 
     columns = pl.BlockSpec((row_count, head_size), lambda h: (0, h))
     parts = pl.pallas_call(
@@ -355,7 +362,9 @@
         name="renew",
     )(mine, far, old)
     back = lax.all_to_all(renewed, "seq", 0, 0, tiled=True)
-    back = back.reshape(2, squares, 2, slots, own_rows, head_size).transpose(1, 3, 0, 2, 4, 5)
+    back = back.reshape(2, squares, 2, slots, own_rows, head_size)
+    back = jnp.stack([back[0], jnp.roll(back[1], turn, axis=0)])
+    back = back.transpose(1, 3, 0, 2, 4, 5)
     back = back.reshape(squares, PLACES * slots, own_rows, head_size)[:, : 3 * heads]
     renewed_out = (
         back.reshape(squares, heads, 3, own_rows, head_size)

time: 101 us -> 99.3 us (0.983)
  waiting for transfers between devices: 50.2 us -> 48.7 us
    ppermute x24, waiting for transfers between devices: 48.1 us -> 46.6 us  [swap(): return lax.ppermute(array, 'seq', [(at, at ^ step) for at in range(size)])]
  transfers between devices with their start and end apart: 25 -> 25, of which waited for: 13 -> 14; matrix products, arithmetic and copies ran while one was open for 0% -> 0% of each run, Pallas kernels for 15% -> 15%
where the time goes in v7:
time: 99.3 us; the launch traced here: 99.1 us
  waiting for transfers between devices  48.7 us (49%)
  starting transfers between devices  28.4 us (29%)
  Pallas kernels  18.4 us (19%)
  local copies, waits for them, and re-layouts  2.24 us (2%)
    ppermute x24, waiting for transfers between devices, swap(): return lax.ppermute(array, 'seq', [(at, at ^ step) for at in range(size)])  46.6 us
    ppermute x24, starting transfers between devices, swap(): return lax.ppermute(array, 'seq', [(at, at ^ step) for at in range(size)])  24.1 us
    pallas_call x1, Pallas kernels, square_body(): pl.pallas_call(functools.partial(key_kernel, squares, heads), grid=(heads...  8.1 us
    all_to_all x1, starting transfers between devices, square_body(): back = lax.all_to_all(renewed, 'seq', 0, 0, tiled=True)  4.24 us
    pallas_call x1, Pallas kernels, square_body(): pl.pallas_call(functools.partial(query_kernel, squares), grid=(heads,), i...  4.06 us
    pallas_call x1, Pallas kernels, square_body(): pl.pallas_call(functools.partial(renew_kernel, squares), in_specs=[vmem]...  3.03 us
    all_to_all x1, waiting for transfers between devices, square_body(): back = lax.all_to_all(renewed, 'seq', 0, 0, tiled=True)  2.12 us
    unnamed x11, local copies, waits for them, and re-layouts  2.11 us
  transfers between devices with their start and end apart: 25, of which 14 were waited for; matrix products, arithmetic and copies ran while one was open for 0% of the time, Pallas kernels for 15%

profile of v7, /device:TPU:0, one launch (start us, length us, event | category | flops | bytes accessed | tf_op | source)
XLA Modules:
  0.0 99.1 jit_solution(10479161940983496025)
XLA Ops:
  0.7 1.2 %copy.10 = bf16[32,3,20,128]{3,0,1,2:T(8,128)(2,1)S(1)} copy(bf16[32,3,20,128]{3,0,2,1:T(8,128)(2,1)} %param.9) | data formatting | bytes 983040 | tf_op args[4]
  1.9 0.0 copy-start
  1.9 0.1 dynamic-slice_bitcast_fusion.1
  2.0 3.1 %collective-permute-start.2 = (bf16[5,3,32,128]{3,2,1,0:T(8,128)(2,1)S(1)}, bf16[5,3,32,128]{3,2,1,0:T(8,128)(2,1)S(1)}, u32[]{:S(2)}, u32[]{:S(2)}) collective-permute-start(bf16[5,3,32,128]{3,2,1,0:T(8,128)(2,1)S(1)} %get-tuple-element.114), channel_id=1, source_target_pairs={{0,4},{1,5},{2,6},{3,7},{4,0},{5,1},{6,2},{7,3},{8,12},{9,13},{10,... | collective-permute-start | bytes 368648 | tf_op jit(solution)/shard_map/ppermute | solution.py:253
  5.1 1.4 %collective-permute-start.3 = (bf16[5,3,32,128]{3,2,1,0:T(8,128)(2,1)S(1)}, bf16[5,3,32,128]{3,2,1,0:T(8,128)(2,1)S(1)}, u32[]{:S(2)}, u32[]{:S(2)}) collective-permute-start(bf16[5,3,32,128]{3,2,1,0:T(8,128)(2,1)S(1)} %get-tuple-element.115), channel_id=1, source_target_pairs={{0,6},{1,7},{2,4},{3,5},{4,2},{5,3},{6,0},{7,1},{8,14},{9,15},{10,... | collective-permute-start | bytes 368648 | tf_op jit(solution)/shard_map/ppermute | solution.py:253
  6.5 0.1 collective-permute-start.1
  6.6 0.1 pad_add_fusion.where_ref
  6.7 0.1 copy.9.rate_ref
  6.8 1.1 %split.1 = (bf16[2,128,640]{2,1,0:T(8,128)(2,1)S(1)}, bf16[2,128,640]{2,1,0:T(8,128)(2,1)S(1)}, bf16[2,128,640]{2,1,0:T(8,128)(2,1)S(1)}, bf16[2,128,640]{2,1,0:...) custom-call(s32[2]{0:T(128)S(1)} %pad_add_fusion.where_ref, ...), custom_call_target="tpu_custom_call" | custom-call | flops 10000000 | bytes 4000000 | tf_op jit(solution)/shard_map/split/pallas_call | solution.py:261
  7.9 2.0 %collective-permute-start.6 = (bf16[2,128,640]{2,1,0:T(8,128)(2,1)S(1)}, bf16[2,128,640]{2,1,0:T(8,128)(2,1)S(1)}, u32[]{:S(2)}, u32[]{:S(2)}) collective-permute-start(bf16[2,128,640]{2,1,0:T(8,128)(2,1)S(1)} %get-tuple-element.60), channel_id=1, source_target_pairs={{0,4},{1,5},{2,6},{3,7},{4,0},{5,1},{6,2},{7,3},{8,12},{9,13},{10,... | collective-permute-start | bytes 983048 | tf_op jit(solution)/shard_map/ppermute | solution.py:253
  9.9 1.4 %collective-permute-start.7 = (bf16[2,128,640]{2,1,0:T(8,128)(2,1)S(1)}, bf16[2,128,640]{2,1,0:T(8,128)(2,1)S(1)}, u32[]{:S(2)}, u32[]{:S(2)}) collective-permute-start(bf16[2,128,640]{2,1,0:T(8,128)(2,1)S(1)} %get-tuple-element.61), channel_id=1, source_target_pairs={{0,6},{1,7},{2,4},{3,5},{4,2},{5,3},{6,0},{7,1},{8,14},{9,15},{10,... | collective-permute-start | bytes 983048 | tf_op jit(solution)/shard_map/ppermute | solution.py:253
  11.3 0.0 collective-permute-done.2
  11.3 2.0 %collective-permute-done.3 = bf16[5,3,32,128]{3,2,1,0:T(8,128)(2,1)S(1)} collective-permute-done((bf16[5,3,32,128]{3,2,1,0:T(8,128)(2,1)S(1)}, bf16[5,3,32,128]{3,2,1,0:T(8,128)(2,1)S(1)}, u32[]{:S(2)}, u32[]{:S(2)}) %collective-permute-start.3) | collective-permute-done | bytes 122912 | tf_op jit(solution)/shard_map/ppermute | solution.py:253
  13.3 0.3 collective-permute-done.1
  13.6 3.7 %collective-permute-start.4 = (bf16[2,5,3,32,128]{4,3,2,1,0:T(8,128)(2,1)S(1)}, bf16[2,5,3,32,128]{4,3,2,1,0:T(8,128)(2,1)S(1)}, u32[]{:S(2)}, u32[]{:S(2)}) collective-permute-start(bf16[2,5,3,32,128]{4,3,2,1,0:T(8,128)(2,1)S(1)} %pad_maximum_fusion.2.refs_4_.refs_0_), channel_id=1, source_target_pairs={{0,12},{1,13},{2,14},{3,15},{4,8},{5,9},{6,10},{7,11},{8,4},{9,5},... | collective-permute-start | bytes 737288 | tf_op jit(solution)/shard_map/ppermute | solution.py:253
  17.3 0.2 collective-permute-start.5
  17.5 0.4 collective-permute-start
  17.9 1.3 %collective-permute-done.6.refs_2_ = bf16[2,128,640]{2,1,0:T(8,128)(2,1)S(1)} collective-permute-done((bf16[2,128,640]{2,1,0:T(8,128)(2,1)S(1)}, bf16[2,128,640]{2,1,0:T(8,128)(2,1)S(1)}, u32[]{:S(2)}, u32[]{:S(2)}) %collective-permute-start.6) | collective-permute-done | bytes 327712 | tf_op jit(solution)/shard_map/ppermute | solution.py:253
  19.3 0.0 collective-permute-start.8
  19.3 7.0 %collective-permute-done.7.refs_3_ = bf16[2,128,640]{2,1,0:T(8,128)(2,1)S(1)} collective-permute-done((bf16[2,128,640]{2,1,0:T(8,128)(2,1)S(1)}, bf16[2,128,640]{2,1,0:T(8,128)(2,1)S(1)}, u32[]{:S(2)}, u32[]{:S(2)}) %collective-permute-start.7) | collective-permute-done | bytes 327712 | tf_op jit(solution)/shard_map/ppermute | solution.py:253
  26.3 0.0 collective-permute-start.9
  26.3 7.4 %collective-permute-done.4.refs_8_.refs_4_ = bf16[2,5,3,32,128]{4,3,2,1,0:T(8,128)(2,1)S(1)} collective-permute-done((bf16[2,5,3,32,128]{4,3,2,1,0:T(8,128)(2,1)S(1)}, bf16[2,5,3,32,128]{4,3,2,1,0:T(8,128)(2,1)S(1)}, u32[]{:S(2)}, u32[]{:S(2)}) %collective-permute-start.4) | collective-permute-done | bytes 245792 | tf_op jit(solution)/shard_map/ppermute | solution.py:253
  33.7 4.2 %collective-permute-done.5.refs_9_.refs_5_ = bf16[2,5,3,32,128]{4,3,2,1,0:T(8,128)(2,1)S(1)} collective-permute-done((bf16[2,5,3,32,128]{4,3,2,1,0:T(8,128)(2,1)S(1)}, bf16[2,5,3,32,128]{4,3,2,1,0:T(8,128)(2,1)S(1)}, u32[]{:S(2)}, u32[]{:S(2)}) %collective-permute-start.5) | collective-permute-done | bytes 245792 | tf_op jit(solution)/shard_map/ppermute | solution.py:253
  37.9 0.0 collective-permute-start.10
  37.9 0.5 collective-permute-start.11
  38.4 0.0 collective-permute-done.refs_1_
  38.4 1.5 %collective-permute-start.16 = (bf16[128,640]{1,0:T(8,128)(2,1)S(1)}, bf16[128,640]{1,0:T(8,128)(2,1)S(1)}, u32[]{:S(2)}, u32[]{:S(2)}) collective-permute-start(bf16[128,640]{1,0:T(8,128)(2,1)S(1)} %get-tuple-element.77), channel_id=1, source_target_pairs={{0,2},{1,3},{2,0},{3,1},{4,6},{5,7},{6,4},{7,5},{8,10},{9,11},{10,... | collective-permute-start | bytes 491528 | tf_op jit(solution)/shard_map/ppermute | solution.py:253
  39.9 0.0 collective-permute-done.8.refs_6_.refs_2_
  39.9 0.0 collective-permute-start.17
  39.9 0.0 collective-permute-done.9.refs_7_.refs_3_
  39.9 2.0 %collective-permute-start.18 = (bf16[128,640]{1,0:T(8,128)(2,1)S(1)}, bf16[128,640]{1,0:T(8,128)(2,1)S(1)}, u32[]{:S(2)}, u32[]{:S(2)}) collective-permute-start(bf16[128,640]{1,0:T(8,128)(2,1)S(1)} %get-tuple-element.79), channel_id=1, source_target_pairs={{0,6},{1,7},{2,4},{3,5},{4,2},{5,3},{6,0},{7,1},{8,14},{9,15},{10,... | collective-permute-start | bytes 491528 | tf_op jit(solution)/shard_map/ppermute | solution.py:253
  41.9 0.0 collective-permute-done.10.refs_10_.refs_6_
  41.9 0.0 collective-permute-done.11.refs_11_.refs_7_
  41.9 8.1 %key_side.1 = (f32[4,512,128]{2,1,0:T(8,128)S(1)}, f32[4,512,128]{2,1,0:T(8,128)S(1)}, bf16[4,512,128]{2,1,0:T(8,128)(2,1)S(1)}, bf16[512,128]{1,0:T(8,128)(2,1)...) custom-call(s32[2]{0:T(128)S(1)} %pad_add_fusion.where_ref, ...), custom_call_target="tpu_custom_call" | custom-call | flops 2000000000 | bytes 4000000 | tf_op jit(solution)/shard_map/key_side/pallas_call | solution.py:293
  50.0 0.1 collective-permute-start.12
  50.1 0.5 collective-permute-start.13
  50.6 0.0 collective-permute-done.16.refs_1_
  50.6 0.1 collective-permute-start.14
  50.6 0.0 collective-permute-done.17.refs_2_
  50.7 0.4 collective-permute-start.15
  51.1 0.0 collective-permute-done.18.refs_3_
  51.1 0.1 collective-permute-start.23
  51.2 0.2 collective-permute-done.12
  51.4 0.2 collective-permute-done.13
  51.6 0.3 collective-permute-done.14
  51.9 0.2 collective-permute-done.15
  52.1 0.1 add_convert_fusion
  52.3 2.6 %collective-permute-start.20 = (bf16[4,512,128]{2,1,0:T(8,128)(2,1)S(1)}, bf16[4,512,128]{2,1,0:T(8,128)(2,1)S(1)}, u32[]{:S(2)}, u32[]{:S(2)}) collective-permute-start(bf16[4,512,128]{2,1,0:T(8,128)(2,1)S(1)} %add_convert_fusion), channel_id=1, source_target_pairs={{0,12},{1,13},{2,14},{3,15},{4,8},{5,9},{6,10},{7,11},{8,4},{9,5},... | collective-permute-start | bytes 1572872 | tf_op jit(solution)/shard_map/ppermute | solution.py:253
  54.9 4.1 %query_side.1 = (bf16[128,640]{1,0:T(8,128)(2,1)S(1)}, bf16[128,640]{1,0:T(8,128)(2,1)S(1)}, bf16[128,640]{1,0:T(8,128)(2,1)S(1)}, bf16[128,640]{1,0:T(8,128)(2,1)S(1)}) custom-call(bf16[128,640]{1,0:T(8,128)(2,1)S(1)} %get-tuple-element.80.refs_0_, bf16[128,640]{1,0:T(8,128)(2,1)S(1)} %collective-permute-done.16.refs_1_, ...), custom_call_target="tpu_custom_call" | custom-call | flops 1000000000 | bytes 4000000 | tf_op jit(solution)/shard_map/query_side/pallas_call | solution.py:321
  59.0 0.1 collective-permute-start.21
  59.0 2.0 %collective-permute-start.22 = (bf16[128,640]{1,0:T(8,128)(2,1)S(1)}, bf16[128,640]{1,0:T(8,128)(2,1)S(1)}, u32[]{:S(2)}, u32[]{:S(2)}) collective-permute-start(bf16[128,640]{1,0:T(8,128)(2,1)S(1)} %get-tuple-element.96), channel_id=1, source_target_pairs={{0,6},{1,7},{2,4},{3,5},{4,2},{5,3},{6,0},{7,1},{8,14},{9,15},{10,... | collective-permute-start | bytes 491528 | tf_op jit(solution)/shard_map/ppermute | solution.py:253
  61.0 0.7 pick.1.old_ref
  61.7 0.0 collective-permute-done.23
  61.7 0.1 convert_add_fusion.mine_ref
  61.8 10.2 %collective-permute-done.21.refs_2_ = bf16[128,640]{1,0:T(8,128)(2,1)S(1)} collective-permute-done((bf16[128,640]{1,0:T(8,128)(2,1)S(1)}, bf16[128,640]{1,0:T(8,128)(2,1)S(1)}, u32[]{:S(2)}, u32[]{:S(2)}) %collective-permute-start.21) | collective-permute-done | bytes 163872 | tf_op jit(solution)/shard_map/ppermute | solution.py:253
  72.0 4.3 %collective-permute-done.22.refs_3_ = bf16[128,640]{1,0:T(8,128)(2,1)S(1)} collective-permute-done((bf16[128,640]{1,0:T(8,128)(2,1)S(1)}, bf16[128,640]{1,0:T(8,128)(2,1)S(1)}, u32[]{:S(2)}, u32[]{:S(2)}) %collective-permute-start.22) | collective-permute-done | bytes 163872 | tf_op jit(solution)/shard_map/ppermute | solution.py:253
  76.3 0.0 collective-permute-done.20.far_ref
  76.3 3.0 %renew.1 = bf16[16,4,32,128]{3,2,1,0:T(8,128)(2,1)} custom-call(f32[4,512,128]{2,1,0:T(8,128)S(1)} %convert_add_fusion.mine_ref, bf16[4,512,128]{2,1,0:T(8,128)(2,1)S(1)} %collective-permute-done.20.far_ref, bf16[16,4,32,128]{3,2,1,0:T(8,128)(2,1)S(1)} %pick.1.old_ref), custom_call_target="tpu_custom_call" | custom-call | flops 2000000000 | bytes 4000000 | tf_op jit(solution)/shard_map/renew/pallas_call | solution.py:354
  79.3 4.2 %all-to-all-start = ((bf16[16,4,32,128]{3,2,1,0:T(8,128)(2,1)}), bf16[16,4,32,128]{3,2,1,0:T(8,128)(2,1)S(1)}, u32[]{:S(2)}, u32[]{:S(2)}) async-start(bf16[16,4,32,128]{3,2,1,0:T(8,128)(2,1)} %renew.1), calls=%async_computation | async-start | bytes 1048576 | tf_op jit(solution)/shard_map/all_to_all | solution.py:364
  83.6 1.9 %collective-permute-start.19 = (bf16[128,640]{1,0:T(8,128)(2,1)S(1)}, bf16[128,640]{1,0:T(8,128)(2,1)S(1)}, u32[]{:S(2)}, u32[]{:S(2)}) collective-permute-start(bf16[128,640]{1,0:T(8,128)(2,1)S(1)} %get-tuple-element.89), channel_id=1, source_target_pairs={{0,2},{1,3},{2,0},{3,1},{4,6},{5,7},{6,4},{7,5},{8,10},{9,11},{10,... | collective-permute-start | bytes 491528 | tf_op jit(solution)/shard_map/ppermute | solution.py:253
  85.5 9.0 %collective-permute-done.19.refs_1_ = bf16[128,640]{1,0:T(8,128)(2,1)S(1)} collective-permute-done((bf16[128,640]{1,0:T(8,128)(2,1)S(1)}, bf16[128,640]{1,0:T(8,128)(2,1)S(1)}, u32[]{:S(2)}, u32[]{:S(2)}) %collective-permute-start.19) | collective-permute-done | bytes 163872 | tf_op jit(solution)/shard_map/ppermute | solution.py:253
  94.5 1.4 %join.1 = bf16[128,2560]{1,0:T(8,128)(2,1)} custom-call(s32[2]{0:T(128)S(1)} %pad_add_fusion.where_ref, bf16[128,640]{1,0:T(8,128)(2,1)S(1)} %get-tuple-element.88.refs_0_, bf16[128,640]{1,0:T(8,128)(2,1)S(1)} %collective-permute-done.19.refs_1_, bf16[128,640]{1,0:T(8,128)(2,1)S(1)} %collective-permute-done.21.refs_2_, ...), custom_call_target="tpu_custom_call" | custom-call | flops 10000000 | bytes 4000000 | tf_op jit(solution)/shard_map/join/pallas_call | solution.py:335
  95.9 2.1 %all-to-all-done = bf16[16,4,32,128]{3,2,1,0:T(8,128)(2,1)S(1)} async-done(((bf16[16,4,32,128]{3,2,1,0:T(8,128)(2,1)}), bf16[16,4,32,128]{3,2,1,0:T(8,128)(2,1)S(1)}, u32[]{:S(2)}, u32[]{:S(2)}) %all-to-all-start) | async-done | bytes 524320 | tf_op jit(solution)/shard_map/all_to_all | solution.py:364
  98.2 0.8 copy.14
  (14 shorter events, 0.2 us)
Async XLA Ops:
  0.7 6.1 %copy-start.1 = (bf16[128,2560]{1,0:T(8,128)(2,1)S(1)}, bf16[128,2560]{1,0:T(8,128)(2,1)}, u32[]{:S(2)}) copy-start(bf16[128,2560]{1,0:T(8,128)(2,1)} %k_ref.1) | copy-start | bytes 1966084
  0.7 6.1 %copy-start.2 = (bf16[128,2560]{1,0:T(8,128)(2,1)S(1)}, bf16[128,2560]{1,0:T(8,128)(2,1)}, u32[]{:S(2)}) copy-start(bf16[128,2560]{1,0:T(8,128)(2,1)} %v_ref.1) | copy-start | bytes 1966084
  1.9 4.9 %copy-start = (bf16[128,2560]{1,0:T(8,128)(2,1)S(1)}, bf16[128,2560]{1,0:T(8,128)(2,1)}, u32[]{:S(2)}) copy-start(bf16[128,2560]{1,0:T(8,128)(2,1)} %q_ref.1) | copy-start | bytes 1966084
  2.0 9.4 %collective-permute-start.2 = (bf16[5,3,32,128]{3,2,1,0:T(8,128)(2,1)S(1)}, bf16[5,3,32,128]{3,2,1,0:T(8,128)(2,1)S(1)}, u32[]{:S(2)}, u32[]{:S(2)}) collective-permute-start(bf16[5,3,32,128]{3,2,1,0:T(8,128)(2,1)S(1)} %get-tuple-element.114), channel_id=1, source_target_pairs={{0,4},{1,5},{2,6},{3,7},{4,0},{5,1},{6,2},{7,3},{8,12},{9,13},{10,... | collective-permute-start | bytes 368648 | tf_op jit(solution)/shard_map/ppermute | solution.py:253
  5.1 1.6 %copy-start.3 = (f32[128,20]{0,1:T(8,128)S(1)}, f32[128,20]{0,1:T(8,128)}, u32[]{:S(2)}) copy-start(f32[128,20]{0,1:T(8,128)} %param.8) | copy-start | bytes 30724
  5.1 8.2 %collective-permute-start.3 = (bf16[5,3,32,128]{3,2,1,0:T(8,128)(2,1)S(1)}, bf16[5,3,32,128]{3,2,1,0:T(8,128)(2,1)S(1)}, u32[]{:S(2)}, u32[]{:S(2)}) collective-permute-start(bf16[5,3,32,128]{3,2,1,0:T(8,128)(2,1)S(1)} %get-tuple-element.115), channel_id=1, source_target_pairs={{0,6},{1,7},{2,4},{3,5},{4,2},{5,3},{6,0},{7,1},{8,14},{9,15},{10,... | collective-permute-start | bytes 368648 | tf_op jit(solution)/shard_map/ppermute | solution.py:253
  6.5 7.1 %collective-permute-start.1 = (bf16[5,3,32,128]{3,2,1,0:T(8,128)(2,1)S(1)}, bf16[5,3,32,128]{3,2,1,0:T(8,128)(2,1)S(1)}, u32[]{:S(2)}, u32[]{:S(2)}) collective-permute-start(bf16[5,3,32,128]{3,2,1,0:T(8,128)(2,1)S(1)} %get-tuple-element.116), channel_id=1, source_target_pairs={{0,2},{1,3},{2,0},{3,1},{4,6},{5,7},{6,4},{7,5},{8,10},{9,11},{10,... | collective-permute-start | bytes 368648 | tf_op jit(solution)/shard_map/ppermute | solution.py:253
  7.9 11.4 %collective-permute-start.6 = (bf16[2,128,640]{2,1,0:T(8,128)(2,1)S(1)}, bf16[2,128,640]{2,1,0:T(8,128)(2,1)S(1)}, u32[]{:S(2)}, u32[]{:S(2)}) collective-permute-start(bf16[2,128,640]{2,1,0:T(8,128)(2,1)S(1)} %get-tuple-element.60), channel_id=1, source_target_pairs={{0,4},{1,5},{2,6},{3,7},{4,0},{5,1},{6,2},{7,3},{8,12},{9,13},{10,... | collective-permute-start | bytes 983048 | tf_op jit(solution)/shard_map/ppermute | solution.py:253
  9.9 16.4 %collective-permute-start.7 = (bf16[2,128,640]{2,1,0:T(8,128)(2,1)S(1)}, bf16[2,128,640]{2,1,0:T(8,128)(2,1)S(1)}, u32[]{:S(2)}, u32[]{:S(2)}) collective-permute-start(bf16[2,128,640]{2,1,0:T(8,128)(2,1)S(1)} %get-tuple-element.61), channel_id=1, source_target_pairs={{0,6},{1,7},{2,4},{3,5},{4,2},{5,3},{6,0},{7,1},{8,14},{9,15},{10,... | collective-permute-start | bytes 983048 | tf_op jit(solution)/shard_map/ppermute | solution.py:253
  13.6 20.1 %collective-permute-start.4 = (bf16[2,5,3,32,128]{4,3,2,1,0:T(8,128)(2,1)S(1)}, bf16[2,5,3,32,128]{4,3,2,1,0:T(8,128)(2,1)S(1)}, u32[]{:S(2)}, u32[]{:S(2)}) collective-permute-start(bf16[2,5,3,32,128]{4,3,2,1,0:T(8,128)(2,1)S(1)} %pad_maximum_fusion.2.refs_4_.refs_0_), channel_id=1, source_target_pairs={{0,12},{1,13},{2,14},{3,15},{4,8},{5,9},{6,10},{7,11},{8,4},{9,5},... | collective-permute-start | bytes 737288 | tf_op jit(solution)/shard_map/ppermute | solution.py:253
  17.3 20.6 %collective-permute-start.5 = (bf16[2,5,3,32,128]{4,3,2,1,0:T(8,128)(2,1)S(1)}, bf16[2,5,3,32,128]{4,3,2,1,0:T(8,128)(2,1)S(1)}, u32[]{:S(2)}, u32[]{:S(2)}) collective-permute-start(bf16[2,5,3,32,128]{4,3,2,1,0:T(8,128)(2,1)S(1)} %pad_maximum_fusion.3.refs_5_.refs_1_), channel_id=1, source_target_pairs={{0,12},{1,13},{2,14},{3,15},{4,8},{5,9},{6,10},{7,11},{8,4},{9,5},... | collective-permute-start | bytes 737288 | tf_op jit(solution)/shard_map/ppermute | solution.py:253
  17.5 20.9 %collective-permute-start = (bf16[2,128,640]{2,1,0:T(8,128)(2,1)S(1)}, bf16[2,128,640]{2,1,0:T(8,128)(2,1)S(1)}, u32[]{:S(2)}, u32[]{:S(2)}) collective-permute-start(bf16[2,128,640]{2,1,0:T(8,128)(2,1)S(1)} %get-tuple-element.57), channel_id=1, source_target_pairs={{0,2},{1,3},{2,0},{3,1},{4,6},{5,7},{6,4},{7,5},{8,10},{9,11},{10,... | collective-permute-start | bytes 983048 | tf_op jit(solution)/shard_map/ppermute | solution.py:253
  19.3 20.6 %collective-permute-start.8 = (bf16[2,5,3,32,128]{4,3,2,1,0:T(8,128)(2,1)S(1)}, bf16[2,5,3,32,128]{4,3,2,1,0:T(8,128)(2,1)S(1)}, u32[]{:S(2)}, u32[]{:S(2)}) collective-permute-start(bf16[2,5,3,32,128]{4,3,2,1,0:T(8,128)(2,1)S(1)} %pad_maximum_fusion.2.refs_4_.refs_0_), channel_id=1, source_target_pairs={{0,1},{1,0},{2,3},{3,2},{4,5},{5,4},{6,7},{7,6},{8,9},{9,8},{10,11... | collective-permute-start | bytes 737288 | tf_op jit(solution)/shard_map/ppermute | solution.py:253
  26.3 13.6 %collective-permute-start.9 = (bf16[2,5,3,32,128]{4,3,2,1,0:T(8,128)(2,1)S(1)}, bf16[2,5,3,32,128]{4,3,2,1,0:T(8,128)(2,1)S(1)}, u32[]{:S(2)}, u32[]{:S(2)}) collective-permute-start(bf16[2,5,3,32,128]{4,3,2,1,0:T(8,128)(2,1)S(1)} %pad_maximum_fusion.3.refs_5_.refs_1_), channel_id=1, source_target_pairs={{0,1},{1,0},{2,3},{3,2},{4,5},{5,4},{6,7},{7,6},{8,9},{9,8},{10,11... | collective-permute-start | bytes 737288 | tf_op jit(solution)/shard_map/ppermute | solution.py:253
  37.9 4.0 %collective-permute-start.10 = (bf16[2,5,3,32,128]{4,3,2,1,0:T(8,128)(2,1)S(1)}, bf16[2,5,3,32,128]{4,3,2,1,0:T(8,128)(2,1)S(1)}, u32[]{:S(2)}, u32[]{:S(2)}) collective-permute-start(bf16[2,5,3,32,128]{4,3,2,1,0:T(8,128)(2,1)S(1)} %collective-permute-done.4.refs_8_.refs_4_), channel_id=1, source_target_pairs={{0,1},{1,0},{2,3},{3,2},{4,5},{5,4},{6,7},{7,6},{8,9},{9,8},{10,11... | collective-permute-start | bytes 737288 | tf_op jit(solution)/shard_map/ppermute | solution.py:253
  37.9 4.0 %collective-permute-start.11 = (bf16[2,5,3,32,128]{4,3,2,1,0:T(8,128)(2,1)S(1)}, bf16[2,5,3,32,128]{4,3,2,1,0:T(8,128)(2,1)S(1)}, u32[]{:S(2)}, u32[]{:S(2)}) collective-permute-start(bf16[2,5,3,32,128]{4,3,2,1,0:T(8,128)(2,1)S(1)} %collective-permute-done.5.refs_9_.refs_5_), channel_id=1, source_target_pairs={{0,1},{1,0},{2,3},{3,2},{4,5},{5,4},{6,7},{7,6},{8,9},{9,8},{10,11... | collective-permute-start | bytes 737288 | tf_op jit(solution)/shard_map/ppermute | solution.py:253
  38.4 12.2 %collective-permute-start.16 = (bf16[128,640]{1,0:T(8,128)(2,1)S(1)}, bf16[128,640]{1,0:T(8,128)(2,1)S(1)}, u32[]{:S(2)}, u32[]{:S(2)}) collective-permute-start(bf16[128,640]{1,0:T(8,128)(2,1)S(1)} %get-tuple-element.77), channel_id=1, source_target_pairs={{0,2},{1,3},{2,0},{3,1},{4,6},{5,7},{6,4},{7,5},{8,10},{9,11},{10,... | collective-permute-start | bytes 491528 | tf_op jit(solution)/shard_map/ppermute | solution.py:253
  39.9 10.8 %collective-permute-start.17 = (bf16[128,640]{1,0:T(8,128)(2,1)S(1)}, bf16[128,640]{1,0:T(8,128)(2,1)S(1)}, u32[]{:S(2)}, u32[]{:S(2)}) collective-permute-start(bf16[128,640]{1,0:T(8,128)(2,1)S(1)} %get-tuple-element.78), channel_id=1, source_target_pairs={{0,4},{1,5},{2,6},{3,7},{4,0},{5,1},{6,2},{7,3},{8,12},{9,13},{10,... | collective-permute-start | bytes 491528 | tf_op jit(solution)/shard_map/ppermute | solution.py:253
  39.9 11.2 %collective-permute-start.18 = (bf16[128,640]{1,0:T(8,128)(2,1)S(1)}, bf16[128,640]{1,0:T(8,128)(2,1)S(1)}, u32[]{:S(2)}, u32[]{:S(2)}) collective-permute-start(bf16[128,640]{1,0:T(8,128)(2,1)S(1)} %get-tuple-element.79), channel_id=1, source_target_pairs={{0,6},{1,7},{2,4},{3,5},{4,2},{5,3},{6,0},{7,1},{8,14},{9,15},{10,... | collective-permute-start | bytes 491528 | tf_op jit(solution)/shard_map/ppermute | solution.py:253
  50.0 1.4 %collective-permute-start.12 = (bf16[512,128]{1,0:T(8,128)(2,1)S(1)}, bf16[512,128]{1,0:T(8,128)(2,1)S(1)}, u32[]{:S(2)}, u32[]{:S(2)}) collective-permute-start(bf16[512,128]{1,0:T(8,128)(2,1)S(1)} %get-tuple-element.72), channel_id=1, source_target_pairs={{0,1},{1,0},{2,3},{3,2},{4,5},{5,4},{6,7},{7,6},{8,9},{9,8},{10,11... | collective-permute-start | bytes 393224 | tf_op jit(solution)/shard_map/ppermute | solution.py:253
  50.1 1.5 %collective-permute-start.13 = (bf16[512,128]{1,0:T(8,128)(2,1)S(1)}, bf16[512,128]{1,0:T(8,128)(2,1)S(1)}, u32[]{:S(2)}, u32[]{:S(2)}) collective-permute-start(bf16[512,128]{1,0:T(8,128)(2,1)S(1)} %get-tuple-element.73), channel_id=1, source_target_pairs={{0,1},{1,0},{2,3},{3,2},{4,5},{5,4},{6,7},{7,6},{8,9},{9,8},{10,11... | collective-permute-start | bytes 393224 | tf_op jit(solution)/shard_map/ppermute | solution.py:253
  50.6 1.3 %collective-permute-start.14 = (bf16[512,128]{1,0:T(8,128)(2,1)S(1)}, bf16[512,128]{1,0:T(8,128)(2,1)S(1)}, u32[]{:S(2)}, u32[]{:S(2)}) collective-permute-start(bf16[512,128]{1,0:T(8,128)(2,1)S(1)} %get-tuple-element.74), channel_id=1, source_target_pairs={{0,1},{1,0},{2,3},{3,2},{4,5},{5,4},{6,7},{7,6},{8,9},{9,8},{10,11... | collective-permute-start | bytes 393224 | tf_op jit(solution)/shard_map/ppermute | solution.py:253
  50.7 1.5 %collective-permute-start.15 = (bf16[512,128]{1,0:T(8,128)(2,1)S(1)}, bf16[512,128]{1,0:T(8,128)(2,1)S(1)}, u32[]{:S(2)}, u32[]{:S(2)}) collective-permute-start(bf16[512,128]{1,0:T(8,128)(2,1)S(1)} %get-tuple-element.75), channel_id=1, source_target_pairs={{0,1},{1,0},{2,3},{3,2},{4,5},{5,4},{6,7},{7,6},{8,9},{9,8},{10,11... | collective-permute-start | bytes 393224 | tf_op jit(solution)/shard_map/ppermute | solution.py:253
  51.1 10.6 %collective-permute-start.23 = (bf16[4,512,128]{2,1,0:T(8,128)(2,1)S(1)}, bf16[4,512,128]{2,1,0:T(8,128)(2,1)S(1)}, u32[]{:S(2)}, u32[]{:S(2)}) collective-permute-start(bf16[4,512,128]{2,1,0:T(8,128)(2,1)S(1)} %get-tuple-element.100), channel_id=1, source_target_pairs={{0,1},{1,0},{2,3},{3,2},{4,5},{5,4},{6,7},{7,6},{8,9},{9,8},{10,11... | collective-permute-start | bytes 1572872 | tf_op jit(solution)/shard_map/ppermute | solution.py:253
  52.3 24.1 %collective-permute-start.20 = (bf16[4,512,128]{2,1,0:T(8,128)(2,1)S(1)}, bf16[4,512,128]{2,1,0:T(8,128)(2,1)S(1)}, u32[]{:S(2)}, u32[]{:S(2)}) collective-permute-start(bf16[4,512,128]{2,1,0:T(8,128)(2,1)S(1)} %add_convert_fusion), channel_id=1, source_target_pairs={{0,12},{1,13},{2,14},{3,15},{4,8},{5,9},{6,10},{7,11},{8,4},{9,5},... | collective-permute-start | bytes 1572872 | tf_op jit(solution)/shard_map/ppermute | solution.py:253
  59.0 13.0 %collective-permute-start.21 = (bf16[128,640]{1,0:T(8,128)(2,1)S(1)}, bf16[128,640]{1,0:T(8,128)(2,1)S(1)}, u32[]{:S(2)}, u32[]{:S(2)}) collective-permute-start(bf16[128,640]{1,0:T(8,128)(2,1)S(1)} %get-tuple-element.95), channel_id=1, source_target_pairs={{0,4},{1,5},{2,6},{3,7},{4,0},{5,1},{6,2},{7,3},{8,12},{9,13},{10,... | collective-permute-start | bytes 491528 | tf_op jit(solution)/shard_map/ppermute | solution.py:253
  59.0 17.3 %collective-permute-start.22 = (bf16[128,640]{1,0:T(8,128)(2,1)S(1)}, bf16[128,640]{1,0:T(8,128)(2,1)S(1)}, u32[]{:S(2)}, u32[]{:S(2)}) collective-permute-start(bf16[128,640]{1,0:T(8,128)(2,1)S(1)} %get-tuple-element.96), channel_id=1, source_target_pairs={{0,6},{1,7},{2,4},{3,5},{4,2},{5,3},{6,0},{7,1},{8,14},{9,15},{10,... | collective-permute-start | bytes 491528 | tf_op jit(solution)/shard_map/ppermute | solution.py:253
  79.3 18.7 %all-to-all-start = ((bf16[16,4,32,128]{3,2,1,0:T(8,128)(2,1)}), bf16[16,4,32,128]{3,2,1,0:T(8,128)(2,1)S(1)}, u32[]{:S(2)}, u32[]{:S(2)}) async-start(bf16[16,4,32,128]{3,2,1,0:T(8,128)(2,1)} %renew.1), calls=%async_computation | async-start | bytes 1048576 | tf_op jit(solution)/shard_map/all_to_all | solution.py:364
  83.6 10.9 %collective-permute-start.19 = (bf16[128,640]{1,0:T(8,128)(2,1)S(1)}, bf16[128,640]{1,0:T(8,128)(2,1)S(1)}, u32[]{:S(2)}, u32[]{:S(2)}) collective-permute-start(bf16[128,640]{1,0:T(8,128)(2,1)S(1)} %get-tuple-element.89), channel_id=1, source_target_pairs={{0,2},{1,3},{2,0},{3,1},{4,6},{5,7},{6,4},{7,5},{8,10},{9,11},{10,... | collective-permute-start | bytes 491528 | tf_op jit(solution)/shard_map/ppermute | solution.py:253

commit v8 on v7

--- a/solution.py
+++ b/solution.py
@@ -281,7 +281,7 @@
     own = list(lax.optimization_barrier(own))
     other = [swap(w, partner) for w in own]
     late, moved[2:] = lax.optimization_barrier((other, moved[2:]))
-    other, asking = lax.optimization_barrier((other, asking))
+    moved[2:], asking = lax.optimization_barrier((moved[2:], asking))
     asking = across(asking)
     weights = [own, [swap(w, 1) for w in own], other, [swap(w, 1) for w in late]]
     weights = [w for pair in weights for w in pair]

time: 99.3 us -> 99.3 us (level)
  no operation moved by 1% of the time
where the time goes in v8:
time: 99.3 us; the launch traced here: 99.1 us
  waiting for transfers between devices  48.7 us (49%)
  starting transfers between devices  28.4 us (29%)
  Pallas kernels  18.4 us (19%)
  local copies, waits for them, and re-layouts  2.24 us (2%)
    ppermute x24, waiting for transfers between devices, swap(): return lax.ppermute(array, 'seq', [(at, at ^ step) for at in range(size)])  46.6 us
    ppermute x24, starting transfers between devices, swap(): return lax.ppermute(array, 'seq', [(at, at ^ step) for at in range(size)])  24.1 us
    pallas_call x1, Pallas kernels, square_body(): pl.pallas_call(functools.partial(key_kernel, squares, heads), grid=(heads...  8.1 us
    all_to_all x1, starting transfers between devices, square_body(): back = lax.all_to_all(renewed, 'seq', 0, 0, tiled=True)  4.24 us
    pallas_call x1, Pallas kernels, square_body(): pl.pallas_call(functools.partial(query_kernel, squares), grid=(heads,), i...  4.06 us
    pallas_call x1, Pallas kernels, square_body(): pl.pallas_call(functools.partial(renew_kernel, squares), in_specs=[vmem]...  3.03 us
    all_to_all x1, waiting for transfers between devices, square_body(): back = lax.all_to_all(renewed, 'seq', 0, 0, tiled=True)  2.12 us
    unnamed x11, local copies, waits for them, and re-layouts  2.11 us
  transfers between devices with their start and end apart: 25, of which 14 were waited for; matrix products, arithmetic and copies ran while one was open for 0% of the time, Pallas kernels for 15%

profile of v8, /device:TPU:0, one launch (start us, length us, event | category | flops | bytes accessed | tf_op | source)
XLA Modules:
  0.0 99.1 jit_solution(10479161940983496025)
XLA Ops:
  0.7 1.2 %copy.10 = bf16[32,3,20,128]{3,0,1,2:T(8,128)(2,1)S(1)} copy(bf16[32,3,20,128]{3,0,2,1:T(8,128)(2,1)} %param.9) | data formatting | bytes 983040 | tf_op args[4]
  1.9 0.0 copy-start
  1.9 0.1 dynamic-slice_bitcast_fusion.1
  2.0 3.1 %collective-permute-start.2 = (bf16[5,3,32,128]{3,2,1,0:T(8,128)(2,1)S(1)}, bf16[5,3,32,128]{3,2,1,0:T(8,128)(2,1)S(1)}, u32[]{:S(2)}, u32[]{:S(2)}) collective-permute-start(bf16[5,3,32,128]{3,2,1,0:T(8,128)(2,1)S(1)} %get-tuple-element.114), channel_id=1, source_target_pairs={{0,4},{1,5},{2,6},{3,7},{4,0},{5,1},{6,2},{7,3},{8,12},{9,13},{10,... | collective-permute-start | bytes 368648 | tf_op jit(solution)/shard_map/ppermute | solution.py:253
  5.1 1.4 %collective-permute-start.3 = (bf16[5,3,32,128]{3,2,1,0:T(8,128)(2,1)S(1)}, bf16[5,3,32,128]{3,2,1,0:T(8,128)(2,1)S(1)}, u32[]{:S(2)}, u32[]{:S(2)}) collective-permute-start(bf16[5,3,32,128]{3,2,1,0:T(8,128)(2,1)S(1)} %get-tuple-element.115), channel_id=1, source_target_pairs={{0,6},{1,7},{2,4},{3,5},{4,2},{5,3},{6,0},{7,1},{8,14},{9,15},{10,... | collective-permute-start | bytes 368648 | tf_op jit(solution)/shard_map/ppermute | solution.py:253
  6.5 0.1 collective-permute-start.1
  6.6 0.1 pad_add_fusion.where_ref
  6.7 0.1 copy.9.rate_ref
  6.8 1.1 %split.1 = (bf16[2,128,640]{2,1,0:T(8,128)(2,1)S(1)}, bf16[2,128,640]{2,1,0:T(8,128)(2,1)S(1)}, bf16[2,128,640]{2,1,0:T(8,128)(2,1)S(1)}, bf16[2,128,640]{2,1,0:...) custom-call(s32[2]{0:T(128)S(1)} %pad_add_fusion.where_ref, ...), custom_call_target="tpu_custom_call" | custom-call | flops 10000000 | bytes 4000000 | tf_op jit(solution)/shard_map/split/pallas_call | solution.py:261
  7.9 2.0 %collective-permute-start.6 = (bf16[2,128,640]{2,1,0:T(8,128)(2,1)S(1)}, bf16[2,128,640]{2,1,0:T(8,128)(2,1)S(1)}, u32[]{:S(2)}, u32[]{:S(2)}) collective-permute-start(bf16[2,128,640]{2,1,0:T(8,128)(2,1)S(1)} %get-tuple-element.60), channel_id=1, source_target_pairs={{0,4},{1,5},{2,6},{3,7},{4,0},{5,1},{6,2},{7,3},{8,12},{9,13},{10,... | collective-permute-start | bytes 983048 | tf_op jit(solution)/shard_map/ppermute | solution.py:253
  9.9 1.4 %collective-permute-start.7 = (bf16[2,128,640]{2,1,0:T(8,128)(2,1)S(1)}, bf16[2,128,640]{2,1,0:T(8,128)(2,1)S(1)}, u32[]{:S(2)}, u32[]{:S(2)}) collective-permute-start(bf16[2,128,640]{2,1,0:T(8,128)(2,1)S(1)} %get-tuple-element.61), channel_id=1, source_target_pairs={{0,6},{1,7},{2,4},{3,5},{4,2},{5,3},{6,0},{7,1},{8,14},{9,15},{10,... | collective-permute-start | bytes 983048 | tf_op jit(solution)/shard_map/ppermute | solution.py:253
  11.3 0.0 collective-permute-done.2
  11.3 2.0 %collective-permute-done.3 = bf16[5,3,32,128]{3,2,1,0:T(8,128)(2,1)S(1)} collective-permute-done((bf16[5,3,32,128]{3,2,1,0:T(8,128)(2,1)S(1)}, bf16[5,3,32,128]{3,2,1,0:T(8,128)(2,1)S(1)}, u32[]{:S(2)}, u32[]{:S(2)}) %collective-permute-start.3) | collective-permute-done | bytes 122912 | tf_op jit(solution)/shard_map/ppermute | solution.py:253
  13.3 0.3 collective-permute-done.1
  13.6 3.7 %collective-permute-start.4 = (bf16[2,5,3,32,128]{4,3,2,1,0:T(8,128)(2,1)S(1)}, bf16[2,5,3,32,128]{4,3,2,1,0:T(8,128)(2,1)S(1)}, u32[]{:S(2)}, u32[]{:S(2)}) collective-permute-start(bf16[2,5,3,32,128]{4,3,2,1,0:T(8,128)(2,1)S(1)} %pad_maximum_fusion.2.refs_4_.refs_0_), channel_id=1, source_target_pairs={{0,12},{1,13},{2,14},{3,15},{4,8},{5,9},{6,10},{7,11},{8,4},{9,5},... | collective-permute-start | bytes 737288 | tf_op jit(solution)/shard_map/ppermute | solution.py:253
  17.3 0.2 collective-permute-start.5
  17.5 0.4 collective-permute-start
  17.9 1.3 %collective-permute-done.6.refs_2_ = bf16[2,128,640]{2,1,0:T(8,128)(2,1)S(1)} collective-permute-done((bf16[2,128,640]{2,1,0:T(8,128)(2,1)S(1)}, bf16[2,128,640]{2,1,0:T(8,128)(2,1)S(1)}, u32[]{:S(2)}, u32[]{:S(2)}) %collective-permute-start.6) | collective-permute-done | bytes 327712 | tf_op jit(solution)/shard_map/ppermute | solution.py:253
  19.3 0.0 collective-permute-start.8
  19.3 7.0 %collective-permute-done.7.refs_3_ = bf16[2,128,640]{2,1,0:T(8,128)(2,1)S(1)} collective-permute-done((bf16[2,128,640]{2,1,0:T(8,128)(2,1)S(1)}, bf16[2,128,640]{2,1,0:T(8,128)(2,1)S(1)}, u32[]{:S(2)}, u32[]{:S(2)}) %collective-permute-start.7) | collective-permute-done | bytes 327712 | tf_op jit(solution)/shard_map/ppermute | solution.py:253
  26.3 0.0 collective-permute-start.9
  26.3 7.4 %collective-permute-done.4.refs_8_.refs_4_ = bf16[2,5,3,32,128]{4,3,2,1,0:T(8,128)(2,1)S(1)} collective-permute-done((bf16[2,5,3,32,128]{4,3,2,1,0:T(8,128)(2,1)S(1)}, bf16[2,5,3,32,128]{4,3,2,1,0:T(8,128)(2,1)S(1)}, u32[]{:S(2)}, u32[]{:S(2)}) %collective-permute-start.4) | collective-permute-done | bytes 245792 | tf_op jit(solution)/shard_map/ppermute | solution.py:253
  33.7 4.2 %collective-permute-done.5.refs_9_.refs_5_ = bf16[2,5,3,32,128]{4,3,2,1,0:T(8,128)(2,1)S(1)} collective-permute-done((bf16[2,5,3,32,128]{4,3,2,1,0:T(8,128)(2,1)S(1)}, bf16[2,5,3,32,128]{4,3,2,1,0:T(8,128)(2,1)S(1)}, u32[]{:S(2)}, u32[]{:S(2)}) %collective-permute-start.5) | collective-permute-done | bytes 245792 | tf_op jit(solution)/shard_map/ppermute | solution.py:253
  37.9 0.0 collective-permute-start.10
  37.9 0.5 collective-permute-start.11
  38.4 0.0 collective-permute-done.refs_1_
  38.4 1.5 %collective-permute-start.16 = (bf16[128,640]{1,0:T(8,128)(2,1)S(1)}, bf16[128,640]{1,0:T(8,128)(2,1)S(1)}, u32[]{:S(2)}, u32[]{:S(2)}) collective-permute-start(bf16[128,640]{1,0:T(8,128)(2,1)S(1)} %get-tuple-element.77), channel_id=1, source_target_pairs={{0,2},{1,3},{2,0},{3,1},{4,6},{5,7},{6,4},{7,5},{8,10},{9,11},{10,... | collective-permute-start | bytes 491528 | tf_op jit(solution)/shard_map/ppermute | solution.py:253
  39.9 0.0 collective-permute-done.8.refs_6_.refs_2_
  39.9 0.0 collective-permute-start.17
  39.9 0.0 collective-permute-done.9.refs_7_.refs_3_
  39.9 2.0 %collective-permute-start.18 = (bf16[128,640]{1,0:T(8,128)(2,1)S(1)}, bf16[128,640]{1,0:T(8,128)(2,1)S(1)}, u32[]{:S(2)}, u32[]{:S(2)}) collective-permute-start(bf16[128,640]{1,0:T(8,128)(2,1)S(1)} %get-tuple-element.79), channel_id=1, source_target_pairs={{0,6},{1,7},{2,4},{3,5},{4,2},{5,3},{6,0},{7,1},{8,14},{9,15},{10,... | collective-permute-start | bytes 491528 | tf_op jit(solution)/shard_map/ppermute | solution.py:253
  41.9 0.0 collective-permute-done.10.refs_10_.refs_6_
  41.9 0.0 collective-permute-done.11.refs_11_.refs_7_
  41.9 8.1 %key_side.1 = (f32[4,512,128]{2,1,0:T(8,128)S(1)}, f32[4,512,128]{2,1,0:T(8,128)S(1)}, bf16[4,512,128]{2,1,0:T(8,128)(2,1)S(1)}, bf16[512,128]{1,0:T(8,128)(2,1)...) custom-call(s32[2]{0:T(128)S(1)} %pad_add_fusion.where_ref, ...), custom_call_target="tpu_custom_call" | custom-call | flops 2000000000 | bytes 4000000 | tf_op jit(solution)/shard_map/key_side/pallas_call | solution.py:293
  50.0 0.1 collective-permute-start.12
  50.1 0.5 collective-permute-start.13
  50.6 0.0 collective-permute-done.16.refs_1_
  50.6 0.1 collective-permute-start.14
  50.6 0.0 collective-permute-done.17.refs_2_
  50.7 0.4 collective-permute-start.15
  51.1 0.0 collective-permute-done.18.refs_3_
  51.1 0.1 collective-permute-start.23
  51.2 0.2 collective-permute-done.12
  51.4 0.2 collective-permute-done.13
  51.6 0.3 collective-permute-done.14
  51.9 0.2 collective-permute-done.15
  52.1 0.1 add_convert_fusion
  52.3 2.6 %collective-permute-start.20 = (bf16[4,512,128]{2,1,0:T(8,128)(2,1)S(1)}, bf16[4,512,128]{2,1,0:T(8,128)(2,1)S(1)}, u32[]{:S(2)}, u32[]{:S(2)}) collective-permute-start(bf16[4,512,128]{2,1,0:T(8,128)(2,1)S(1)} %add_convert_fusion), channel_id=1, source_target_pairs={{0,12},{1,13},{2,14},{3,15},{4,8},{5,9},{6,10},{7,11},{8,4},{9,5},... | collective-permute-start | bytes 1572872 | tf_op jit(solution)/shard_map/ppermute | solution.py:253
  54.9 4.1 %query_side.1 = (bf16[128,640]{1,0:T(8,128)(2,1)S(1)}, bf16[128,640]{1,0:T(8,128)(2,1)S(1)}, bf16[128,640]{1,0:T(8,128)(2,1)S(1)}, bf16[128,640]{1,0:T(8,128)(2,1)S(1)}) custom-call(bf16[128,640]{1,0:T(8,128)(2,1)S(1)} %get-tuple-element.80.refs_0_, bf16[128,640]{1,0:T(8,128)(2,1)S(1)} %collective-permute-done.16.refs_1_, ...), custom_call_target="tpu_custom_call" | custom-call | flops 1000000000 | bytes 4000000 | tf_op jit(solution)/shard_map/query_side/pallas_call | solution.py:321
  59.0 0.1 collective-permute-start.21
  59.0 2.0 %collective-permute-start.22 = (bf16[128,640]{1,0:T(8,128)(2,1)S(1)}, bf16[128,640]{1,0:T(8,128)(2,1)S(1)}, u32[]{:S(2)}, u32[]{:S(2)}) collective-permute-start(bf16[128,640]{1,0:T(8,128)(2,1)S(1)} %get-tuple-element.96), channel_id=1, source_target_pairs={{0,6},{1,7},{2,4},{3,5},{4,2},{5,3},{6,0},{7,1},{8,14},{9,15},{10,... | collective-permute-start | bytes 491528 | tf_op jit(solution)/shard_map/ppermute | solution.py:253
  61.0 0.7 pick.1.old_ref
  61.7 0.0 collective-permute-done.23
  61.7 0.1 convert_add_fusion.mine_ref
  61.8 10.2 %collective-permute-done.21.refs_2_ = bf16[128,640]{1,0:T(8,128)(2,1)S(1)} collective-permute-done((bf16[128,640]{1,0:T(8,128)(2,1)S(1)}, bf16[128,640]{1,0:T(8,128)(2,1)S(1)}, u32[]{:S(2)}, u32[]{:S(2)}) %collective-permute-start.21) | collective-permute-done | bytes 163872 | tf_op jit(solution)/shard_map/ppermute | solution.py:253
  72.0 4.3 %collective-permute-done.22.refs_3_ = bf16[128,640]{1,0:T(8,128)(2,1)S(1)} collective-permute-done((bf16[128,640]{1,0:T(8,128)(2,1)S(1)}, bf16[128,640]{1,0:T(8,128)(2,1)S(1)}, u32[]{:S(2)}, u32[]{:S(2)}) %collective-permute-start.22) | collective-permute-done | bytes 163872 | tf_op jit(solution)/shard_map/ppermute | solution.py:253
  76.3 0.0 collective-permute-done.20.far_ref
  76.3 3.0 %renew.1 = bf16[16,4,32,128]{3,2,1,0:T(8,128)(2,1)} custom-call(f32[4,512,128]{2,1,0:T(8,128)S(1)} %convert_add_fusion.mine_ref, bf16[4,512,128]{2,1,0:T(8,128)(2,1)S(1)} %collective-permute-done.20.far_ref, bf16[16,4,32,128]{3,2,1,0:T(8,128)(2,1)S(1)} %pick.1.old_ref), custom_call_target="tpu_custom_call" | custom-call | flops 2000000000 | bytes 4000000 | tf_op jit(solution)/shard_map/renew/pallas_call | solution.py:354
  79.3 4.2 %all-to-all-start = ((bf16[16,4,32,128]{3,2,1,0:T(8,128)(2,1)}), bf16[16,4,32,128]{3,2,1,0:T(8,128)(2,1)S(1)}, u32[]{:S(2)}, u32[]{:S(2)}) async-start(bf16[16,4,32,128]{3,2,1,0:T(8,128)(2,1)} %renew.1), calls=%async_computation | async-start | bytes 1048576 | tf_op jit(solution)/shard_map/all_to_all | solution.py:364
  83.6 1.9 %collective-permute-start.19 = (bf16[128,640]{1,0:T(8,128)(2,1)S(1)}, bf16[128,640]{1,0:T(8,128)(2,1)S(1)}, u32[]{:S(2)}, u32[]{:S(2)}) collective-permute-start(bf16[128,640]{1,0:T(8,128)(2,1)S(1)} %get-tuple-element.89), channel_id=1, source_target_pairs={{0,2},{1,3},{2,0},{3,1},{4,6},{5,7},{6,4},{7,5},{8,10},{9,11},{10,... | collective-permute-start | bytes 491528 | tf_op jit(solution)/shard_map/ppermute | solution.py:253
  85.5 9.0 %collective-permute-done.19.refs_1_ = bf16[128,640]{1,0:T(8,128)(2,1)S(1)} collective-permute-done((bf16[128,640]{1,0:T(8,128)(2,1)S(1)}, bf16[128,640]{1,0:T(8,128)(2,1)S(1)}, u32[]{:S(2)}, u32[]{:S(2)}) %collective-permute-start.19) | collective-permute-done | bytes 163872 | tf_op jit(solution)/shard_map/ppermute | solution.py:253
  94.5 1.4 %join.1 = bf16[128,2560]{1,0:T(8,128)(2,1)} custom-call(s32[2]{0:T(128)S(1)} %pad_add_fusion.where_ref, bf16[128,640]{1,0:T(8,128)(2,1)S(1)} %get-tuple-element.88.refs_0_, bf16[128,640]{1,0:T(8,128)(2,1)S(1)} %collective-permute-done.19.refs_1_, bf16[128,640]{1,0:T(8,128)(2,1)S(1)} %collective-permute-done.21.refs_2_, ...), custom_call_target="tpu_custom_call" | custom-call | flops 10000000 | bytes 4000000 | tf_op jit(solution)/shard_map/join/pallas_call | solution.py:335
  95.9 2.1 %all-to-all-done = bf16[16,4,32,128]{3,2,1,0:T(8,128)(2,1)S(1)} async-done(((bf16[16,4,32,128]{3,2,1,0:T(8,128)(2,1)}), bf16[16,4,32,128]{3,2,1,0:T(8,128)(2,1)S(1)}, u32[]{:S(2)}, u32[]{:S(2)}) %all-to-all-start) | async-done | bytes 524320 | tf_op jit(solution)/shard_map/all_to_all | solution.py:364
  98.2 0.8 copy.14
  (14 shorter events, 0.2 us)
Async XLA Ops:
  0.7 6.1 %copy-start.1 = (bf16[128,2560]{1,0:T(8,128)(2,1)S(1)}, bf16[128,2560]{1,0:T(8,128)(2,1)}, u32[]{:S(2)}) copy-start(bf16[128,2560]{1,0:T(8,128)(2,1)} %k_ref.1) | copy-start | bytes 1966084
  0.7 6.1 %copy-start.2 = (bf16[128,2560]{1,0:T(8,128)(2,1)S(1)}, bf16[128,2560]{1,0:T(8,128)(2,1)}, u32[]{:S(2)}) copy-start(bf16[128,2560]{1,0:T(8,128)(2,1)} %v_ref.1) | copy-start | bytes 1966084
  1.9 4.9 %copy-start = (bf16[128,2560]{1,0:T(8,128)(2,1)S(1)}, bf16[128,2560]{1,0:T(8,128)(2,1)}, u32[]{:S(2)}) copy-start(bf16[128,2560]{1,0:T(8,128)(2,1)} %q_ref.1) | copy-start | bytes 1966084
  2.0 9.4 %collective-permute-start.2 = (bf16[5,3,32,128]{3,2,1,0:T(8,128)(2,1)S(1)}, bf16[5,3,32,128]{3,2,1,0:T(8,128)(2,1)S(1)}, u32[]{:S(2)}, u32[]{:S(2)}) collective-permute-start(bf16[5,3,32,128]{3,2,1,0:T(8,128)(2,1)S(1)} %get-tuple-element.114), channel_id=1, source_target_pairs={{0,4},{1,5},{2,6},{3,7},{4,0},{5,1},{6,2},{7,3},{8,12},{9,13},{10,... | collective-permute-start | bytes 368648 | tf_op jit(solution)/shard_map/ppermute | solution.py:253
  5.1 1.6 %copy-start.3 = (f32[128,20]{0,1:T(8,128)S(1)}, f32[128,20]{0,1:T(8,128)}, u32[]{:S(2)}) copy-start(f32[128,20]{0,1:T(8,128)} %param.8) | copy-start | bytes 30724
  5.1 8.2 %collective-permute-start.3 = (bf16[5,3,32,128]{3,2,1,0:T(8,128)(2,1)S(1)}, bf16[5,3,32,128]{3,2,1,0:T(8,128)(2,1)S(1)}, u32[]{:S(2)}, u32[]{:S(2)}) collective-permute-start(bf16[5,3,32,128]{3,2,1,0:T(8,128)(2,1)S(1)} %get-tuple-element.115), channel_id=1, source_target_pairs={{0,6},{1,7},{2,4},{3,5},{4,2},{5,3},{6,0},{7,1},{8,14},{9,15},{10,... | collective-permute-start | bytes 368648 | tf_op jit(solution)/shard_map/ppermute | solution.py:253
  6.5 7.1 %collective-permute-start.1 = (bf16[5,3,32,128]{3,2,1,0:T(8,128)(2,1)S(1)}, bf16[5,3,32,128]{3,2,1,0:T(8,128)(2,1)S(1)}, u32[]{:S(2)}, u32[]{:S(2)}) collective-permute-start(bf16[5,3,32,128]{3,2,1,0:T(8,128)(2,1)S(1)} %get-tuple-element.116), channel_id=1, source_target_pairs={{0,2},{1,3},{2,0},{3,1},{4,6},{5,7},{6,4},{7,5},{8,10},{9,11},{10,... | collective-permute-start | bytes 368648 | tf_op jit(solution)/shard_map/ppermute | solution.py:253
  7.9 11.4 %collective-permute-start.6 = (bf16[2,128,640]{2,1,0:T(8,128)(2,1)S(1)}, bf16[2,128,640]{2,1,0:T(8,128)(2,1)S(1)}, u32[]{:S(2)}, u32[]{:S(2)}) collective-permute-start(bf16[2,128,640]{2,1,0:T(8,128)(2,1)S(1)} %get-tuple-element.60), channel_id=1, source_target_pairs={{0,4},{1,5},{2,6},{3,7},{4,0},{5,1},{6,2},{7,3},{8,12},{9,13},{10,... | collective-permute-start | bytes 983048 | tf_op jit(solution)/shard_map/ppermute | solution.py:253
  9.9 16.4 %collective-permute-start.7 = (bf16[2,128,640]{2,1,0:T(8,128)(2,1)S(1)}, bf16[2,128,640]{2,1,0:T(8,128)(2,1)S(1)}, u32[]{:S(2)}, u32[]{:S(2)}) collective-permute-start(bf16[2,128,640]{2,1,0:T(8,128)(2,1)S(1)} %get-tuple-element.61), channel_id=1, source_target_pairs={{0,6},{1,7},{2,4},{3,5},{4,2},{5,3},{6,0},{7,1},{8,14},{9,15},{10,... | collective-permute-start | bytes 983048 | tf_op jit(solution)/shard_map/ppermute | solution.py:253
  13.6 20.1 %collective-permute-start.4 = (bf16[2,5,3,32,128]{4,3,2,1,0:T(8,128)(2,1)S(1)}, bf16[2,5,3,32,128]{4,3,2,1,0:T(8,128)(2,1)S(1)}, u32[]{:S(2)}, u32[]{:S(2)}) collective-permute-start(bf16[2,5,3,32,128]{4,3,2,1,0:T(8,128)(2,1)S(1)} %pad_maximum_fusion.2.refs_4_.refs_0_), channel_id=1, source_target_pairs={{0,12},{1,13},{2,14},{3,15},{4,8},{5,9},{6,10},{7,11},{8,4},{9,5},... | collective-permute-start | bytes 737288 | tf_op jit(solution)/shard_map/ppermute | solution.py:253
  17.3 20.6 %collective-permute-start.5 = (bf16[2,5,3,32,128]{4,3,2,1,0:T(8,128)(2,1)S(1)}, bf16[2,5,3,32,128]{4,3,2,1,0:T(8,128)(2,1)S(1)}, u32[]{:S(2)}, u32[]{:S(2)}) collective-permute-start(bf16[2,5,3,32,128]{4,3,2,1,0:T(8,128)(2,1)S(1)} %pad_maximum_fusion.3.refs_5_.refs_1_), channel_id=1, source_target_pairs={{0,12},{1,13},{2,14},{3,15},{4,8},{5,9},{6,10},{7,11},{8,4},{9,5},... | collective-permute-start | bytes 737288 | tf_op jit(solution)/shard_map/ppermute | solution.py:253
  17.5 20.9 %collective-permute-start = (bf16[2,128,640]{2,1,0:T(8,128)(2,1)S(1)}, bf16[2,128,640]{2,1,0:T(8,128)(2,1)S(1)}, u32[]{:S(2)}, u32[]{:S(2)}) collective-permute-start(bf16[2,128,640]{2,1,0:T(8,128)(2,1)S(1)} %get-tuple-element.57), channel_id=1, source_target_pairs={{0,2},{1,3},{2,0},{3,1},{4,6},{5,7},{6,4},{7,5},{8,10},{9,11},{10,... | collective-permute-start | bytes 983048 | tf_op jit(solution)/shard_map/ppermute | solution.py:253
  19.3 20.6 %collective-permute-start.8 = (bf16[2,5,3,32,128]{4,3,2,1,0:T(8,128)(2,1)S(1)}, bf16[2,5,3,32,128]{4,3,2,1,0:T(8,128)(2,1)S(1)}, u32[]{:S(2)}, u32[]{:S(2)}) collective-permute-start(bf16[2,5,3,32,128]{4,3,2,1,0:T(8,128)(2,1)S(1)} %pad_maximum_fusion.2.refs_4_.refs_0_), channel_id=1, source_target_pairs={{0,1},{1,0},{2,3},{3,2},{4,5},{5,4},{6,7},{7,6},{8,9},{9,8},{10,11... | collective-permute-start | bytes 737288 | tf_op jit(solution)/shard_map/ppermute | solution.py:253
  26.3 13.6 %collective-permute-start.9 = (bf16[2,5,3,32,128]{4,3,2,1,0:T(8,128)(2,1)S(1)}, bf16[2,5,3,32,128]{4,3,2,1,0:T(8,128)(2,1)S(1)}, u32[]{:S(2)}, u32[]{:S(2)}) collective-permute-start(bf16[2,5,3,32,128]{4,3,2,1,0:T(8,128)(2,1)S(1)} %pad_maximum_fusion.3.refs_5_.refs_1_), channel_id=1, source_target_pairs={{0,1},{1,0},{2,3},{3,2},{4,5},{5,4},{6,7},{7,6},{8,9},{9,8},{10,11... | collective-permute-start | bytes 737288 | tf_op jit(solution)/shard_map/ppermute | solution.py:253
  37.9 4.0 %collective-permute-start.10 = (bf16[2,5,3,32,128]{4,3,2,1,0:T(8,128)(2,1)S(1)}, bf16[2,5,3,32,128]{4,3,2,1,0:T(8,128)(2,1)S(1)}, u32[]{:S(2)}, u32[]{:S(2)}) collective-permute-start(bf16[2,5,3,32,128]{4,3,2,1,0:T(8,128)(2,1)S(1)} %collective-permute-done.4.refs_8_.refs_4_), channel_id=1, source_target_pairs={{0,1},{1,0},{2,3},{3,2},{4,5},{5,4},{6,7},{7,6},{8,9},{9,8},{10,11... | collective-permute-start | bytes 737288 | tf_op jit(solution)/shard_map/ppermute | solution.py:253
  37.9 4.0 %collective-permute-start.11 = (bf16[2,5,3,32,128]{4,3,2,1,0:T(8,128)(2,1)S(1)}, bf16[2,5,3,32,128]{4,3,2,1,0:T(8,128)(2,1)S(1)}, u32[]{:S(2)}, u32[]{:S(2)}) collective-permute-start(bf16[2,5,3,32,128]{4,3,2,1,0:T(8,128)(2,1)S(1)} %collective-permute-done.5.refs_9_.refs_5_), channel_id=1, source_target_pairs={{0,1},{1,0},{2,3},{3,2},{4,5},{5,4},{6,7},{7,6},{8,9},{9,8},{10,11... | collective-permute-start | bytes 737288 | tf_op jit(solution)/shard_map/ppermute | solution.py:253
  38.4 12.2 %collective-permute-start.16 = (bf16[128,640]{1,0:T(8,128)(2,1)S(1)}, bf16[128,640]{1,0:T(8,128)(2,1)S(1)}, u32[]{:S(2)}, u32[]{:S(2)}) collective-permute-start(bf16[128,640]{1,0:T(8,128)(2,1)S(1)} %get-tuple-element.77), channel_id=1, source_target_pairs={{0,2},{1,3},{2,0},{3,1},{4,6},{5,7},{6,4},{7,5},{8,10},{9,11},{10,... | collective-permute-start | bytes 491528 | tf_op jit(solution)/shard_map/ppermute | solution.py:253
  39.9 10.8 %collective-permute-start.17 = (bf16[128,640]{1,0:T(8,128)(2,1)S(1)}, bf16[128,640]{1,0:T(8,128)(2,1)S(1)}, u32[]{:S(2)}, u32[]{:S(2)}) collective-permute-start(bf16[128,640]{1,0:T(8,128)(2,1)S(1)} %get-tuple-element.78), channel_id=1, source_target_pairs={{0,4},{1,5},{2,6},{3,7},{4,0},{5,1},{6,2},{7,3},{8,12},{9,13},{10,... | collective-permute-start | bytes 491528 | tf_op jit(solution)/shard_map/ppermute | solution.py:253
  39.9 11.2 %collective-permute-start.18 = (bf16[128,640]{1,0:T(8,128)(2,1)S(1)}, bf16[128,640]{1,0:T(8,128)(2,1)S(1)}, u32[]{:S(2)}, u32[]{:S(2)}) collective-permute-start(bf16[128,640]{1,0:T(8,128)(2,1)S(1)} %get-tuple-element.79), channel_id=1, source_target_pairs={{0,6},{1,7},{2,4},{3,5},{4,2},{5,3},{6,0},{7,1},{8,14},{9,15},{10,... | collective-permute-start | bytes 491528 | tf_op jit(solution)/shard_map/ppermute | solution.py:253
  50.0 1.4 %collective-permute-start.12 = (bf16[512,128]{1,0:T(8,128)(2,1)S(1)}, bf16[512,128]{1,0:T(8,128)(2,1)S(1)}, u32[]{:S(2)}, u32[]{:S(2)}) collective-permute-start(bf16[512,128]{1,0:T(8,128)(2,1)S(1)} %get-tuple-element.72), channel_id=1, source_target_pairs={{0,1},{1,0},{2,3},{3,2},{4,5},{5,4},{6,7},{7,6},{8,9},{9,8},{10,11... | collective-permute-start | bytes 393224 | tf_op jit(solution)/shard_map/ppermute | solution.py:253
  50.1 1.5 %collective-permute-start.13 = (bf16[512,128]{1,0:T(8,128)(2,1)S(1)}, bf16[512,128]{1,0:T(8,128)(2,1)S(1)}, u32[]{:S(2)}, u32[]{:S(2)}) collective-permute-start(bf16[512,128]{1,0:T(8,128)(2,1)S(1)} %get-tuple-element.73), channel_id=1, source_target_pairs={{0,1},{1,0},{2,3},{3,2},{4,5},{5,4},{6,7},{7,6},{8,9},{9,8},{10,11... | collective-permute-start | bytes 393224 | tf_op jit(solution)/shard_map/ppermute | solution.py:253
  50.6 1.3 %collective-permute-start.14 = (bf16[512,128]{1,0:T(8,128)(2,1)S(1)}, bf16[512,128]{1,0:T(8,128)(2,1)S(1)}, u32[]{:S(2)}, u32[]{:S(2)}) collective-permute-start(bf16[512,128]{1,0:T(8,128)(2,1)S(1)} %get-tuple-element.74), channel_id=1, source_target_pairs={{0,1},{1,0},{2,3},{3,2},{4,5},{5,4},{6,7},{7,6},{8,9},{9,8},{10,11... | collective-permute-start | bytes 393224 | tf_op jit(solution)/shard_map/ppermute | solution.py:253
  50.7 1.5 %collective-permute-start.15 = (bf16[512,128]{1,0:T(8,128)(2,1)S(1)}, bf16[512,128]{1,0:T(8,128)(2,1)S(1)}, u32[]{:S(2)}, u32[]{:S(2)}) collective-permute-start(bf16[512,128]{1,0:T(8,128)(2,1)S(1)} %get-tuple-element.75), channel_id=1, source_target_pairs={{0,1},{1,0},{2,3},{3,2},{4,5},{5,4},{6,7},{7,6},{8,9},{9,8},{10,11... | collective-permute-start | bytes 393224 | tf_op jit(solution)/shard_map/ppermute | solution.py:253
  51.1 10.6 %collective-permute-start.23 = (bf16[4,512,128]{2,1,0:T(8,128)(2,1)S(1)}, bf16[4,512,128]{2,1,0:T(8,128)(2,1)S(1)}, u32[]{:S(2)}, u32[]{:S(2)}) collective-permute-start(bf16[4,512,128]{2,1,0:T(8,128)(2,1)S(1)} %get-tuple-element.100), channel_id=1, source_target_pairs={{0,1},{1,0},{2,3},{3,2},{4,5},{5,4},{6,7},{7,6},{8,9},{9,8},{10,11... | collective-permute-start | bytes 1572872 | tf_op jit(solution)/shard_map/ppermute | solution.py:253
  52.3 24.1 %collective-permute-start.20 = (bf16[4,512,128]{2,1,0:T(8,128)(2,1)S(1)}, bf16[4,512,128]{2,1,0:T(8,128)(2,1)S(1)}, u32[]{:S(2)}, u32[]{:S(2)}) collective-permute-start(bf16[4,512,128]{2,1,0:T(8,128)(2,1)S(1)} %add_convert_fusion), channel_id=1, source_target_pairs={{0,12},{1,13},{2,14},{3,15},{4,8},{5,9},{6,10},{7,11},{8,4},{9,5},... | collective-permute-start | bytes 1572872 | tf_op jit(solution)/shard_map/ppermute | solution.py:253
  59.0 13.0 %collective-permute-start.21 = (bf16[128,640]{1,0:T(8,128)(2,1)S(1)}, bf16[128,640]{1,0:T(8,128)(2,1)S(1)}, u32[]{:S(2)}, u32[]{:S(2)}) collective-permute-start(bf16[128,640]{1,0:T(8,128)(2,1)S(1)} %get-tuple-element.95), channel_id=1, source_target_pairs={{0,4},{1,5},{2,6},{3,7},{4,0},{5,1},{6,2},{7,3},{8,12},{9,13},{10,... | collective-permute-start | bytes 491528 | tf_op jit(solution)/shard_map/ppermute | solution.py:253
  59.0 17.3 %collective-permute-start.22 = (bf16[128,640]{1,0:T(8,128)(2,1)S(1)}, bf16[128,640]{1,0:T(8,128)(2,1)S(1)}, u32[]{:S(2)}, u32[]{:S(2)}) collective-permute-start(bf16[128,640]{1,0:T(8,128)(2,1)S(1)} %get-tuple-element.96), channel_id=1, source_target_pairs={{0,6},{1,7},{2,4},{3,5},{4,2},{5,3},{6,0},{7,1},{8,14},{9,15},{10,... | collective-permute-start | bytes 491528 | tf_op jit(solution)/shard_map/ppermute | solution.py:253
  79.3 18.7 %all-to-all-start = ((bf16[16,4,32,128]{3,2,1,0:T(8,128)(2,1)}), bf16[16,4,32,128]{3,2,1,0:T(8,128)(2,1)S(1)}, u32[]{:S(2)}, u32[]{:S(2)}) async-start(bf16[16,4,32,128]{3,2,1,0:T(8,128)(2,1)} %renew.1), calls=%async_computation | async-start | bytes 1048576 | tf_op jit(solution)/shard_map/all_to_all | solution.py:364
  83.6 10.9 %collective-permute-start.19 = (bf16[128,640]{1,0:T(8,128)(2,1)S(1)}, bf16[128,640]{1,0:T(8,128)(2,1)S(1)}, u32[]{:S(2)}, u32[]{:S(2)}) collective-permute-start(bf16[128,640]{1,0:T(8,128)(2,1)S(1)} %get-tuple-element.89), channel_id=1, source_target_pairs={{0,2},{1,3},{2,0},{3,1},{4,6},{5,7},{6,4},{7,5},{8,10},{9,11},{10,... | collective-permute-start | bytes 491528 | tf_op jit(solution)/shard_map/ppermute | solution.py:253
